TPU v7x, 32 devices: a whole 2x2x4 slice. The times are simulated.
32 devices in a mesh: grp: 2 (over y), ep: 4 (over x, core), sub: 4 (over z).
Axes of the slice: x: 2, y: 2, z: 4, core: 2. Of those that a mesh axis runs over, the one named last changes fastest.
Arguments:
- tokens: bfloat16 [2, 512, 2880], P(None, ('grp', 'ep', 'sub')), parts along dimension 1
- norm_gain: float32 [2880], replicated, may hold values from 0.25 to 1.75
- copy_ids: int32 [2, 512, 4], P(None, ('grp', 'ep', 'sub')), parts along dimension 1, may hold values from 0 to 7, as said below
- gate_scores: float32 [2, 512, 4], P(None, ('grp', 'ep', 'sub')), parts along dimension 1, may hold values from 0.05 to 1
- inner_codes: bfloat16 [8, 2880, 2, 2880], P('ep', None, None, 'sub'), may hold values from -6 to 6
- inner_scales: bfloat16 [8, 90, 2, 2880], P('ep', None, None, 'sub'), may hold values from 0.0099487305 to 0.029907227
- down_codes: bfloat16 [8, 2880, 2880], P('ep', None, 'sub'), may hold values from -6 to 6
- down_scales: bfloat16 [8, 90, 2880], P('ep', None, 'sub'), may hold values from 0.014953613 to 0.044921875
Outputs:
- moe_out: bfloat16 [2, 512, 2880], P(None, ('grp', 'ep', 'sub')), parts along dimension 1
There are 2 independent parts, one for each index of `grp`. A program takes and returns all parts, laid end to end along the dimension named above; an argument that names none is the same for every part. Nothing has to cross between parts.
Inputs may be any that keep to these rules, and one draw needn't show every extreme that they name: `copy_ids`: each token names 4 different experts. Among the tokens of one device in one step (aligned blocks of 16 tokens) no expert is named more than 12 times, and in each step one expert is named exactly 12 times by the tokens of every device.
All inputs are finite; a program needn't handle non-finite values.
Results may differ from a plain program's by a relative error of at most 0.0085.
Values may be sent and summed in bfloat16 or wider, within the bound.
No kernel may reach another device: no remote copies, remote signals or barrier semaphores. Data moves between devices by JAX's collectives and lax.ppermute only.
A program may use at most 192 MiB of HBM per device.

v0:
```python
import jax
import jax.numpy as jnp
from jax import lax
from jax.sharding import PartitionSpec as P

epsilon = 1e-05
swish_beta = 1.702


def dequant_inner(codes, scales):
    grouped = codes.reshape(
        codes.shape[0], codes.shape[1] // 32, 32, codes.shape[2], codes.shape[3]
    )
    product = grouped * scales[:, :, None]
    return product.reshape(codes.shape[0], codes.shape[1], codes.shape[2] * codes.shape[3])


def dequant_outer(codes, scales):
    grouped = codes.reshape(codes.shape[0], codes.shape[1] // 32, 32, codes.shape[2])
    product = grouped * scales[:, :, None, :]
    return product.reshape(codes.shape)


def local(
    tokens, norm_gain, copy_ids, gate_scores, inner_codes, inner_scales, down_codes, down_scales
):
    ep_count = lax.axis_size("ep")
    sub_count = lax.axis_size("sub")
    slot_count = inner_codes.shape[0]
    step_count = copy_ids.shape[0]
    tok_rows = copy_ids.shape[1]
    top_count = copy_ids.shape[2]
    model_width = tokens.shape[2]
    capacity = (3 * tok_rows * top_count + 2 * ep_count * slot_count - 1) // (
        2 * ep_count * slot_count
    )
    inner_weights = dequant_inner(inner_codes, inner_scales)
    outer_weights = dequant_outer(down_codes, down_scales)
    unit_count = inner_weights.shape[2] // 2
    column_width = outer_weights.shape[2]
    pieces = []
    for step_index in range(step_count):
        step_ids = copy_ids[step_index : step_index + 1]
        step_scores = gate_scores[step_index : step_index + 1]
        batch = step_ids.shape[0]
        values = tokens[step_index : step_index + 1].astype(jnp.float32)
        normed = (
            values
            * lax.rsqrt(jnp.mean(values * values, axis=-1, keepdims=True) + epsilon)
            * norm_gain
        ).astype(jnp.bfloat16)
        flat_ids = step_ids.reshape(batch, tok_rows * top_count)
        onehot = (
            flat_ids[:, :, None] == jnp.arange(ep_count * slot_count, dtype=jnp.int32)
        ).astype(jnp.int32)
        earlier = jnp.cumsum(onehot, axis=1) - onehot
        within = jnp.sum(earlier * onehot, axis=2)
        target_ep = flat_ids // slot_count
        target_slot = flat_ids % slot_count
        position = ((target_slot * ep_count + target_ep) * capacity + within).reshape(
            batch, tok_rows, top_count
        )
        total_slots = slot_count * ep_count * capacity
        matches = position[:, :, :, None] == jnp.arange(total_slots, dtype=jnp.int32)
        placing = jnp.any(matches, axis=2).astype(jnp.bfloat16)
        outgoing = jnp.einsum(
            "stp,std->spd", placing, normed, preferred_element_type=jnp.float32
        ).astype(jnp.bfloat16)
        outgoing = outgoing.reshape(batch, slot_count, ep_count, capacity, model_width)
        arrived_rows = lax.all_to_all(outgoing, "ep", split_axis=2, concat_axis=2, tiled=True)
        received = lax.all_gather(arrived_rows[:, :, :, None], "sub", axis=3, tiled=True)
        gathered_rows = received.reshape(
            batch, slot_count, ep_count * sub_count * capacity, model_width
        )
        hidden = jnp.einsum(
            "sjrd,jdf->sjrf", gathered_rows, inner_weights, preferred_element_type=jnp.float32
        )
        gating = hidden[..., :unit_count]
        upward = hidden[..., unit_count:]
        activation = (gating * jax.nn.sigmoid(swish_beta * gating) * (upward + 1.0)).astype(
            jnp.bfloat16
        )
        expert_out = jnp.einsum(
            "sjrf,jfe->sjre",
            lax.all_gather(activation, "sub", axis=3, tiled=True),
            outer_weights,
            preferred_element_type=jnp.float32,
        ).astype(jnp.bfloat16)
        arranged = expert_out.reshape(
            batch, slot_count, ep_count, sub_count, capacity, column_width
        )
        mixed_back = lax.all_to_all(
            arranged.reshape(batch, slot_count, ep_count * sub_count, capacity, column_width),
            ("ep", "sub"),
            split_axis=2,
            concat_axis=2,
            tiled=True,
        )
        back = jnp.moveaxis(
            mixed_back.reshape(batch, slot_count, ep_count, sub_count, capacity, column_width), 3, 4
        )
        flat_back = back.reshape(batch, total_slots, model_width)
        weights = step_scores / jnp.sum(step_scores, axis=-1, keepdims=True)
        mixing = jnp.einsum("stk,stkp->stp", weights, matches.astype(jnp.float32))
        combined = jnp.einsum(
            "stp,spd->std", mixing, flat_back.astype(jnp.float32), precision=lax.Precision.HIGHEST
        )
        pieces.append(combined.astype(jnp.bfloat16))
    output = jnp.concatenate(pieces, axis=0)
    return output


def solution(mesh):
    return jax.shard_map(
        local,
        mesh=mesh,
        in_specs=(
            P(None, ("grp", "ep", "sub"), None),
            P(),
            P(None, ("grp", "ep", "sub"), None),
            P(None, ("grp", "ep", "sub"), None),
            P("ep", None, None, "sub"),
            P("ep", None, None, "sub"),
            P("ep", None, "sub"),
            P("ep", None, "sub"),
        ),
        out_specs=P(None, ("grp", "ep", "sub"), None),
        check_vma=False,
    )
```

profile of v0, /device:TPU:0, one launch (start us, length us, event | category | flops | bytes accessed | tf_op | source)
XLA Modules:
  0.0 336.2 jit_solution(2687398779352061886)
XLA Ops:
  8.7 1.1 fusion.32
  9.8 0.7 fusion.59
  10.6 1.3 convolution_convert_fusion
  12.6 13.3 %all_to_all.20 = bf16[1,2,4,12,2880]{4,1,3,0,2:T(2,128)(2,1)S(1)} all-to-all(bf16[1,2,4,12,2880]{4,1,3,0,2:T(2,128)(2,1)S(1)} %copy.128), channel_id=1, replica_groups=mesh['grp'=2,'ep'=4,'sub'=4] {'ep'}, dimensions={2} | all-to-all | bytes 1105920 | tf_op jit(solution)/shard_map/all_to_all | solution.py:70
  25.9 1.0 copy.129
  27.5 1.4 copy.117
  28.9 3.5 %all-to-all-start = ((bf16[1,2,4,12,2880]{4,1,3,0,2:T(2,128)(2,1)}), bf16[1,2,4,12,2880]{4,1,3,0,2:T(2,128)(2,1)S(1)}, u32[]{:S(2)}, u32[]{:S(2)}) async-start(bf16[1,2,4,12,2880]{4,1,3,0,2:T(2,128)(2,1)} %copy.117), calls=%async_computation | async-start | bytes 1130496 | tf_op jit(solution)/shard_map/all_to_all | solution.py:70
  32.5 11.2 %mul.124 = bf16[2,90,32,2,720]{4,3,2,1,0:T(2,128)(2,1)} broadcast(bf16[2,90,2,720]{3,2,1,0:T(2,128)(2,1)S(1)} %copy-done.1), dimensions={0,1,3,4} | broadcast | bytes 17107200 | tf_op jit(solution)/shard_map/mul | solution.py:14
  43.7 39.4 %mul.125 = bf16[2,2880,1440]{2,1,0:T(8,128)(2,1)} reshape(bf16[2,90,32,2,720]{4,3,2,1,0:T(2,128)(2,1)} %mul.124) | data formatting | bytes 33177600 | tf_op jit(solution)/shard_map/mul | solution.py:14
  83.1 21.6 %copy.116 = bf16[2,2880,1440]{1,2,0:T(8,128)(2,1)} copy(bf16[2,2880,1440]{2,1,0:T(8,128)(2,1)} %mul.125) | data formatting | bytes 33177600 | tf_op jit(solution)/shard_map/mul | solution.py:14
  104.6 1.0 copy.118
  105.8 17.5 %bitcast_multiply_fusion = bf16[2,2880,1440]{1,2,0:T(8,128)(2,1)} fusion(bf16[2,2880,1440]{1,2,0:T(8,128)(2,1)} %copy.116, bf16[2,2880,2,720]{1,3,2,0:T(8,128)(2,1)} %param.12), kind=kLoop, calls=%fused_computation | loop fusion | flops 8294400 | bytes 49766400 | tf_op jit(solution)/shard_map/mul | solution.py:14
  123.2 1.9 copy.130
  125.1 9.1 %convolution_bitcast_fusion = f32[1,2,192,1440]{3,2,1,0:T(8,128)S(1)} fusion(bf16[2,2880,1440]{1,2,0:T(8,128)(2,1)} %bitcast_multiply_fusion, bf16[2,192,2880]{2,1,0:T(8,128)(2,1)S(1)} %bitcast.119), kind=kOutput, calls=%fused_computation.11 | convolution fusion | flops 3185049600 | bytes 21012480 | tf_op jit(solution)/shard_map/sjrd,jdf->sjrf/dot_general | solution.py:75
  134.7 1.8 copy.131
  136.7 19.7 %all-gather.11.cloned.1.call-done = bf16[1,2,4,48,2880]{4,2,1,0,3:T(4,128)(2,1)} async-done(((bf16[1,2,4,12,2880]{4,2,1,0,3:T(4,128)(2,1)}), bf16[1,2,4,48,2880]{4,2,1,0,3:T(4,128)(2,1)}) %all-gather.11.cloned.1.call-update) | async-done | bytes 2211856 | tf_op jit(solution)/shard_map/all_gather | solution.py:71
  156.4 1.9 copy.119
  158.3 9.1 %convolution_bitcast_fusion.1 = f32[1,2,192,1440]{3,2,1,0:T(8,128)S(1)} fusion(bf16[2,2880,1440]{1,2,0:T(8,128)(2,1)} %bitcast_multiply_fusion, bf16[2,192,2880]{2,1,0:T(8,128)(2,1)S(1)} %bitcast.118), kind=kOutput, calls=%fused_computation.12 | convolution fusion | flops 3185049600 | bytes 21012480 | tf_op jit(solution)/shard_map/sjrd,jdf->sjrf/dot_general | solution.py:75
  167.8 1.8 copy.120
  169.6 4.0 %mul.121 = bf16[2,90,32,720]{3,2,1,0:T(8,128)(2,1)} broadcast(bf16[2,90,720]{2,1,0:T(8,128)(2,1)S(1)} %copy.114), dimensions={0,1,3} | broadcast | bytes 8553600 | tf_op jit(solution)/shard_map/mul | solution.py:20
  173.7 11.8 %copy.115 = bf16[2,2880,720]{1,2,0:T(8,128)(2,1)} copy(bf16[2,2880,720]{2,1,0:T(8,128)(2,1)} %bitcast.113) | data formatting | bytes 16588800 | tf_op jit(solution)/shard_map/mul | solution.py:20
  185.5 31.6 %all-gather.9.cloned.1.call-done = bf16[1,2,192,2880]{2,1,0,3:T(2,128)(2,1)} async-done(((bf16[1,2,192,720]{2,1,0,3:T(2,128)(2,1)}), bf16[1,2,192,2880]{2,1,0,3:T(2,128)(2,1)}) %all-gather.9.cloned.1.call-update) | async-done | bytes 2211856 | tf_op jit(solution)/shard_map/all_gather | solution.py:85
  217.1 7.1 %copy.132 = bf16[1,2,192,2880]{3,2,1,0:T(8,128)(2,1)S(1)} copy(bf16[1,2,192,2880]{2,1,0,3:T(2,128)(2,1)} %all-gather.9.cloned.1.call-done) | data formatting | bytes 4423680 | tf_op jit(solution)/shard_map/all_gather | solution.py:85
  224.3 8.9 %fusion.18 = bf16[1,2,192,720]{3,2,1,0:T(8,128)(2,1)S(1)} fusion(bf16[1,2,192,2880]{3,2,1,0:T(8,128)(2,1)S(1)} %copy.132, bf16[2,2880,720]{1,2,0:T(8,128)(2,1)} %param.14, bf16[2,2880,720]{1,2,0:T(8,128)(2,1)} %copy.115), kind=kOutput, calls=%fused_computation.17 | convolution fusion | flops 1596948480 | bytes 19353600 | tf_op jit(solution)/shard_map/sjrf,jfe->sjre/dot_general | solution.py:83
  233.2 1.4 copy.133
  234.6 3.7 %all-to-all-start.3 = ((bf16[1,2,16,12,720]{4,1,3,0,2:T(2,128)(2,1)}), bf16[1,2,16,12,720]{4,1,3,0,2:T(2,128)(2,1)S(1)}, u32[]{:S(2)}, u32[]{:S(2)}) async-start(bf16[1,2,16,12,720]{4,1,3,0,2:T(2,128)(2,1)} %bitcast.34), calls=%async_computation.3 | async-start | bytes 1179648 | tf_op jit(solution)/shard_map/all_to_all | solution.py:92
  238.3 51.6 %all-gather.7.cloned.1.call-done = bf16[1,2,192,2880]{2,1,0,3:T(2,128)(2,1)} async-done(((bf16[1,2,192,720]{2,1,0,3:T(2,128)(2,1)}), bf16[1,2,192,2880]{2,1,0,3:T(2,128)(2,1)}) %all-gather.7.cloned.1.call-update) | async-done | bytes 2211856 | tf_op jit(solution)/shard_map/all_gather | solution.py:85
  289.9 7.1 %copy.121 = bf16[1,2,192,2880]{3,2,1,0:T(8,128)(2,1)S(1)} copy(bf16[1,2,192,2880]{2,1,0,3:T(2,128)(2,1)} %all-gather.7.cloned.1.call-done) | data formatting | bytes 4423680 | tf_op jit(solution)/shard_map/all_gather | solution.py:85
  297.0 8.5 %fusion.23 = bf16[1,2,192,720]{3,2,1,0:T(8,128)(2,1)S(1)} fusion(bf16[1,2,192,2880]{3,2,1,0:T(8,128)(2,1)S(1)} %copy.121, bf16[2,2880,720]{1,2,0:T(8,128)(2,1)} %param.14, bf16[2,2880,720]{1,2,0:T(8,128)(2,1)} %copy.115), kind=kOutput, calls=%fused_computation.18 | convolution fusion | flops 1596948480 | bytes 19353600 | tf_op jit(solution)/shard_map/sjrf,jfe->sjre/dot_general | solution.py:83
  305.5 1.4 copy.122
  307.0 3.6 %all-to-all-start.1 = ((bf16[1,2,16,12,720]{4,1,3,0,2:T(2,128)(2,1)}), bf16[1,2,16,12,720]{4,1,3,0,2:T(2,128)(2,1)S(1)}, u32[]{:S(2)}, u32[]{:S(2)}) async-start(bf16[1,2,16,12,720]{4,1,3,0,2:T(2,128)(2,1)} %bitcast.16), calls=%async_computation.1 | async-start | bytes 1179648 | tf_op jit(solution)/shard_map/all_to_all | solution.py:92
  312.1 15.5 %all-to-all-done.1 = bf16[1,2,16,12,720]{4,1,3,0,2:T(2,128)(2,1)S(1)} async-done(((bf16[1,2,16,12,720]{4,1,3,0,2:T(2,128)(2,1)}), bf16[1,2,16,12,720]{4,1,3,0,2:T(2,128)(2,1)S(1)}, u32[]{:S(2)}, u32[]{:S(2)}) %all-to-all-start.1) | async-done | bytes 552992 | tf_op jit(solution)/shard_map/all_to_all | solution.py:92
  (60 shorter events, 8.3 us)
Async XLA Ops:
  6.5 116.7 %all-gather.13.cloned.1.call-start = ((), (), s32[]{:S(2)}) async-start(), calls=%async_computation.7 | async-start | bytes 2826240 | tf_op jit(solution)/shard_map/all_gather | solution.py:71
  12.0 15.0 %copy-start = (bf16[2,16,2880]{2,1,0:T(8,128)(2,1)S(1)}, bf16[2,16,2880]{2,1,0:T(8,128)(2,1)}, u32[]{:S(2)}) copy-start(bf16[2,16,2880]{2,1,0:T(8,128)(2,1)} %param.8) | copy-start | bytes 552964
  12.0 15.0 %copy-start.3 = (f32[2880]{0:T(1024)S(1)}, f32[2880]{0:T(1024)}, u32[]{:S(2)}) copy-start(f32[2880]{0:T(1024)} %param.9) | copy-start | bytes 34564
  27.0 5.5 %copy-start.1 = (bf16[2,90,2,720]{3,2,1,0:T(2,128)(2,1)S(1)}, bf16[2,90,2,720]{3,2,1,0:T(2,128)(2,1)}, u32[]{:S(2)}) copy-start(bf16[2,90,2,720]{3,2,1,0:T(2,128)(2,1)} %param.13) | copy-start | bytes 1555204
  28.9 75.7 %all-to-all-start = ((bf16[1,2,4,12,2880]{4,1,3,0,2:T(2,128)(2,1)}), bf16[1,2,4,12,2880]{4,1,3,0,2:T(2,128)(2,1)S(1)}, u32[]{:S(2)}, u32[]{:S(2)}) async-start(bf16[1,2,4,12,2880]{4,1,3,0,2:T(2,128)(2,1)} %copy.117), calls=%async_computation | async-start | bytes 1130496 | tf_op jit(solution)/shard_map/all_to_all | solution.py:70
  32.4 124.0 %all-gather.11.cloned.1.call-start = ((), (), s32[]{:S(2)}) async-start(), calls=%async_computation.6 | async-start | bytes 2826240 | tf_op jit(solution)/shard_map/all_gather | solution.py:71
  105.7 111.4 %all-gather.9.cloned.1.call-start = ((), (), s32[]{:S(2)}) async-start(), calls=%async_computation.5 | async-start | bytes 3686400 | tf_op jit(solution)/shard_map/all_gather | solution.py:85
  136.5 153.4 %all-gather.7.cloned.1.call-start = ((), (), s32[]{:S(2)}) async-start(), calls=%async_computation.4 | async-start | bytes 3686400 | tf_op jit(solution)/shard_map/all_gather | solution.py:85
  167.4 2.2 copy-start.2
  234.6 72.4 %all-to-all-start.3 = ((bf16[1,2,16,12,720]{4,1,3,0,2:T(2,128)(2,1)}), bf16[1,2,16,12,720]{4,1,3,0,2:T(2,128)(2,1)S(1)}, u32[]{:S(2)}, u32[]{:S(2)}) async-start(bf16[1,2,16,12,720]{4,1,3,0,2:T(2,128)(2,1)} %bitcast.34), calls=%async_computation.3 | async-start | bytes 1179648 | tf_op jit(solution)/shard_map/all_to_all | solution.py:92
  305.5 5.2 %copy-start.4 = (f32[2,16,4]{1,2,0:T(4,128)S(1)}, f32[2,16,4]{1,2,0:T(4,128)}, u32[]{:S(2)}) copy-start(f32[2,16,4]{1,2,0:T(4,128)} %param.11) | copy-start | bytes 1540
  307.0 20.6 %all-to-all-start.1 = ((bf16[1,2,16,12,720]{4,1,3,0,2:T(2,128)(2,1)}), bf16[1,2,16,12,720]{4,1,3,0,2:T(2,128)(2,1)S(1)}, u32[]{:S(2)}, u32[]{:S(2)}) async-start(bf16[1,2,16,12,720]{4,1,3,0,2:T(2,128)(2,1)} %bitcast.16), calls=%async_computation.1 | async-start | bytes 1179648 | tf_op jit(solution)/shard_map/all_to_all | solution.py:92
Sparse Core Ops, SparseCore 0:
  27.1 49.1 all-gather.12
  105.8 50.5 all-gather.10
  158.0 59.0 all-gather.8
  218.5 71.3 all-gather.6
where the time goes:
time: 339 us; the launch traced here: 336 us
  local copies, waits for them, and re-layouts  120 us (35%)
  waiting for transfers between devices  118 us (35%)
  matrix products  38.3 us (11%)
  other arithmetic  21.7 us (6%)
  between operations  13.4 us (4%)
  blocking collectives  13.3 us (4%)
  starting transfers between devices  11.1 us (3%)
    all_gather x2, waiting for transfers between devices, local(): lax.all_gather(activation, 'sub', axis=3, tiled=True)  83.2 us
    mul x3, local copies, waits for them, and re-layouts, dequant_inner(): product = grouped * scales[:, :, None]  72.2 us
    all_gather x2, waiting for transfers between devices, local(): lax.all_gather(arrived_rows[:, :, :, None], 'sub', axis=3, tiled=True)  19.7 us
    dot_general x2, matrix products, local(): jnp.einsum('sjrd,jdf->sjrf', gathered_rows, inner_weights, preferred_elem...  18.2 us
    mul x1, other arithmetic, dequant_inner(): product = grouped * scales[:, :, None]  17.5 us
    dot_general x2, matrix products, local(): jnp.einsum('sjrf,jfe->sjre', lax.all_gather(activation, 'sub', axis=3, ti...  17.4 us
    mul x2, local copies, waits for them, and re-layouts, dequant_outer(): product = grouped * scales[:, :, None, :]  15.8 us
    all_to_all x2, waiting for transfers between devices, local(): lax.all_to_all(arranged.reshape(batch, slot_count, ep_count * sub_count,...  15.5 us
  transfers between devices with their start and end apart: 7, of which 4 were waited for; matrix products, arithmetic and copies ran while one was open for 51% of the time, Pallas kernels for 0%

commit v1 on v0

v1 whole, which is shorter than its diff:
```python
import functools

import jax
import jax.numpy as jnp
from jax import lax
from jax.experimental import pallas as pl
from jax.experimental.pallas import tpu as pltpu
from jax.sharding import PartitionSpec as P

epsilon = 1e-05
swish_beta = 1.702
META = 64
LANES = 128
VMEM_LIMIT = 56 * 1024 * 1024
F32 = jnp.float32
BF16 = jnp.bfloat16


def params():
    return pltpu.CompilerParams(vmem_limit_bytes=VMEM_LIMIT)


def dot(a, b, contract):
    return lax.dot_general(a, b, (contract, ((), ())), preferred_element_type=F32)


def pack_kernel(tokens_ref, gain_ref, ids_ref, scores_ref, out_ref):
    steps, rows, width = tokens_ref.shape
    top = ids_ref.shape[2]
    for s in range(steps):
        values = tokens_ref[s].astype(F32)
        mean = jnp.mean(values * values, axis=-1, keepdims=True)
        normed = (values * lax.rsqrt(mean + epsilon) * gain_ref[...]).astype(BF16)
        at = slice(s * rows, (s + 1) * rows)
        out_ref[at, :width] = normed
        scores = scores_ref[s]
        weights = scores / jnp.sum(scores, axis=-1, keepdims=True)
        high = weights.astype(BF16)
        rest = weights - high.astype(F32)
        middle = rest.astype(BF16)
        low = (rest - middle.astype(F32)).astype(BF16)
        lane = lax.broadcasted_iota(jnp.int32, (rows, META), 1)
        meta = jnp.zeros((rows, META), F32)
        parts = (ids_ref[s].astype(F32), high.astype(F32), middle.astype(F32), low.astype(F32))
        for p, part in enumerate(parts):
            for k in range(top):
                meta = jnp.where(lane == p * top + k, part[:, k : k + 1], meta)
        out_ref[at, width:] = meta.astype(BF16)


def pack(tokens, gain, ids, scores):
    steps, rows, width = tokens.shape
    return pl.pallas_call(
        pack_kernel,
        out_shape=jax.ShapeDtypeStruct((steps * rows, width + META), BF16),
        compiler_params=params(),
    )(tokens, gain.reshape(1, width), ids, scores)


def dequant_kernel(codes_ref, scales_ref, spread_ref, out_ref):
    width = codes_ref.shape[2]
    chunk = 256
    scales = scales_ref[0]
    for at in range(0, width, chunk):
        end = min(at + chunk, width)
        wide = dot(scales, spread_ref[:, at:end], ((1,), (0,)))
        out_ref[0, :, at:end] = (codes_ref[0, :, at:end].astype(F32) * wide).astype(BF16)


def dequant(codes, scales):
    count, rows, width = codes.shape
    blocks = scales.shape[2]
    spread = (
        jnp.arange(blocks)[:, None] == jnp.arange(width)[None, :] // (width // blocks)
    ).astype(BF16)
    return pl.pallas_call(
        dequant_kernel,
        grid=(count,),
        in_specs=[
            pl.BlockSpec((1, rows, width), lambda i: (i, 0, 0)),
            pl.BlockSpec((1, rows, blocks), lambda i: (i, 0, 0)),
            pl.BlockSpec((blocks, width), lambda i: (0, 0)),
        ],
        out_specs=pl.BlockSpec((1, rows, width), lambda i: (i, 0, 0)),
        out_shape=jax.ShapeDtypeStruct(codes.shape, BF16),
        compiler_params=params(),
        cost_estimate=pl.CostEstimate(
            flops=2 * count * rows * width * 128,
            bytes_accessed=4 * count * rows * width,
            transcendentals=0,
        ),
    )(codes, scales, spread)


class Plan:
    def __init__(self, first, rows, holds, slots, subs, group, top, eps):
        self.first, self.rows = first, rows
        self.holds = holds
        self.slots, self.subs, self.group, self.top, self.eps = slots, subs, group, top, eps


def chosen(meta, expert, top):
    named = jnp.zeros((meta.shape[0], 1), F32)
    weight = jnp.zeros((meta.shape[0], 1), F32)
    for k in range(top):
        hit = (meta[:, META + k : META + k + 1] == expert).astype(F32)
        at = META + k
        total = (
            meta[:, at + top : at + top + 1]
            + meta[:, at + 2 * top : at + 2 * top + 1]
            + meta[:, at + 3 * top : at + 3 * top + 1]
        )
        named = named + hit
        weight = weight + hit * total
    return named, weight


def order_mask(count, plan, sub):
    def key(dim):
        t = lax.broadcasted_iota(jnp.int32, (count, count), dim)
        block = lax.rem(lax.div(t, plan.group), plan.subs)
        return t + (jnp.bitwise_xor(block, sub) - block) * plan.group

    return (key(1) < key(0)).astype(BF16)


def route(metas, plan, ep, sub):
    count = metas[0].shape[0]
    earlier = order_mask(count, plan, sub)
    lane = lax.broadcasted_iota(jnp.int32, (count, LANES), 1)
    start = jnp.zeros((1, 1), F32)
    result = []
    bounds = []
    for column, meta in enumerate(metas):
        if column:
            start = jnp.maximum(start, float(plan.holds[column - 1]))
        found = []
        flags = jnp.zeros((count, LANES), F32)
        for slot in range(plan.slots):
            named, weight = chosen(meta, (ep * plan.slots + slot).astype(F32), plan.top)
            found.append((named, weight))
            flags = jnp.where(lane == slot, named, flags)
        prefix = dot(earlier, flags.astype(BF16), ((1,), (0,)))
        places = []
        for slot, (named, weight) in enumerate(found):
            place = jnp.where(named > 0.0, prefix[:, slot : slot + 1] + start, -1.0)
            places.append((place, weight))
            end = start + jnp.sum(named, axis=0, keepdims=True)
            bounds.append((slot, start, end))
            start = end
        result.append(places)
    return result, bounds


def slot_masks(bounds, plan):
    row = lax.broadcasted_iota(jnp.int32, (1, plan.rows), 1).astype(F32) + float(plan.first)
    masks = []
    for slot in range(plan.slots):
        mask = jnp.zeros((1, plan.rows), F32)
        for which, start, end in bounds:
            if which == slot:
                mask = mask + jnp.logical_and(row >= start, row < end).astype(F32)
        masks.append(mask)
    return masks


def rows_of(places, plan):
    return (
        lax.broadcasted_iota(jnp.int32, (places.shape[0], plan.rows), 1).astype(F32)
        + float(plan.first)
        == places
    )


def inner_kernel(plan, arrays, place_ref, *refs):
    tokens = refs[:arrays]
    weight_ref = refs[arrays]
    act_ref, most_ref = refs[arrays + 1], refs[arrays + 2]
    rows_ref, mask_ref = refs[arrays + 3], refs[arrays + 4]
    width = weight_ref.shape[3]

    @pl.when(pl.program_id(0) == 0)
    def _():
        ep, sub = place_ref[0], place_ref[1]
        metas = []
        for c in range(arrays // 2):
            pair = [tokens[2 * c + h][:, width - META :].astype(F32) for h in range(2)]
            metas.append(jnp.concatenate(pair, axis=0))
        columns, bounds = route(metas, plan, ep, sub)
        for slot, mask in enumerate(slot_masks(bounds, plan)):
            mask_ref[slot : slot + 1] = mask
        half = tokens[0].shape[0]
        hots = []
        for places in columns:
            hot = None
            for place, _w in places:
                hit = rows_of(place, plan).astype(F32)
                hot = hit if hot is None else hot + hit
            hots.append(hot.astype(BF16))
        chunk = 256
        for at in range(0, width, chunk):
            end = min(at + chunk, width)
            total = None
            for c, hot in enumerate(hots):
                for h in range(2):
                    part = dot(
                        tokens[2 * c + h][:, at:end], hot[h * half : (h + 1) * half], ((0,), (0,))
                    )
                    total = part if total is None else total + part
            rows_ref[at:end] = total.astype(BF16)
        lane = lax.broadcasted_iota(jnp.int32, (metas[0].shape[0], LANES), 1).astype(F32)
        start = [jnp.zeros((1, 1), F32)] * plan.eps
        owner = lax.div(lax.broadcasted_iota(jnp.int32, (1, LANES), 1), plan.slots)
        for column, meta in enumerate(metas):
            flags = jnp.zeros((meta.shape[0], LANES), F32)
            for k in range(plan.top):
                flags = flags + (meta[:, META + k : META + k + 1] == lane).astype(F32)
            counts = jnp.sum(flags, axis=0, keepdims=True)
            for e in range(plan.eps):
                if column:
                    start[e] = jnp.maximum(start[e], float(plan.holds[column - 1]))
                start[e] = start[e] + jnp.sum(
                    jnp.where(owner == e, counts, 0.0), axis=1, keepdims=True
                )
        most_ref[...] = jnp.broadcast_to(functools.reduce(jnp.maximum, start), most_ref.shape)

    gating = upward = None
    x = rows_ref[...]
    for slot in range(plan.slots):
        gate = dot(weight_ref[slot, 0], x, ((1,), (0,)))
        up = dot(weight_ref[slot, 1], x, ((1,), (0,)))
        if slot == 0:
            gating, upward = gate, up
        else:
            mine = mask_ref[slot : slot + 1] > 0.0
            gating = jnp.where(mine, gate, gating)
            upward = jnp.where(mine, up, upward)
    act_ref[...] = (gating * jax.nn.sigmoid(swish_beta * gating) * (upward + 1.0)).astype(BF16)


def piece(total):
    for size in (144, 120, 72, 40, 24, 16, 8):
        if total % size == 0:
            return size
    return total


def inner(plan, place, tokens, weights):
    slots, _two, units, width = weights.shape
    block = piece(units)
    arrays = len(tokens)
    return pl.pallas_call(
        functools.partial(inner_kernel, plan, arrays),
        grid=(units // block,),
        in_specs=[pl.BlockSpec(memory_space=pltpu.SMEM)]
        + [pl.BlockSpec(t.shape, lambda i: (0, 0)) for t in tokens]
        + [pl.BlockSpec((slots, 2, block, width), lambda i: (0, 0, i, 0))],
        out_specs=[
            pl.BlockSpec((block, plan.rows), lambda i: (i, 0)),
            pl.BlockSpec((8, LANES), lambda i: (0, 0)),
        ],
        out_shape=[
            jax.ShapeDtypeStruct((units, plan.rows), BF16),
            jax.ShapeDtypeStruct((8, LANES), F32),
        ],
        scratch_shapes=[
            pltpu.VMEM((width, plan.rows), BF16),
            pltpu.VMEM((8, plan.rows), F32),
        ],
        compiler_params=params(),
        cost_estimate=pl.CostEstimate(
            flops=2 * plan.rows * slots * 2 * units * width,
            bytes_accessed=slots * 2 * units * width * 2,
            transcendentals=units * plan.rows,
        ),
    )(place, *tokens, weights)


def outer_kernel(plan, arrays, before, blocks, place_ref, *refs):
    metas_in = refs[:arrays]
    parts = refs[arrays : arrays + blocks]
    befores = refs[arrays + blocks : arrays + blocks + before]
    rest = refs[arrays + blocks + before :]
    weight_ref, keep_ref, send_ref, act_ref, sum_ref = rest
    sub = place_ref[1]
    units = parts[0].shape[0]
    slot = pl.program_id(0)

    @pl.when(slot == 0)
    def _():
        for b in range(plan.subs):
            for k in range(plan.subs):

                @pl.when(jnp.bitwise_xor(sub, k) == b)
                def _():
                    at = slice(b * units, (b + 1) * units)
                    if k == 3 and blocks == 5:
                        inside = jnp.logical_or(sub == 1, sub == 2)

                        @pl.when(inside)
                        def _():
                            act_ref[at] = parts[3][...]

                        @pl.when(jnp.logical_not(inside))
                        def _():
                            act_ref[at] = parts[4][...]
                    else:
                        act_ref[at] = parts[k][...]

    ep = place_ref[0]

    def routed():
        metas = []
        for c in range(arrays // 2):
            pair = [metas_in[2 * c + h][...].astype(F32) for h in range(2)]
            metas.append(jnp.concatenate(pair, axis=0))
        return route(metas, plan, ep, sub)

    out = dot(weight_ref[0], act_ref[...], ((1,), (0,)))

    @pl.when(slot == 0)
    def _():
        sum_ref[...] = out.astype(BF16)

    @pl.when(slot > 0)
    def _():
        _columns, bounds = routed()
        masks = slot_masks(bounds, plan)
        mine = masks[0]
        for s in range(1, plan.slots):
            mine = jnp.where(slot == s, masks[s], mine)
        sum_ref[...] = jnp.where(mine > 0.0, out.astype(BF16), sum_ref[...])

    @pl.when(slot == plan.slots - 1)
    def _():
        columns, _bounds = routed()
        done = sum_ref[...]
        for c, places in enumerate(columns):
            mix = None
            for place, weight in places:
                part = jnp.where(rows_of(place, plan), weight, 0.0)
                mix = part if mix is None else mix + part
            high = mix.astype(BF16)
            low = (mix - high.astype(F32)).astype(BF16)
            total = dot(high, done, ((1,), (1,))) + dot(low, done, ((1,), (1,)))
            half = total.shape[0] // 2
            for h, ref in enumerate((keep_ref, send_ref)):
                value = total[h * half : (h + 1) * half]
                if before and c < befores[h].shape[0]:
                    value = value + befores[h][c].astype(F32)
                ref[c] = value.astype(BF16)


def outer(plan, place, tokens, parts, befores, weights):
    slots, columns_out, width = weights.shape
    arrays, blocks = len(tokens), len(parts)
    half = tokens[0].shape[0]
    last = tokens[0].shape[1] // LANES - 1
    result = jax.ShapeDtypeStruct((arrays // 2, half, columns_out), BF16)
    return pl.pallas_call(
        functools.partial(outer_kernel, plan, arrays, len(befores), blocks),
        grid=(slots,),
        in_specs=[pl.BlockSpec(memory_space=pltpu.SMEM)]
        + [pl.BlockSpec((half, LANES), lambda i: (0, last)) for t in tokens]
        + [pl.BlockSpec(p.shape, lambda i: (0, 0)) for p in parts]
        + [pl.BlockSpec(b.shape, lambda i: (0, 0, 0)) for b in befores]
        + [pl.BlockSpec((1, columns_out, width), lambda i: (i, 0, 0))],
        out_specs=[pl.BlockSpec(result.shape, lambda i: (0, 0, 0))] * 2,
        out_shape=[result, result],
        scratch_shapes=[
            pltpu.VMEM((width, plan.rows), BF16),
            pltpu.VMEM((columns_out, plan.rows), BF16),
        ],
        compiler_params=params(),
        cost_estimate=pl.CostEstimate(
            flops=2 * plan.rows * slots * columns_out * width,
            bytes_accessed=slots * columns_out * width * 2,
            transcendentals=0,
        ),
    )(place, *tokens, *parts, *befores, weights)


def finish_kernel(subs, place_ref, *refs):
    parts, out_ref = refs[:subs], refs[subs]
    sub = place_ref[1]
    width = parts[0].shape[1]
    steps, rows, _ = out_ref.shape
    for b in range(subs):
        value = parts[0][...]
        for k in range(1, subs):
            value = jnp.where(jnp.bitwise_xor(sub, k) == b, parts[k][...], value)
        for s in range(steps):
            out_ref[s, :, b * width : (b + 1) * width] = value[s * rows : (s + 1) * rows]


def finish(place, parts, steps):
    rows, width = parts[0].shape
    subs = len(parts)
    return pl.pallas_call(
        functools.partial(finish_kernel, subs),
        in_specs=[pl.BlockSpec(memory_space=pltpu.SMEM)]
        + [pl.BlockSpec(memory_space=pltpu.VMEM)] * subs,
        out_specs=pl.BlockSpec(memory_space=pltpu.VMEM),
        out_shape=jax.ShapeDtypeStruct((steps, rows // steps, width * subs), BF16),
        compiler_params=params(),
    )(place, *parts)


def swap(x, axis, offset, count):
    return lax.ppermute(x, axis, [(i, i ^ offset) for i in range(count)])


def gather_sub(x, subs):
    if subs != 4:
        return [x] + [swap(x, "sub", k, subs) for k in range(1, subs)]
    two = swap(x, "sub", 2, subs)
    one = swap(x, "sub", 1, subs)
    middle = lax.ppermute(x, "sub", [(1, 2), (2, 1)])
    ends = lax.ppermute(two, "sub", [(2, 3), (1, 0)])
    return [x, one, two, middle, ends]


def add(a, b):
    return (a.astype(F32) + b.astype(F32)).astype(BF16)


def local(
    tokens, norm_gain, copy_ids, gate_scores, inner_codes, inner_scales, down_codes, down_scales
):
    eps, subs, groups = lax.axis_size("ep"), lax.axis_size("sub"), lax.axis_size("grp")
    slots = inner_codes.shape[0]
    steps, rows, top = copy_ids.shape
    units = inner_codes.shape[3]
    experts = eps * slots
    capacity = (3 * rows * top + 2 * experts - 1) // (2 * experts)
    columns = eps // 2
    place = jnp.stack([lax.axis_index("ep"), lax.axis_index("sub")]).astype(jnp.int32)
    group = steps * rows

    packed = pack(tokens, norm_gain, copy_ids, gate_scores)
    near = [packed] + [swap(packed, "sub", k, subs) for k in range(1, subs)]
    codes = jnp.transpose(inner_codes, (0, 2, 3, 1)).reshape(slots * 2, units, -1)
    scales = jnp.transpose(inner_scales, (0, 2, 3, 1)).reshape(slots * 2, units, -1)
    inner_weights = dequant(codes, scales).reshape(slots, 2, units, -1)
    outer_weights = dequant(
        jnp.transpose(down_codes, (0, 2, 1)), jnp.transpose(down_scales, (0, 2, 1))
    )
    own = jnp.concatenate(near, axis=0)
    other = swap(own, "ep", 1, eps)
    held = [[own, other]]
    for j in range(1, columns):
        arrived = swap(own, "ep", 2 * j, eps)
        held.append([arrived, swap(arrived, "ep", 1, eps)])

    capacity_rows = group * subs * 2 // rows * slots * capacity

    def plan(first, count, holds):
        return Plan(first, count, holds, slots, subs, group, top, eps)

    if columns == 2 and capacity_rows % 384 == 0:
        most = 2 * capacity_rows
        first = capacity_rows // 384 * 256
        second = capacity_rows
        last = most - first - second
        holds = (first,)
        plan0, plan1 = plan(0, first, holds), plan(first, second, holds)
        plan2 = plan(first + second, last, holds)
        everything = held[0] + held[1]
        act0, _ = inner(plan0, place, held[0], inner_weights)
        parts0 = gather_sub(act0, subs)
        act1, longest = inner(plan1, place, everything, inner_weights)
        parts1 = gather_sub(act1, subs)
        for shift in range(1, groups):
            moved = lax.ppermute(
                longest, "grp", [(i, (i + shift) % groups) for i in range(groups)]
            )
            longest = jnp.maximum(longest, moved)
        sums = outer(plan0, place, held[0], parts0, [], outer_weights)
        sums = outer(plan1, place, everything, parts1, sums, outer_weights)

        def more(kept, sent):
            act, _ = inner(plan2, place, everything, inner_weights)
            return tuple(
                outer(
                    plan2, place, everything, gather_sub(act, subs), [kept, sent], outer_weights
                )
            )

        keep, send = lax.cond(
            longest[0, 0] > float(first + second), more, lambda a, b: (a, b), *sums
        )
    else:
        count = -(-capacity_rows // LANES) * LANES
        each = plan(0, count, ())
        keeps, sends = [], []
        for pair in held:
            act, _ = inner(each, place, pair, inner_weights)
            kept, sent = outer(each, place, pair, gather_sub(act, subs), [], outer_weights)
            keeps.append(kept)
            sends.append(sent)
        keep, send = jnp.concatenate(keeps, axis=0), jnp.concatenate(sends, axis=0)

    chip = add(keep, swap(send, "ep", 1, eps))
    total = chip[0].astype(F32)
    for j in range(1, columns):
        total = total + swap(chip[j], "ep", 2 * j, eps).astype(F32)
    total = total.astype(BF16).reshape(subs, group, -1)
    arrived = [total[0]] + [swap(total[k], "sub", k, subs) for k in range(1, subs)]
    return finish(place, arrived, steps)


def solution(mesh):
    return jax.shard_map(
        local,
        mesh=mesh,
        in_specs=(
            P(None, ("grp", "ep", "sub"), None),
            P(),
            P(None, ("grp", "ep", "sub"), None),
            P(None, ("grp", "ep", "sub"), None),
            P("ep", None, None, "sub"),
            P("ep", None, None, "sub"),
            P("ep", None, "sub"),
            P("ep", None, "sub"),
        ),
        out_specs=P(None, ("grp", "ep", "sub"), None),
        check_vma=False,
    )
```

time: 339 us -> 190 us (0.56)
  local copies, waits for them, and re-layouts: 120 us -> 9.14 us
  Pallas kernels: 0 us -> 73 us
  waiting for transfers between devices: 118 us -> 73.9 us
  matrix products: 38.3 us -> 0 us
  other arithmetic: 21.7 us -> 2.11 us
  starting transfers between devices: 11.1 us -> 30.1 us
  blocking collectives: 13.3 us -> 0 us
  between operations: 13.4 us -> 0.77 us
    all_gather x4 -> x0, waiting for transfers between devices: 103 us -> none  [the longest x2 83.2 us: local(): lax.all_gather(activation, 'sub', axis=3, tiled=True)]
    mul x5 -> x0, local copies, waits for them, and re-layouts: 88 us -> none  [the longest x3 72.2 us: dequant_inner(): product = grouped * scales[:, :, None]]
    ppermute x0 -> x20, waiting for transfers between devices: none -> 73.9 us  [the longest x15 67.3 us: swap(): return lax.ppermute(x, axis, [(i, i ^ offset) for i in range(count)])]
    pallas_call x0 -> x8, Pallas kernels: none -> 73 us  [the longest x2 27.8 us: inner(): pl.pallas_call(functools.partial(inner_kernel, plan, arrays), grid=(units...]
    dot_general x10 -> x0, matrix products: 38.3 us -> none  [the longest x2 18.2 us: local(): jnp.einsum('sjrd,jdf->sjrf', gathered_rows, inner_weights, preferred_elem...]
    ppermute x0 -> x20, starting transfers between devices: none -> 30.1 us  [the longest x15 22.9 us: swap(): return lax.ppermute(x, axis, [(i, i ^ offset) for i in range(count)])]
    all_gather x4 -> x0, local copies, waits for them, and re-layouts: 18 us -> none  [the longest x2 14.3 us: local(): lax.all_gather(activation, 'sub', axis=3, tiled=True)]
    mul x1 -> x0, other arithmetic: 17.5 us -> none  [dequant_inner(): product = grouped * scales[:, :, None]]
  transfers between devices with their start and end apart: 7 -> 20, of which waited for: 4 -> 9; matrix products, arithmetic and copies ran while one was open for 51% -> 3% of each run, Pallas kernels for 0% -> 22%
where the time goes in v1:
time: 190 us; the launch traced here: 189 us
  waiting for transfers between devices  73.9 us (39%)
  Pallas kernels  73 us (38%)
  starting transfers between devices  30.1 us (16%)
  local copies, waits for them, and re-layouts  9.14 us (5%)
  other arithmetic  2.11 us (1%)
    ppermute x15, waiting for transfers between devices, swap(): return lax.ppermute(x, axis, [(i, i ^ offset) for i in range(count)])  67.3 us
    pallas_call x2, Pallas kernels, inner(): pl.pallas_call(functools.partial(inner_kernel, plan, arrays), grid=(units...  27.8 us
    ppermute x15, starting transfers between devices, swap(): return lax.ppermute(x, axis, [(i, i ^ offset) for i in range(count)])  22.9 us
    pallas_call x2, Pallas kernels, dequant(): pl.pallas_call(dequant_kernel, grid=(count,), in_specs=[pl.BlockSpec((1,...  21.7 us
    pallas_call x2, Pallas kernels, outer(): pl.pallas_call(functools.partial(outer_kernel, plan, arrays, len(befores)...  19.9 us
    ppermute x2, waiting for transfers between devices, gather_sub(): ends = lax.ppermute(two, 'sub', [(2, 3), (1, 0)])  6.54 us
    unnamed x15, local copies, waits for them, and re-layouts  5.31 us
  transfers between devices with their start and end apart: 20, of which 9 were waited for; matrix products, arithmetic and copies ran while one was open for 3% of the time, Pallas kernels for 22%

profile of v1, /device:TPU:0, one launch (start us, length us, event | category | flops | bytes accessed | tf_op | source)
XLA Modules:
  0.0 189.0 jit_solution(15903082004300061111)
XLA Ops:
  0.0 1.4 reshape.64.gain_ref
  1.4 1.4 copy.9.ids_ref
  2.7 1.4 copy.10.scores_ref
  4.1 1.9 %shard_map.82 = bf16[32,2944]{1,0:T(8,128)(2,1)} custom-call(bf16[2,16,2880]{2,1,0:T(8,128)(2,1)} %tokens_ref.1, f32[1,2880]{1,0:T(1,128)} %reshape.64.gain_ref, s32[2,16,4]{2,1,0:T(8,128)} %copy.9.ids_ref, f32[2,16,4]{2,1,0:T(8,128)} %copy.10.scores_ref), custom_call_target="tpu_custom_call" | custom-call | tf_op jit(solution)/shard_map/pallas_call | solution.py:53
  6.0 5.0 %collective-permute-start.6 = (bf16[32,2944]{1,0:T(8,128)(2,1)}, bf16[32,2944]{1,0:T(8,128)(2,1)S(1)}, u32[]{:S(2)}, u32[]{:S(2)}) collective-permute-start(bf16[32,2944]{1,0:T(8,128)(2,1)} %shard_map.82), channel_id=1, source_target_pairs={{0,3},{1,2},{2,1},{3,0},{4,7},{5,6},{6,5},{7,4},{8,11},{9,10},{10,... | collective-permute-start | bytes 565256 | tf_op jit(solution)/shard_map/ppermute | solution.py:410
  11.7 5.3 %collective-permute-done.6 = bf16[32,2944]{1,0:T(8,128)(2,1)S(1)} collective-permute-done((bf16[32,2944]{1,0:T(8,128)(2,1)}, bf16[32,2944]{1,0:T(8,128)(2,1)S(1)}, u32[]{:S(2)}, u32[]{:S(2)}) %collective-permute-start.6) | collective-permute-done | bytes 188448 | tf_op jit(solution)/shard_map/ppermute | solution.py:410
  17.0 10.3 %collective-permute-done.5 = bf16[32,2944]{1,0:T(8,128)(2,1)S(1)} collective-permute-done((bf16[32,2944]{1,0:T(8,128)(2,1)}, bf16[32,2944]{1,0:T(8,128)(2,1)S(1)}, u32[]{:S(2)}, u32[]{:S(2)}) %collective-permute-start.5) | collective-permute-done | bytes 188448 | tf_op jit(solution)/shard_map/ppermute | solution.py:410
  28.3 1.6 collective-permute-start.8
  29.8 1.3 copy.11
  31.2 15.0 %collective-permute-done.8.refs_2_ = bf16[128,2944]{1,0:T(8,128)(2,1)S(1)} collective-permute-done((bf16[128,2944]{1,0:T(8,128)(2,1)S(1)}, bf16[128,2944]{1,0:T(8,128)(2,1)S(1)}, u32[]{:S(2)}, u32[]{:S(2)}) %collective-permute-start.8) | collective-permute-done | bytes 753696 | tf_op jit(solution)/shard_map/ppermute | solution.py:410
  47.2 14.6 %shard_map.83 = bf16[4,720,2880]{2,1,0:T(8,128)(2,1)} custom-call(bf16[4,720,2880]{2,1,0:T(8,128)(2,1)} %bitcast.21, bf16[4,720,90]{2,1,0:T(8,128)(2,1)} %bitcast.23, bf16[90,2880]{1,0:T(8,128)(2,1)} %fusion.spread_ref), custom_call_target="tpu_custom_call" | custom-call | flops 2123366400 | bytes 33177600 | tf_op jit(solution)/shard_map/pallas_call | solution.py:76
  61.8 16.2 %shard_map.84 = (bf16[720,384]{1,0:T(8,128)(2,1)}, f32[8,128]{1,0:T(8,128)}) custom-call(s32[2]{0:T(128)S(1)} %pad_add_fusion.place_ref, bf16[128,2944]{1,0:T(8,128)(2,1)S(1)} %pad_maximum_fusion.refs_0_, bf16[128,2944]{1,0:T(8,128)(2,1)S(1)} %collective-permute-done.7.refs_1_, bf16[128,2944]{1,0:T(8,128)(2,1)S(1)} %collective-permute-done.8.refs_2_, ...), custom_call_target="tpu_custom_call" | custom-call | flops 6370099200 | bytes 16588800 | tf_op jit(solution)/shard_map/pallas_call | solution.py:252
  78.0 11.5 %shard_map.85 = (bf16[720,256]{1,0:T(8,128)(2,1)}, f32[8,128]{1,0:T(8,128)}) custom-call(s32[2]{0:T(128)S(1)} %pad_add_fusion.place_ref, bf16[128,2944]{1,0:T(8,128)(2,1)S(1)} %pad_maximum_fusion.refs_0_, bf16[128,2944]{1,0:T(8,128)(2,1)S(1)} %collective-permute-done.7.refs_1_, bf16[2,2,720,2880]{3,2,1,0:T(8,128)(2,1)} %bitcast.19), custom_call_target="tpu_custom_call" | custom-call | flops 4246732800 | bytes 16588800 | tf_op jit(solution)/shard_map/pallas_call | solution.py:252
  89.6 2.9 %collective-permute-start.16 = (bf16[720,256]{1,0:T(8,128)(2,1)}, bf16[720,256]{1,0:T(8,128)(2,1)S(1)}, u32[]{:S(2)}, u32[]{:S(2)}) collective-permute-start(bf16[720,256]{1,0:T(8,128)(2,1)} %get-tuple-element.57.refs_2_), channel_id=1, source_target_pairs={{0,2},{1,3},{2,0},{3,1},{4,6},{5,7},{6,4},{7,5},{8,10},{9,11},{10,... | collective-permute-start | bytes 1105928 | tf_op jit(solution)/shard_map/ppermute | solution.py:410
  92.5 1.4 collective-permute-start.17
  95.0 26.4 %collective-permute-done.16.refs_4_ = bf16[720,256]{1,0:T(8,128)(2,1)S(1)} collective-permute-done((bf16[720,256]{1,0:T(8,128)(2,1)}, bf16[720,256]{1,0:T(8,128)(2,1)S(1)}, u32[]{:S(2)}, u32[]{:S(2)}) %collective-permute-start.16) | collective-permute-done | bytes 368672 | tf_op jit(solution)/shard_map/ppermute | solution.py:410
  122.8 1.5 collective-permute-start.13
  124.2 5.7 %collective-permute-start.11 = (bf16[720,384]{1,0:T(8,128)(2,1)}, bf16[720,384]{1,0:T(8,128)(2,1)}, u32[]{:S(2)}, u32[]{:S(2)}) collective-permute-start(bf16[720,384]{1,0:T(8,128)(2,1)} %get-tuple-element.56.refs_4_), channel_id=1, source_target_pairs={{0,1},{1,0},{2,3},{3,2},{4,5},{5,4},{6,7},{7,6},{8,9},{9,8},{10,11... | collective-permute-start | bytes 1658888 | tf_op jit(solution)/shard_map/ppermute | solution.py:410
  130.0 1.5 collective-permute-start.14
  131.5 1.9 %copy.12 = bf16[2,90,720]{1,2,0:T(8,128)(2,1)} copy(bf16[2,90,720]{2,0,1:T(2,128)(2,1)} %param.17) | data formatting | bytes 518400 | tf_op args[7]
  133.4 7.0 %shard_map.86.refs_7_.refs_11_ = bf16[2,720,2880]{2,1,0:T(8,128)(2,1)} custom-call(bf16[2,720,2880]{2,1,0:T(8,128)(2,1)} %bitcast.22, bf16[2,720,90]{2,1,0:T(8,128)(2,1)} %bitcast.24, bf16[90,2880]{1,0:T(8,128)(2,1)} %fusion.spread_ref), custom_call_target="tpu_custom_call" | custom-call | flops 1061683200 | bytes 16588800 | tf_op jit(solution)/shard_map/pallas_call | solution.py:76
  140.4 1.6 collective-permute-start.10
  142.0 7.9 %shard_map.87 = (bf16[1,128,720]{2,1,0:T(8,128)(2,1)}, bf16[1,128,720]{2,1,0:T(8,128)(2,1)}) custom-call(s32[2]{0:T(128)S(1)} %pad_add_fusion.place_ref, bf16[128,2944]{1,0:T(8,128)(2,1)S(1)} %pad_maximum_fusion.refs_0_, bf16[128,2944]{1,0:T(8,128)(2,1)S(1)} %collective-permute-done.7.refs_1_, bf16[720,256]{1,0:T(8,128)(2,1)} %get-tuple-element.57.refs_2_, ...), custom_call_target="tpu_custom_call" | custom-call | flops 2123366400 | bytes 8294400 | tf_op jit(solution)/shard_map/pallas_call | solution.py:360
  151.1 6.5 %collective-permute-done.14.refs_8_ = bf16[720,384]{1,0:T(8,128)(2,1)} collective-permute-done((bf16[720,384]{1,0:T(8,128)(2,1)}, bf16[720,384]{1,0:T(8,128)(2,1)}, u32[]{:S(2)}, u32[]{:S(2)}) %collective-permute-start.14) | collective-permute-done | bytes 552992 | tf_op jit(solution)/shard_map/ppermute | solution.py:419
  157.7 12.1 %shard_map.88 = (bf16[2,128,720]{2,1,0:T(8,128)(2,1)S(1)}, bf16[2,128,720]{2,1,0:T(8,128)(2,1)}) custom-call(s32[2]{0:T(128)S(1)} %pad_add_fusion.place_ref, bf16[128,2944]{1,0:T(8,128)(2,1)S(1)} %pad_maximum_fusion.refs_0_, bf16[128,2944]{1,0:T(8,128)(2,1)S(1)} %collective-permute-done.7.refs_1_, bf16[128,2944]{1,0:T(8,128)(2,1)S(1)} %collective-permute-done.8.refs_2_, ...), custom_call_target="tpu_custom_call" | custom-call | flops 3185049600 | bytes 8294400 | tf_op jit(solution)/shard_map/pallas_call | solution.py:360
  169.7 1.9 %collective-permute-done.19 = bf16[2,128,720]{2,1,0:T(8,128)(2,1)S(1)} collective-permute-done((bf16[2,128,720]{2,1,0:T(8,128)(2,1)}, bf16[2,128,720]{2,1,0:T(8,128)(2,1)S(1)}, u32[]{:S(2)}, u32[]{:S(2)}) %collective-permute-start.19) | collective-permute-done | bytes 368672 | tf_op jit(solution)/shard_map/ppermute | solution.py:410
  171.8 1.6 collective-permute-start.20
  173.3 5.5 %collective-permute-done.20 = bf16[128,720]{1,0:T(8,128)(2,1)S(1)} collective-permute-done((bf16[128,720]{1,0:T(8,128)(2,1)S(1)}, bf16[128,720]{1,0:T(8,128)(2,1)S(1)}, u32[]{:S(2)}, u32[]{:S(2)}) %collective-permute-start.20) | collective-permute-done | bytes 184352 | tf_op jit(solution)/shard_map/ppermute | solution.py:410
  179.5 1.5 collective-permute-start.23
  181.0 2.9 %collective-permute-start.21 = (bf16[32,720]{1,0:T(8,128)(2,1)S(1)}, bf16[32,720]{1,0:T(8,128)(2,1)S(1)}, u32[]{:S(2)}, u32[]{:S(2)}) collective-permute-start(bf16[32,720]{1,0:T(8,128)(2,1)S(1)} %get-tuple-element.71), channel_id=1, source_target_pairs={{0,1},{1,0},{2,3},{3,2},{4,5},{5,4},{6,7},{7,6},{8,9},{9,8},{10,11... | collective-permute-start | bytes 138248 | tf_op jit(solution)/shard_map/ppermute | solution.py:410
  183.8 2.0 %collective-permute-done.23.refs_3_ = bf16[32,720]{1,0:T(8,128)(2,1)S(1)} collective-permute-done((bf16[32,720]{1,0:T(8,128)(2,1)S(1)}, bf16[32,720]{1,0:T(8,128)(2,1)S(1)}, u32[]{:S(2)}, u32[]{:S(2)}) %collective-permute-start.23) | collective-permute-done | bytes 46112 | tf_op jit(solution)/shard_map/ppermute | solution.py:410
  187.4 1.7 shard_map.89
  (44 shorter events, 7.8 us)
Async XLA Ops:
  0.0 29.8 %copy-start = (bf16[2,90,2,720]{3,2,1,0:T(2,128)(2,1)S(1)}, bf16[2,90,2,720]{3,2,1,0:T(2,128)(2,1)}, u32[]{:S(2)}) copy-start(bf16[2,90,2,720]{3,2,1,0:T(2,128)(2,1)} %param.15) | copy-start | bytes 1555204
  6.0 11.0 %collective-permute-start.6 = (bf16[32,2944]{1,0:T(8,128)(2,1)}, bf16[32,2944]{1,0:T(8,128)(2,1)S(1)}, u32[]{:S(2)}, u32[]{:S(2)}) collective-permute-start(bf16[32,2944]{1,0:T(8,128)(2,1)} %shard_map.82), channel_id=1, source_target_pairs={{0,3},{1,2},{2,1},{3,0},{4,7},{5,6},{6,5},{7,4},{8,11},{9,10},{10,... | collective-permute-start | bytes 565256 | tf_op jit(solution)/shard_map/ppermute | solution.py:410
  11.1 16.2 %collective-permute-start.5 = (bf16[32,2944]{1,0:T(8,128)(2,1)}, bf16[32,2944]{1,0:T(8,128)(2,1)S(1)}, u32[]{:S(2)}, u32[]{:S(2)}) collective-permute-start(bf16[32,2944]{1,0:T(8,128)(2,1)} %shard_map.82), channel_id=1, source_target_pairs={{0,2},{1,3},{2,0},{3,1},{4,6},{5,7},{6,4},{7,5},{8,10},{9,11},{10,... | collective-permute-start | bytes 565256 | tf_op jit(solution)/shard_map/ppermute | solution.py:410
  11.1 16.2 %collective-permute-start.4 = (bf16[32,2944]{1,0:T(8,128)(2,1)}, bf16[32,2944]{1,0:T(8,128)(2,1)S(1)}, u32[]{:S(2)}, u32[]{:S(2)}) collective-permute-start(bf16[32,2944]{1,0:T(8,128)(2,1)} %shard_map.82), channel_id=1, source_target_pairs={{0,1},{1,0},{2,3},{3,2},{4,5},{5,4},{6,7},{7,6},{8,9},{9,8},{10,11... | collective-permute-start | bytes 565256 | tf_op jit(solution)/shard_map/ppermute | solution.py:410
  28.3 18.0 %collective-permute-start.8 = (bf16[128,2944]{1,0:T(8,128)(2,1)S(1)}, bf16[128,2944]{1,0:T(8,128)(2,1)S(1)}, u32[]{:S(2)}, u32[]{:S(2)}) collective-permute-start(bf16[128,2944]{1,0:T(8,128)(2,1)S(1)} %pad_maximum_fusion.refs_0_), channel_id=1, source_target_pairs={{0,8},{4,12},{8,0},{12,4},{1,9},{5,13},{9,1},{13,5},{2,10},{6,14},... | collective-permute-start | bytes 2261000 | tf_op jit(solution)/shard_map/ppermute | solution.py:410
  31.2 30.6 %collective-permute-start.7 = (bf16[128,2944]{1,0:T(8,128)(2,1)S(1)}, bf16[128,2944]{1,0:T(8,128)(2,1)S(1)}, u32[]{:S(2)}, u32[]{:S(2)}) collective-permute-start(bf16[128,2944]{1,0:T(8,128)(2,1)S(1)} %pad_maximum_fusion.refs_0_), channel_id=1, source_target_pairs={{0,4},{4,0},{8,12},{12,8},{1,5},{5,1},{9,13},{13,9},{2,6},{6,2},{1... | collective-permute-start | bytes 2261000 | tf_op jit(solution)/shard_map/ppermute | solution.py:410
  46.2 15.6 %collective-permute-start.9 = (bf16[128,2944]{1,0:T(8,128)(2,1)S(1)}, bf16[128,2944]{1,0:T(8,128)(2,1)S(1)}, u32[]{:S(2)}, u32[]{:S(2)}) collective-permute-start(bf16[128,2944]{1,0:T(8,128)(2,1)S(1)} %collective-permute-done.8.refs_2_), channel_id=1, source_target_pairs={{0,4},{4,0},{8,12},{12,8},{1,5},{5,1},{9,13},{13,9},{2,6},{6,2},{1... | collective-permute-start | bytes 2261000 | tf_op jit(solution)/shard_map/ppermute | solution.py:410
  78.0 52.0 %collective-permute-start.12 = (bf16[720,384]{1,0:T(8,128)(2,1)}, bf16[720,384]{1,0:T(8,128)(2,1)}, u32[]{:S(2)}, u32[]{:S(2)}) collective-permute-start(bf16[720,384]{1,0:T(8,128)(2,1)} %get-tuple-element.56.refs_4_), channel_id=1, source_target_pairs={{0,2},{1,3},{2,0},{3,1},{4,6},{5,7},{6,4},{7,5},{8,10},{9,11},{10,... | collective-permute-start | bytes 1658888 | tf_op jit(solution)/shard_map/ppermute | solution.py:410
  89.6 31.9 %collective-permute-start.16 = (bf16[720,256]{1,0:T(8,128)(2,1)}, bf16[720,256]{1,0:T(8,128)(2,1)S(1)}, u32[]{:S(2)}, u32[]{:S(2)}) collective-permute-start(bf16[720,256]{1,0:T(8,128)(2,1)} %get-tuple-element.57.refs_2_), channel_id=1, source_target_pairs={{0,2},{1,3},{2,0},{3,1},{4,6},{5,7},{6,4},{7,5},{8,10},{9,11},{10,... | collective-permute-start | bytes 1105928 | tf_op jit(solution)/shard_map/ppermute | solution.py:410
  92.5 31.8 %collective-permute-start.17 = (bf16[720,256]{1,0:T(8,128)(2,1)}, bf16[720,256]{1,0:T(8,128)(2,1)}, u32[]{:S(2)}, u32[]{:S(2)}) collective-permute-start(bf16[720,256]{1,0:T(8,128)(2,1)} %get-tuple-element.57.refs_2_), channel_id=1, source_target_pairs={{1,2},{2,1},{5,6},{6,5},{9,10},{10,9},{13,14},{14,13},{17,18},{18,... | collective-permute-start | bytes 1105928 | tf_op jit(solution)/shard_map/ppermute | solution.py:418
  93.9 46.6 %collective-permute-start.15 = (bf16[720,256]{1,0:T(8,128)(2,1)}, bf16[720,256]{1,0:T(8,128)(2,1)}, u32[]{:S(2)}, u32[]{:S(2)}) collective-permute-start(bf16[720,256]{1,0:T(8,128)(2,1)} %get-tuple-element.57.refs_2_), channel_id=1, source_target_pairs={{0,1},{1,0},{2,3},{3,2},{4,5},{5,4},{6,7},{7,6},{8,9},{9,8},{10,11... | collective-permute-start | bytes 1105928 | tf_op jit(solution)/shard_map/ppermute | solution.py:410
  121.5 19.0 %copy-start.2 = (bf16[720,256]{1,0:T(8,128)(2,1)}, bf16[720,256]{1,0:T(8,128)(2,1)S(1)}, u32[]{:S(2)}) copy-start(bf16[720,256]{1,0:T(8,128)(2,1)S(1)} %collective-permute-done.16.refs_4_) | copy-start | bytes 1105924
  121.5 20.6 %collective-permute-start.18 = (bf16[720,256]{1,0:T(8,128)(2,1)S(1)}, bf16[720,256]{1,0:T(8,128)(2,1)}, u32[]{:S(2)}, u32[]{:S(2)}) collective-permute-start(bf16[720,256]{1,0:T(8,128)(2,1)S(1)} %collective-permute-done.16.refs_4_), channel_id=1, source_target_pairs={{2,3},{1,0},{6,7},{5,4},{10,11},{9,8},{14,15},{13,12},{18,19},{17,... | collective-permute-start | bytes 1105928 | tf_op jit(solution)/shard_map/ppermute | solution.py:419
  122.8 28.4 %collective-permute-start.13 = (bf16[720,384]{1,0:T(8,128)(2,1)}, bf16[720,384]{1,0:T(8,128)(2,1)}, u32[]{:S(2)}, u32[]{:S(2)}) collective-permute-start(bf16[720,384]{1,0:T(8,128)(2,1)} %get-tuple-element.56.refs_4_), channel_id=1, source_target_pairs={{1,2},{2,1},{5,6},{6,5},{9,10},{10,9},{13,14},{14,13},{17,18},{18,... | collective-permute-start | bytes 1658888 | tf_op jit(solution)/shard_map/ppermute | solution.py:418
  124.2 26.9 %collective-permute-start.11 = (bf16[720,384]{1,0:T(8,128)(2,1)}, bf16[720,384]{1,0:T(8,128)(2,1)}, u32[]{:S(2)}, u32[]{:S(2)}) collective-permute-start(bf16[720,384]{1,0:T(8,128)(2,1)} %get-tuple-element.56.refs_4_), channel_id=1, source_target_pairs={{0,1},{1,0},{2,3},{3,2},{4,5},{5,4},{6,7},{7,6},{8,9},{9,8},{10,11... | collective-permute-start | bytes 1658888 | tf_op jit(solution)/shard_map/ppermute | solution.py:410
  130.0 27.7 %collective-permute-start.14 = (bf16[720,384]{1,0:T(8,128)(2,1)}, bf16[720,384]{1,0:T(8,128)(2,1)}, u32[]{:S(2)}, u32[]{:S(2)}) collective-permute-start(bf16[720,384]{1,0:T(8,128)(2,1)} %collective-permute-done.12.refs_6_), channel_id=1, source_target_pairs={{2,3},{1,0},{6,7},{5,4},{10,11},{9,8},{14,15},{13,12},{18,19},{17,... | collective-permute-start | bytes 1658888 | tf_op jit(solution)/shard_map/ppermute | solution.py:419
  133.4 7.1 %copy-start.10 = (f32[8,128]{1,0:T(8,128)S(1)}, f32[8,128]{1,0:T(8,128)}, u32[]{:S(2)}) copy-start(f32[8,128]{1,0:T(8,128)} %get-tuple-element.55) | copy-start | bytes 12292
  140.4 9.5 %collective-permute-start.10 = (f32[8,128]{1,0:T(8,128)S(1)}, f32[8,128]{1,0:T(8,128)S(1)}, u32[]{:S(2)}, u32[]{:S(2)}) collective-permute-start(f32[8,128]{1,0:T(8,128)S(1)} %copy-done.10), channel_id=1, source_target_pairs={{0,16},{16,0},{1,17},{17,1},{2,18},{18,2},{3,19},{19,3},{4,20},{20... | collective-permute-start | bytes 12296 | tf_op jit(solution)/shard_map/ppermute | solution.py:474
  169.7 1.9 %collective-permute-start.19 = (bf16[2,128,720]{2,1,0:T(8,128)(2,1)}, bf16[2,128,720]{2,1,0:T(8,128)(2,1)S(1)}, u32[]{:S(2)}, u32[]{:S(2)}) collective-permute-start(bf16[2,128,720]{2,1,0:T(8,128)(2,1)} %get-tuple-element.67), channel_id=1, source_target_pairs={{0,4},{4,0},{8,12},{12,8},{1,5},{5,1},{9,13},{13,9},{2,6},{6,2},{1... | collective-permute-start | bytes 1105928 | tf_op jit(solution)/shard_map/ppermute | solution.py:410
  171.8 7.0 %collective-permute-start.20 = (bf16[128,720]{1,0:T(8,128)(2,1)S(1)}, bf16[128,720]{1,0:T(8,128)(2,1)S(1)}, u32[]{:S(2)}, u32[]{:S(2)}) collective-permute-start(bf16[128,720]{1,0:T(8,128)(2,1)S(1)} %slice_bitcast_fusion), channel_id=1, source_target_pairs={{0,8},{4,12},{8,0},{12,4},{1,9},{5,13},{9,1},{13,5},{2,10},{6,14},... | collective-permute-start | bytes 552968 | tf_op jit(solution)/shard_map/ppermute | solution.py:410
  179.5 6.4 %collective-permute-start.23 = (bf16[32,720]{1,0:T(8,128)(2,1)S(1)}, bf16[32,720]{1,0:T(8,128)(2,1)S(1)}, u32[]{:S(2)}, u32[]{:S(2)}) collective-permute-start(bf16[32,720]{1,0:T(8,128)(2,1)S(1)} %get-tuple-element.69), channel_id=1, source_target_pairs={{0,3},{1,2},{2,1},{3,0},{4,7},{5,6},{6,5},{7,4},{8,11},{9,10},{10,... | collective-permute-start | bytes 138248 | tf_op jit(solution)/shard_map/ppermute | solution.py:410
  181.0 5.7 %collective-permute-start.22 = (bf16[32,720]{1,0:T(8,128)(2,1)S(1)}, bf16[32,720]{1,0:T(8,128)(2,1)S(1)}, u32[]{:S(2)}, u32[]{:S(2)}) collective-permute-start(bf16[32,720]{1,0:T(8,128)(2,1)S(1)} %get-tuple-element.70), channel_id=1, source_target_pairs={{0,2},{1,3},{2,0},{3,1},{4,6},{5,7},{6,4},{7,5},{8,10},{9,11},{10,... | collective-permute-start | bytes 138248 | tf_op jit(solution)/shard_map/ppermute | solution.py:410
  181.0 5.7 %collective-permute-start.21 = (bf16[32,720]{1,0:T(8,128)(2,1)S(1)}, bf16[32,720]{1,0:T(8,128)(2,1)S(1)}, u32[]{:S(2)}, u32[]{:S(2)}) collective-permute-start(bf16[32,720]{1,0:T(8,128)(2,1)S(1)} %get-tuple-element.71), channel_id=1, source_target_pairs={{0,1},{1,0},{2,3},{3,2},{4,5},{5,4},{6,7},{7,6},{8,9},{9,8},{10,11... | collective-permute-start | bytes 138248 | tf_op jit(solution)/shard_map/ppermute | solution.py:410
  185.9 0.8 copy-start.7
  186.7 0.6 copy-start.8
  186.7 0.6 copy-start.9

commit v2 on v1

--- a/solution.py
+++ b/solution.py
@@ -11,7 +11,8 @@
 swish_beta = 1.702
 META = 64
 LANES = 128
-VMEM_LIMIT = 56 * 1024 * 1024
+VMEM_LIMIT = 26 * 1024 * 1024
+HINT = pl.CostEstimate(flops=1024, bytes_accessed=1024, transcendentals=0)
 F32 = jnp.float32
 BF16 = jnp.bfloat16
 
@@ -26,15 +27,24 @@
 
 def pack_kernel(tokens_ref, gain_ref, ids_ref, scores_ref, out_ref):
     steps, rows, width = tokens_ref.shape
-    top = ids_ref.shape[2]
+    top = ids_ref.shape[1]
+    gain = gain_ref[...].reshape(1, width)
+    eye = (
+        lax.broadcasted_iota(jnp.int32, (rows, rows), 0)
+        == lax.broadcasted_iota(jnp.int32, (rows, rows), 1)
+    ).astype(F32)
+
+    def column(row):
+        return jnp.sum(eye * row, axis=1, keepdims=True)
+
     for s in range(steps):
         values = tokens_ref[s].astype(F32)
         mean = jnp.mean(values * values, axis=-1, keepdims=True)
-        normed = (values * lax.rsqrt(mean + epsilon) * gain_ref[...]).astype(BF16)
+        normed = (values * lax.rsqrt(mean + epsilon) * gain).astype(BF16)
         at = slice(s * rows, (s + 1) * rows)
         out_ref[at, :width] = normed
         scores = scores_ref[s]
-        weights = scores / jnp.sum(scores, axis=-1, keepdims=True)
+        weights = scores / jnp.sum(scores, axis=0, keepdims=True)
         high = weights.astype(BF16)
         rest = weights - high.astype(F32)
         middle = rest.astype(BF16)
@@ -44,7 +54,7 @@
         parts = (ids_ref[s].astype(F32), high.astype(F32), middle.astype(F32), low.astype(F32))
         for p, part in enumerate(parts):
             for k in range(top):
-                meta = jnp.where(lane == p * top + k, part[:, k : k + 1], meta)
+                meta = jnp.where(lane == p * top + k, column(part[k : k + 1]), meta)
         out_ref[at, width:] = meta.astype(BF16)
 
 
@@ -54,42 +64,63 @@
         pack_kernel,
         out_shape=jax.ShapeDtypeStruct((steps * rows, width + META), BF16),
         compiler_params=params(),
-    )(tokens, gain.reshape(1, width), ids, scores)
-
-
-def dequant_kernel(codes_ref, scales_ref, spread_ref, out_ref):
+    )(
+        tokens, gain, jnp.transpose(ids, (0, 2, 1)), jnp.transpose(scores, (0, 2, 1))
+    )
+
+
+def dequant_kernel(codes_ref, scales_ref, _after_ref, out_ref):
     width = codes_ref.shape[2]
+    scales = scales_ref[0]
+    blocks = scales.shape[1]
     chunk = 256
-    scales = scales_ref[0]
     for at in range(0, width, chunk):
         end = min(at + chunk, width)
-        wide = dot(scales, spread_ref[:, at:end], ((1,), (0,)))
+        column = lax.broadcasted_iota(jnp.int32, (blocks, end - at), 1) + at
+        block = lax.broadcasted_iota(jnp.int32, (blocks, end - at), 0)
+        first = block * (width // blocks)
+        inside = jnp.logical_and(column >= first, column < first + width // blocks)
+        wide = dot(scales, inside.astype(F32).astype(BF16), ((1,), (0,)))
         out_ref[0, :, at:end] = (codes_ref[0, :, at:end].astype(F32) * wide).astype(BF16)
 
 
-def dequant(codes, scales):
+def dequant(codes, scales, after):
     count, rows, width = codes.shape
     blocks = scales.shape[2]
-    spread = (
-        jnp.arange(blocks)[:, None] == jnp.arange(width)[None, :] // (width // blocks)
-    ).astype(BF16)
     return pl.pallas_call(
         dequant_kernel,
         grid=(count,),
         in_specs=[
             pl.BlockSpec((1, rows, width), lambda i: (i, 0, 0)),
             pl.BlockSpec((1, rows, blocks), lambda i: (i, 0, 0)),
-            pl.BlockSpec((blocks, width), lambda i: (0, 0)),
+            pl.BlockSpec(memory_space=pl.ANY),
         ],
         out_specs=pl.BlockSpec((1, rows, width), lambda i: (i, 0, 0)),
         out_shape=jax.ShapeDtypeStruct(codes.shape, BF16),
         compiler_params=params(),
-        cost_estimate=pl.CostEstimate(
-            flops=2 * count * rows * width * 128,
-            bytes_accessed=4 * count * rows * width,
-            transcendentals=0,
-        ),
-    )(codes, scales, spread)
+        cost_estimate=HINT,
+    )(codes, scales, after)
+
+
+def join_kernel(count, *refs):
+    out_ref = refs[count + 1]
+    rows = refs[0].shape[0]
+    for k in range(count):
+        out_ref[k * rows : (k + 1) * rows] = refs[k][...]
+
+
+def join(parts, after):
+    rows, width = parts[0].shape
+    count = len(parts)
+    return pl.pallas_call(
+        functools.partial(join_kernel, count),
+        grid=(1,),
+        in_specs=[pl.BlockSpec((rows, width), lambda i: (0, 0))] * count
+        + [pl.BlockSpec(memory_space=pl.ANY)],
+        out_specs=pl.BlockSpec((count * rows, width), lambda i: (0, 0)),
+        out_shape=jax.ShapeDtypeStruct((count * rows, width), BF16),
+        compiler_params=params(),
+    )(*parts, after)
 
 
 class Plan:
@@ -175,8 +206,7 @@
 def inner_kernel(plan, arrays, place_ref, *refs):
     tokens = refs[:arrays]
     weight_ref = refs[arrays]
-    act_ref, most_ref = refs[arrays + 1], refs[arrays + 2]
-    rows_ref, mask_ref = refs[arrays + 3], refs[arrays + 4]
+    act_ref, most_ref, rows_ref, mask_ref = refs[arrays + 2 :]
     width = weight_ref.shape[3]
 
     @pl.when(pl.program_id(0) == 0)
@@ -224,28 +254,25 @@
                 )
         most_ref[...] = jnp.broadcast_to(functools.reduce(jnp.maximum, start), most_ref.shape)
 
-    gating = upward = None
-    x = rows_ref[...]
-    for slot in range(plan.slots):
-        gate = dot(weight_ref[slot, 0], x, ((1,), (0,)))
-        up = dot(weight_ref[slot, 1], x, ((1,), (0,)))
-        if slot == 0:
-            gating, upward = gate, up
-        else:
-            mine = mask_ref[slot : slot + 1] > 0.0
-            gating = jnp.where(mine, gate, gating)
-            upward = jnp.where(mine, up, upward)
+    slots, _two, block, _width = weight_ref.shape
+    both = dot(weight_ref[...].reshape(slots * 2 * block, width), rows_ref[...], ((1,), (0,)))
+    gating, upward = both[:block], both[block : 2 * block]
+    for slot in range(1, plan.slots):
+        mine = mask_ref[slot : slot + 1] > 0.0
+        at = 2 * slot * block
+        gating = jnp.where(mine, both[at : at + block], gating)
+        upward = jnp.where(mine, both[at + block : at + 2 * block], upward)
     act_ref[...] = (gating * jax.nn.sigmoid(swish_beta * gating) * (upward + 1.0)).astype(BF16)
 
 
 def piece(total):
-    for size in (144, 120, 72, 40, 24, 16, 8):
+    for size in (240, 120, 72, 40, 24, 16, 8):
         if total % size == 0:
             return size
     return total
 
 
-def inner(plan, place, tokens, weights):
+def inner(plan, place, tokens, weights, after):
     slots, _two, units, width = weights.shape
     block = piece(units)
     arrays = len(tokens)
@@ -254,7 +281,8 @@
         grid=(units // block,),
         in_specs=[pl.BlockSpec(memory_space=pltpu.SMEM)]
         + [pl.BlockSpec(t.shape, lambda i: (0, 0)) for t in tokens]
-        + [pl.BlockSpec((slots, 2, block, width), lambda i: (0, 0, i, 0))],
+        + [pl.BlockSpec((slots, 2, block, width), lambda i: (0, 0, i, 0))]
+        + [pl.BlockSpec(memory_space=pl.ANY)],
         out_specs=[
             pl.BlockSpec((block, plan.rows), lambda i: (i, 0)),
             pl.BlockSpec((8, LANES), lambda i: (0, 0)),
@@ -268,12 +296,8 @@
             pltpu.VMEM((8, plan.rows), F32),
         ],
         compiler_params=params(),
-        cost_estimate=pl.CostEstimate(
-            flops=2 * plan.rows * slots * 2 * units * width,
-            bytes_accessed=slots * 2 * units * width * 2,
-            transcendentals=units * plan.rows,
-        ),
-    )(place, *tokens, weights)
+        cost_estimate=HINT,
+    )(place, *tokens, weights, after)
 
 
 def outer_kernel(plan, arrays, before, blocks, place_ref, *refs):
@@ -372,38 +396,42 @@
             pltpu.VMEM((columns_out, plan.rows), BF16),
         ],
         compiler_params=params(),
-        cost_estimate=pl.CostEstimate(
-            flops=2 * plan.rows * slots * columns_out * width,
-            bytes_accessed=slots * columns_out * width * 2,
-            transcendentals=0,
-        ),
+        cost_estimate=HINT,
     )(place, *tokens, *parts, *befores, weights)
 
 
-def finish_kernel(subs, place_ref, *refs):
-    parts, out_ref = refs[:subs], refs[subs]
+def finish_kernel(subs, columns, place_ref, *refs):
+    out_ref = refs[-1]
     sub = place_ref[1]
-    width = parts[0].shape[1]
+    width = refs[0].shape[1]
     steps, rows, _ = out_ref.shape
+    sums = []
+    for k in range(subs):
+        value = refs[k * columns][...].astype(F32)
+        for j in range(1, columns):
+            value = value + refs[k * columns + j][...].astype(F32)
+        sums.append(value)
     for b in range(subs):
-        value = parts[0][...]
+        value = sums[0]
         for k in range(1, subs):
-            value = jnp.where(jnp.bitwise_xor(sub, k) == b, parts[k][...], value)
+            value = jnp.where(jnp.bitwise_xor(sub, k) == b, sums[k], value)
+        value = value.astype(BF16)
         for s in range(steps):
             out_ref[s, :, b * width : (b + 1) * width] = value[s * rows : (s + 1) * rows]
 
 
 def finish(place, parts, steps):
-    rows, width = parts[0].shape
-    subs = len(parts)
+    subs, columns = len(parts), len(parts[0])
+    rows, width = parts[0][0].shape
     return pl.pallas_call(
-        functools.partial(finish_kernel, subs),
+        functools.partial(finish_kernel, subs, columns),
+        grid=(1,),
         in_specs=[pl.BlockSpec(memory_space=pltpu.SMEM)]
-        + [pl.BlockSpec(memory_space=pltpu.VMEM)] * subs,
-        out_specs=pl.BlockSpec(memory_space=pltpu.VMEM),
+        + [pl.BlockSpec((rows, width), lambda i: (0, 0))] * (subs * columns),
+        out_specs=pl.BlockSpec((steps, rows // steps, width * subs), lambda i: (0, 0, 0)),
         out_shape=jax.ShapeDtypeStruct((steps, rows // steps, width * subs), BF16),
         compiler_params=params(),
-    )(place, *parts)
+    )(place, *[p for several in parts for p in several])
 
 
 def swap(x, axis, offset, count):
@@ -441,11 +469,10 @@
     near = [packed] + [swap(packed, "sub", k, subs) for k in range(1, subs)]
     codes = jnp.transpose(inner_codes, (0, 2, 3, 1)).reshape(slots * 2, units, -1)
     scales = jnp.transpose(inner_scales, (0, 2, 3, 1)).reshape(slots * 2, units, -1)
-    inner_weights = dequant(codes, scales).reshape(slots, 2, units, -1)
-    outer_weights = dequant(
-        jnp.transpose(down_codes, (0, 2, 1)), jnp.transpose(down_scales, (0, 2, 1))
-    )
-    own = jnp.concatenate(near, axis=0)
+    inner_weights = dequant(codes, scales, packed).reshape(slots, 2, units, -1)
+    outer_codes = jnp.transpose(down_codes, (0, 2, 1))
+    outer_scales = jnp.transpose(down_scales, (0, 2, 1))
+    own = join(near, inner_weights)
     other = swap(own, "ep", 1, eps)
     held = [[own, other]]
     for j in range(1, columns):
@@ -466,20 +493,22 @@
         plan0, plan1 = plan(0, first, holds), plan(first, second, holds)
         plan2 = plan(first + second, last, holds)
         everything = held[0] + held[1]
-        act0, _ = inner(plan0, place, held[0], inner_weights)
+        act0, mark = inner(plan0, place, held[0], inner_weights, own)
+        mark = swap(mark, "ep", 1, eps)
         parts0 = gather_sub(act0, subs)
-        act1, longest = inner(plan1, place, everything, inner_weights)
+        act1, longest = inner(plan1, place, everything, inner_weights, mark)
         parts1 = gather_sub(act1, subs)
         for shift in range(1, groups):
             moved = lax.ppermute(
                 longest, "grp", [(i, (i + shift) % groups) for i in range(groups)]
             )
             longest = jnp.maximum(longest, moved)
+        outer_weights = dequant(outer_codes, outer_scales, longest)
         sums = outer(plan0, place, held[0], parts0, [], outer_weights)
         sums = outer(plan1, place, everything, parts1, sums, outer_weights)
 
         def more(kept, sent):
-            act, _ = inner(plan2, place, everything, inner_weights)
+            act, _ = inner(plan2, place, everything, inner_weights, kept)
             return tuple(
                 outer(
                     plan2, place, everything, gather_sub(act, subs), [kept, sent], outer_weights
@@ -492,20 +521,27 @@
     else:
         count = -(-capacity_rows // LANES) * LANES
         each = plan(0, count, ())
+        outer_weights = dequant(outer_codes, outer_scales, own)
         keeps, sends = [], []
         for pair in held:
-            act, _ = inner(each, place, pair, inner_weights)
+            act, _ = inner(each, place, pair, inner_weights, own)
             kept, sent = outer(each, place, pair, gather_sub(act, subs), [], outer_weights)
             keeps.append(kept)
             sends.append(sent)
         keep, send = jnp.concatenate(keeps, axis=0), jnp.concatenate(sends, axis=0)
 
     chip = add(keep, swap(send, "ep", 1, eps))
-    total = chip[0].astype(F32)
-    for j in range(1, columns):
-        total = total + swap(chip[j], "ep", 2 * j, eps).astype(F32)
-    total = total.astype(BF16).reshape(subs, group, -1)
-    arrived = [total[0]] + [swap(total[k], "sub", k, subs) for k in range(1, subs)]
+    chip = chip.reshape(columns, subs, group, -1)
+    arrived = []
+    for k in range(subs):
+        arrived.append([])
+        for j in range(columns):
+            pairs = []
+            for e in range(eps):
+                for z in range(subs):
+                    pairs.append((e * subs + z, (e ^ (2 * j)) * subs + (z ^ k)))
+            block = chip[j, k]
+            arrived[-1].append(lax.ppermute(block, ("ep", "sub"), pairs) if j + k else block)
     return finish(place, arrived, steps)
 
 

time: 190 us -> 176 us (0.926)
  Pallas kernels: 73 us -> 50.7 us
  local copies, waits for them, and re-layouts: 9.14 us -> 20.8 us
  waiting for transfers between devices: 73.9 us -> 71.2 us
  other arithmetic: 2.11 us -> 0.18 us
    pallas_call x2, Pallas kernels: 21.7 us -> 8.03 us  [dequant(): pl.pallas_call(dequant_kernel, grid=(count,), in_specs=[pl.BlockSpec((1,...]
    unnamed x15 -> x29, local copies, waits for them, and re-layouts: 5.31 us -> 18.7 us
    ppermute x0 -> x7, starting transfers between devices: none -> 11.9 us  [local(): lax.ppermute(block, ('ep', 'sub'), pairs)]
    ppermute x15 -> x12, waiting for transfers between devices: 67.3 us -> 57.4 us  [swap(): return lax.ppermute(x, axis, [(i, i ^ offset) for i in range(count)])]
    ppermute x15 -> x12, starting transfers between devices: 22.9 us -> 13 us  [swap(): return lax.ppermute(x, axis, [(i, i ^ offset) for i in range(count)])]
    ppermute x0 -> x7, waiting for transfers between devices: none -> 6.74 us  [local(): lax.ppermute(block, ('ep', 'sub'), pairs)]
    pallas_call x2, Pallas kernels: 19.9 us -> 14.7 us  [outer(): pl.pallas_call(functools.partial(outer_kernel, plan, arrays, len(befores)...]
  transfers between devices with their start and end apart: 20 -> 24, of which waited for: 9 -> 9; matrix products, arithmetic and copies ran while one was open for 3% -> 2% of each run, Pallas kernels for 22% -> 14%
where the time goes in v2:
time: 176 us; the launch traced here: 175 us
  waiting for transfers between devices  71.2 us (40%)
  Pallas kernels  50.7 us (29%)
  starting transfers between devices  31.2 us (18%)
  local copies, waits for them, and re-layouts  20.8 us (12%)
    ppermute x12, waiting for transfers between devices, swap(): return lax.ppermute(x, axis, [(i, i ^ offset) for i in range(count)])  57.4 us
    pallas_call x2, Pallas kernels, inner(): pl.pallas_call(functools.partial(inner_kernel, plan, arrays), grid=(units...  26.3 us
    unnamed x29, local copies, waits for them, and re-layouts  18.7 us
    pallas_call x2, Pallas kernels, outer(): pl.pallas_call(functools.partial(outer_kernel, plan, arrays, len(befores)...  14.7 us
    ppermute x12, starting transfers between devices, swap(): return lax.ppermute(x, axis, [(i, i ^ offset) for i in range(count)])  13 us
    ppermute x7, starting transfers between devices, local(): lax.ppermute(block, ('ep', 'sub'), pairs)  11.9 us
    pallas_call x2, Pallas kernels, dequant(): pl.pallas_call(dequant_kernel, grid=(count,), in_specs=[pl.BlockSpec((1,...  8.03 us
    ppermute x2, waiting for transfers between devices, gather_sub(): ends = lax.ppermute(two, 'sub', [(2, 3), (1, 0)])  7.1 us
  transfers between devices with their start and end apart: 24, of which 9 were waited for; matrix products, arithmetic and copies ran while one was open for 2% of the time, Pallas kernels for 14%

profile of v2, /device:TPU:0, one launch (start us, length us, event | category | flops | bytes accessed | tf_op | source)
XLA Modules:
  0.0 175.1 jit_solution(3463307050055209653)
XLA Ops:
  3.2 3.0 %collective-permute-start.4 = (bf16[32,2944]{1,0:T(8,128)(2,1)S(1)}, bf16[32,2944]{1,0:T(8,128)(2,1)S(1)}, u32[]{:S(2)}, u32[]{:S(2)}) collective-permute-start(bf16[32,2944]{1,0:T(8,128)(2,1)S(1)} %shard_map.82._after_ref.refs_0_), channel_id=1, source_target_pairs={{0,1},{1,0},{2,3},{3,2},{4,5},{5,4},{6,7},{7,6},{8,9},{9,8},{10,11... | collective-permute-start | bytes 565256 | tf_op jit(solution)/shard_map/ppermute | solution.py:438
  6.3 2.6 %collective-permute-start.5 = (bf16[32,2944]{1,0:T(8,128)(2,1)S(1)}, bf16[32,2944]{1,0:T(8,128)(2,1)S(1)}, u32[]{:S(2)}, u32[]{:S(2)}) collective-permute-start(bf16[32,2944]{1,0:T(8,128)(2,1)S(1)} %shard_map.82._after_ref.refs_0_), channel_id=1, source_target_pairs={{0,2},{1,3},{2,0},{3,1},{4,6},{5,7},{6,4},{7,5},{8,10},{9,11},{10,... | collective-permute-start | bytes 565256 | tf_op jit(solution)/shard_map/ppermute | solution.py:438
  8.9 1.5 copy.9
  10.4 5.8 %copy-done = bf16[2,2880,2,720]{1,3,2,0:T(8,128)(2,1)S(1)} copy-done((bf16[2,2880,2,720]{1,3,2,0:T(8,128)(2,1)S(1)}, bf16[2,2880,2,720]{1,3,2,0:T(8,128)(2,1)}, u32[]{:S(2)}) %copy-start) | copy-done | bytes 16588824
  16.3 5.4 %shard_map.83 = bf16[4,720,2880]{2,1,0:T(8,128)(2,1)S(1)} custom-call(bf16[4,720,2880]{2,1,0:T(8,128)(2,1)S(1)} %bitcast.30, bf16[4,720,90]{2,1,0:T(8,128)(2,1)S(1)} %bitcast.32, bf16[32,2944]{1,0:T(8,128)(2,1)S(1)} %shard_map.82._after_ref.refs_0_), custom_call_target="tpu_custom_call" | custom-call | flops 1024 | bytes 1024 | tf_op jit(solution)/shard_map/pallas_call | solution.py:90
  21.6 1.3 collective-permute-done.5.refs_2_
  23.0 4.5 %copy-done.8 = bf16[4,720,2880]{2,1,0:T(8,128)(2,1)} copy-done((bf16[4,720,2880]{2,1,0:T(8,128)(2,1)}, bf16[4,720,2880]{2,1,0:T(8,128)(2,1)S(1)}, u32[]{:S(2)}) %copy-start.8) | copy-done | bytes 16588824
  27.5 1.7 collective-permute-start.8
  29.2 16.4 %collective-permute-done.8.refs_2_ = bf16[128,2944]{1,0:T(8,128)(2,1)} collective-permute-done((bf16[128,2944]{1,0:T(8,128)(2,1)S(1)}, bf16[128,2944]{1,0:T(8,128)(2,1)}, u32[]{:S(2)}, u32[]{:S(2)}) %collective-permute-start.8) | collective-permute-done | bytes 753696 | tf_op jit(solution)/shard_map/ppermute | solution.py:438
  45.7 11.3 %shard_map.85 = (bf16[720,256]{1,0:T(8,128)(2,1)S(1)}, f32[8,128]{1,0:T(8,128)S(1)}) custom-call(s32[2]{0:T(128)S(1)} %pad_add_fusion.place_ref, bf16[128,2944]{1,0:T(8,128)(2,1)S(1)} %shard_map.84.refs_0_.refs_3_, bf16[128,2944]{1,0:T(8,128)(2,1)S(1)} %collective-permute-done.7.refs_1_, bf16[2,2,720,2880]{3,2,1,0:T(8,128)(2,1)} %bitcast.37, ...), custom_call_target="tpu_custom_call" | custom-call | flops 1024 | bytes 1024 | tf_op jit(solution)/shard_map/pallas_call | solution.py:279
  58.4 15.1 %shard_map.86 = (bf16[720,384]{1,0:T(8,128)(2,1)S(1)}, f32[8,128]{1,0:T(8,128)S(1)}) custom-call(s32[2]{0:T(128)S(1)} %pad_add_fusion.place_ref, bf16[128,2944]{1,0:T(8,128)(2,1)S(1)} %shard_map.84.refs_0_.refs_3_, bf16[128,2944]{1,0:T(8,128)(2,1)S(1)} %collective-permute-done.7.refs_1_, bf16[128,2944]{1,0:T(8,128)(2,1)} %collective-permute-done.8.refs_2_, ...), custom_call_target="tpu_custom_call" | custom-call | flops 1024 | bytes 1024 | tf_op jit(solution)/shard_map/pallas_call | solution.py:279
  73.5 1.7 collective-permute-start.13
  75.2 1.3 collective-permute-start.17
  79.2 30.5 %collective-permute-done.13.refs_6_ = bf16[720,384]{1,0:T(8,128)(2,1)S(1)} collective-permute-done((bf16[720,384]{1,0:T(8,128)(2,1)S(1)}, bf16[720,384]{1,0:T(8,128)(2,1)S(1)}, u32[]{:S(2)}, u32[]{:S(2)}) %collective-permute-start.13) | collective-permute-done | bytes 552992 | tf_op jit(solution)/shard_map/ppermute | solution.py:438
  109.6 1.3 collective-permute-start.15
  110.9 6.7 %collective-permute-done.17.refs_4_ = bf16[720,256]{1,0:T(8,128)(2,1)} collective-permute-done((bf16[720,256]{1,0:T(8,128)(2,1)S(1)}, bf16[720,256]{1,0:T(8,128)(2,1)}, u32[]{:S(2)}, u32[]{:S(2)}) %collective-permute-start.17) | collective-permute-done | bytes 368672 | tf_op jit(solution)/shard_map/ppermute | solution.py:438
  117.6 1.5 collective-permute-start.11
  119.9 1.4 collective-permute-start.18
  121.3 1.5 collective-permute-start.19
  124.0 3.4 %copy-done.1 = bf16[2,2880,720]{1,2,0:T(8,128)(2,1)S(1)} copy-done((bf16[2,2880,720]{1,2,0:T(8,128)(2,1)S(1)}, bf16[2,2880,720]{1,2,0:T(8,128)(2,1)}, u32[]{:S(2)}) %copy-start.1) | copy-done | bytes 8294424
  127.4 2.7 %shard_map.87.refs_7_.refs_11_ = bf16[2,720,2880]{2,1,0:T(8,128)(2,1)S(1)} custom-call(bf16[2,720,2880]{2,1,0:T(8,128)(2,1)S(1)} %bitcast.31, bf16[2,720,90]{2,1,0:T(8,128)(2,1)S(1)} %bitcast.33, f32[8,128]{1,0:T(8,128)S(1)} %max.3._after_ref), custom_call_target="tpu_custom_call" | custom-call | flops 1024 | bytes 1024 | tf_op jit(solution)/shard_map/pallas_call | solution.py:90
  130.1 7.1 %collective-permute-done.19.refs_6_ = bf16[720,256]{1,0:T(8,128)(2,1)} collective-permute-done((bf16[720,256]{1,0:T(8,128)(2,1)}, bf16[720,256]{1,0:T(8,128)(2,1)}, u32[]{:S(2)}, u32[]{:S(2)}) %collective-permute-start.19) | collective-permute-done | bytes 368672 | tf_op jit(solution)/shard_map/ppermute | solution.py:447
  137.2 5.7 %shard_map.88 = (bf16[1,128,720]{2,1,0:T(8,128)(2,1)S(1)}, bf16[1,128,720]{2,1,0:T(8,128)(2,1)S(1)}) custom-call(s32[2]{0:T(128)S(1)} %pad_add_fusion.place_ref, bf16[128,2944]{1,0:T(8,128)(2,1)S(1)} %copy-done.11, bf16[128,2944]{1,0:T(8,128)(2,1)S(1)} %copy-done.13, bf16[720,256]{1,0:T(8,128)(2,1)S(1)} %get-tuple-element.59.refs_2_, ...), custom_call_target="tpu_custom_call" | custom-call | flops 1024 | bytes 1024 | tf_op jit(solution)/shard_map/pallas_call | solution.py:384
  144.1 9.1 %shard_map.89 = (bf16[2,128,720]{2,1,0:T(8,128)(2,1)S(1)}, bf16[2,128,720]{2,1,0:T(8,128)(2,1)S(1)}) custom-call(s32[2]{0:T(128)S(1)} %pad_add_fusion.place_ref, bf16[128,2944]{1,0:T(8,128)(2,1)S(1)} %copy-done.11, bf16[128,2944]{1,0:T(8,128)(2,1)S(1)} %copy-done.13, bf16[128,2944]{1,0:T(8,128)(2,1)} %collective-permute-done.8.refs_2_, ...), custom_call_target="tpu_custom_call" | custom-call | flops 1024 | bytes 1024 | tf_op jit(solution)/shard_map/pallas_call | solution.py:384
  153.3 1.7 collective-permute-done.20
  155.1 1.5 collective-permute-start.21
  156.8 1.8 %collective-permute-start.23 = (bf16[32,720]{1,0:T(8,128)(2,1)S(1)}, bf16[32,720]{1,0:T(8,128)(2,1)S(1)}, u32[]{:S(2)}, u32[]{:S(2)}) collective-permute-start(bf16[32,720]{1,0:T(8,128)(2,1)S(1)} %get-tuple-element.75), channel_id=1, source_target_pairs={{0,9},{1,8},{2,11},{3,10},{4,13},{5,12},{6,15},{7,14},{8,1},{9,0},... | collective-permute-start | bytes 138248 | tf_op jit(solution)/shard_map/ppermute | solution.py:544
  158.7 3.0 %collective-permute-start.24 = (bf16[32,720]{1,0:T(8,128)(2,1)S(1)}, bf16[32,720]{1,0:T(8,128)(2,1)S(1)}, u32[]{:S(2)}, u32[]{:S(2)}) collective-permute-start(bf16[32,720]{1,0:T(8,128)(2,1)S(1)} %get-tuple-element.74), channel_id=1, source_target_pairs={{0,2},{1,3},{2,0},{3,1},{4,6},{5,7},{6,4},{7,5},{8,10},{9,11},{10,... | collective-permute-start | bytes 138248 | tf_op jit(solution)/shard_map/ppermute | solution.py:544
  162.6 4.4 %collective-permute-start.26 = (bf16[32,720]{1,0:T(8,128)(2,1)S(1)}, bf16[32,720]{1,0:T(8,128)(2,1)S(1)}, u32[]{:S(2)}, u32[]{:S(2)}) collective-permute-start(bf16[32,720]{1,0:T(8,128)(2,1)S(1)} %get-tuple-element.72), channel_id=1, source_target_pairs={{0,3},{1,2},{2,1},{3,0},{4,7},{5,6},{6,5},{7,4},{8,11},{9,10},{10,... | collective-permute-start | bytes 138248 | tf_op jit(solution)/shard_map/ppermute | solution.py:544
  167.0 2.9 %collective-permute-done.25.refs_5_ = bf16[32,720]{1,0:T(8,128)(2,1)S(1)} collective-permute-done((bf16[32,720]{1,0:T(8,128)(2,1)S(1)}, bf16[32,720]{1,0:T(8,128)(2,1)S(1)}, u32[]{:S(2)}, u32[]{:S(2)}) %collective-permute-start.25) | collective-permute-done | bytes 46112 | tf_op jit(solution)/shard_map/ppermute | solution.py:544
  169.9 3.8 %collective-permute-done.27.refs_7_ = bf16[32,720]{1,0:T(8,128)(2,1)S(1)} collective-permute-done((bf16[32,720]{1,0:T(8,128)(2,1)S(1)}, bf16[32,720]{1,0:T(8,128)(2,1)S(1)}, u32[]{:S(2)}, u32[]{:S(2)}) %collective-permute-start.27) | collective-permute-done | bytes 46112 | tf_op jit(solution)/shard_map/ppermute | solution.py:544
  173.7 1.4 shard_map.90
  (61 shorter events, 11.4 us)
Async XLA Ops:
  3.2 18.4 %collective-permute-start.4 = (bf16[32,2944]{1,0:T(8,128)(2,1)S(1)}, bf16[32,2944]{1,0:T(8,128)(2,1)S(1)}, u32[]{:S(2)}, u32[]{:S(2)}) collective-permute-start(bf16[32,2944]{1,0:T(8,128)(2,1)S(1)} %shard_map.82._after_ref.refs_0_), channel_id=1, source_target_pairs={{0,1},{1,0},{2,3},{3,2},{4,5},{5,4},{6,7},{7,6},{8,9},{9,8},{10,11... | collective-permute-start | bytes 565256 | tf_op jit(solution)/shard_map/ppermute | solution.py:438
  6.3 16.6 %collective-permute-start.5 = (bf16[32,2944]{1,0:T(8,128)(2,1)S(1)}, bf16[32,2944]{1,0:T(8,128)(2,1)S(1)}, u32[]{:S(2)}, u32[]{:S(2)}) collective-permute-start(bf16[32,2944]{1,0:T(8,128)(2,1)S(1)} %shard_map.82._after_ref.refs_0_), channel_id=1, source_target_pairs={{0,2},{1,3},{2,0},{3,1},{4,6},{5,7},{6,4},{7,5},{8,10},{9,11},{10,... | collective-permute-start | bytes 565256 | tf_op jit(solution)/shard_map/ppermute | solution.py:438
  8.9 14.0 %collective-permute-start.6 = (bf16[32,2944]{1,0:T(8,128)(2,1)S(1)}, bf16[32,2944]{1,0:T(8,128)(2,1)S(1)}, u32[]{:S(2)}, u32[]{:S(2)}) collective-permute-start(bf16[32,2944]{1,0:T(8,128)(2,1)S(1)} %shard_map.82._after_ref.refs_0_), channel_id=1, source_target_pairs={{0,3},{1,2},{2,1},{3,0},{4,7},{5,6},{6,5},{7,4},{8,11},{9,10},{10,... | collective-permute-start | bytes 565256 | tf_op jit(solution)/shard_map/ppermute | solution.py:438
  10.4 5.8 %copy-start = (bf16[2,2880,2,720]{1,3,2,0:T(8,128)(2,1)S(1)}, bf16[2,2880,2,720]{1,3,2,0:T(8,128)(2,1)}, u32[]{:S(2)}) copy-start(bf16[2,2880,2,720]{1,3,2,0:T(8,128)(2,1)} %param.14) | copy-start | bytes 49766404
  21.6 5.9 %copy-start.8 = (bf16[4,720,2880]{2,1,0:T(8,128)(2,1)}, bf16[4,720,2880]{2,1,0:T(8,128)(2,1)S(1)}, u32[]{:S(2)}) copy-start(bf16[4,720,2880]{2,1,0:T(8,128)(2,1)S(1)} %shard_map.83) | copy-start | bytes 49766404
  27.5 46.0 %copy-start.10 = (bf16[128,2944]{1,0:T(8,128)(2,1)}, bf16[128,2944]{1,0:T(8,128)(2,1)S(1)}, u32[]{:S(2)}) copy-start(bf16[128,2944]{1,0:T(8,128)(2,1)S(1)} %shard_map.84.refs_0_.refs_3_) | copy-start | bytes 2260996
  27.5 18.1 %collective-permute-start.8 = (bf16[128,2944]{1,0:T(8,128)(2,1)S(1)}, bf16[128,2944]{1,0:T(8,128)(2,1)}, u32[]{:S(2)}, u32[]{:S(2)}) collective-permute-start(bf16[128,2944]{1,0:T(8,128)(2,1)S(1)} %shard_map.84.refs_0_.refs_3_), channel_id=1, source_target_pairs={{0,8},{4,12},{8,0},{12,4},{1,9},{5,13},{9,1},{13,5},{2,10},{6,14},... | collective-permute-start | bytes 2261000 | tf_op jit(solution)/shard_map/ppermute | solution.py:438
  29.2 16.5 %collective-permute-start.7 = (bf16[128,2944]{1,0:T(8,128)(2,1)S(1)}, bf16[128,2944]{1,0:T(8,128)(2,1)S(1)}, u32[]{:S(2)}, u32[]{:S(2)}) collective-permute-start(bf16[128,2944]{1,0:T(8,128)(2,1)S(1)} %shard_map.84.refs_0_.refs_3_), channel_id=1, source_target_pairs={{0,4},{4,0},{8,12},{12,8},{1,5},{5,1},{9,13},{13,9},{2,6},{6,2},{1... | collective-permute-start | bytes 2261000 | tf_op jit(solution)/shard_map/ppermute | solution.py:438
  45.6 12.8 %collective-permute-start.9 = (bf16[128,2944]{1,0:T(8,128)(2,1)}, bf16[128,2944]{1,0:T(8,128)(2,1)}, u32[]{:S(2)}, u32[]{:S(2)}) collective-permute-start(bf16[128,2944]{1,0:T(8,128)(2,1)} %collective-permute-done.8.refs_2_), channel_id=1, source_target_pairs={{0,4},{4,0},{8,12},{12,8},{1,5},{5,1},{9,13},{13,9},{2,6},{6,2},{1... | collective-permute-start | bytes 2261000 | tf_op jit(solution)/shard_map/ppermute | solution.py:438
  45.6 12.8 %copy-start.9 = (bf16[4,720,2880]{2,1,0:T(8,128)(2,1)S(1)}, bf16[4,720,2880]{2,1,0:T(8,128)(2,1)}, u32[]{:S(2)}) copy-start(bf16[4,720,2880]{2,1,0:T(8,128)(2,1)} %copy-done.8) | copy-start | bytes 49766404
  45.7 27.8 %copy-start.12 = (bf16[128,2944]{1,0:T(8,128)(2,1)}, bf16[128,2944]{1,0:T(8,128)(2,1)S(1)}, u32[]{:S(2)}) copy-start(bf16[128,2944]{1,0:T(8,128)(2,1)S(1)} %collective-permute-done.7.refs_1_) | copy-start | bytes 2260996
  57.0 1.4 collective-permute-start.10
  73.5 36.2 %collective-permute-start.13 = (bf16[720,384]{1,0:T(8,128)(2,1)S(1)}, bf16[720,384]{1,0:T(8,128)(2,1)S(1)}, u32[]{:S(2)}, u32[]{:S(2)}) collective-permute-start(bf16[720,384]{1,0:T(8,128)(2,1)S(1)} %get-tuple-element.58.refs_4_), channel_id=1, source_target_pairs={{0,2},{1,3},{2,0},{3,1},{4,6},{5,7},{6,4},{7,5},{8,10},{9,11},{10,... | collective-permute-start | bytes 1658888 | tf_op jit(solution)/shard_map/ppermute | solution.py:438
  75.2 42.4 %collective-permute-start.17 = (bf16[720,256]{1,0:T(8,128)(2,1)S(1)}, bf16[720,256]{1,0:T(8,128)(2,1)}, u32[]{:S(2)}, u32[]{:S(2)}) collective-permute-start(bf16[720,256]{1,0:T(8,128)(2,1)S(1)} %get-tuple-element.59.refs_2_), channel_id=1, source_target_pairs={{0,2},{1,3},{2,0},{3,1},{4,6},{5,7},{6,4},{7,5},{8,10},{9,11},{10,... | collective-permute-start | bytes 1105928 | tf_op jit(solution)/shard_map/ppermute | solution.py:438
  76.5 42.6 %collective-permute-start.16 = (bf16[720,256]{1,0:T(8,128)(2,1)S(1)}, bf16[720,256]{1,0:T(8,128)(2,1)S(1)}, u32[]{:S(2)}, u32[]{:S(2)}) collective-permute-start(bf16[720,256]{1,0:T(8,128)(2,1)S(1)} %get-tuple-element.59.refs_2_), channel_id=1, source_target_pairs={{0,1},{1,0},{2,3},{3,2},{4,5},{5,4},{6,7},{7,6},{8,9},{9,8},{10,11... | collective-permute-start | bytes 1105928 | tf_op jit(solution)/shard_map/ppermute | solution.py:438
  77.7 66.3 %collective-permute-start.12 = (bf16[720,384]{1,0:T(8,128)(2,1)S(1)}, bf16[720,384]{1,0:T(8,128)(2,1)S(1)}, u32[]{:S(2)}, u32[]{:S(2)}) collective-permute-start(bf16[720,384]{1,0:T(8,128)(2,1)S(1)} %get-tuple-element.58.refs_4_), channel_id=1, source_target_pairs={{0,1},{1,0},{2,3},{3,2},{4,5},{5,4},{6,7},{7,6},{8,9},{9,8},{10,11... | collective-permute-start | bytes 1658888 | tf_op jit(solution)/shard_map/ppermute | solution.py:438
  78.5 65.6 %collective-permute-start.14 = (bf16[720,384]{1,0:T(8,128)(2,1)S(1)}, bf16[720,384]{1,0:T(8,128)(2,1)S(1)}, u32[]{:S(2)}, u32[]{:S(2)}) collective-permute-start(bf16[720,384]{1,0:T(8,128)(2,1)S(1)} %get-tuple-element.58.refs_4_), channel_id=1, source_target_pairs={{1,2},{2,1},{5,6},{6,5},{9,10},{10,9},{13,14},{14,13},{17,18},{18,... | collective-permute-start | bytes 1658888 | tf_op jit(solution)/shard_map/ppermute | solution.py:446
  109.6 34.4 %collective-permute-start.15 = (bf16[720,384]{1,0:T(8,128)(2,1)S(1)}, bf16[720,384]{1,0:T(8,128)(2,1)S(1)}, u32[]{:S(2)}, u32[]{:S(2)}) collective-permute-start(bf16[720,384]{1,0:T(8,128)(2,1)S(1)} %collective-permute-done.13.refs_6_), channel_id=1, source_target_pairs={{2,3},{1,0},{6,7},{5,4},{10,11},{9,8},{14,15},{13,12},{18,19},{17,... | collective-permute-start | bytes 1658888 | tf_op jit(solution)/shard_map/ppermute | solution.py:447
  117.6 3.7 %collective-permute-start.11 = (f32[8,128]{1,0:T(8,128)S(1)}, f32[8,128]{1,0:T(8,128)S(1)}, u32[]{:S(2)}, u32[]{:S(2)}) collective-permute-start(f32[8,128]{1,0:T(8,128)S(1)} %get-tuple-element.57), channel_id=1, source_target_pairs={{0,16},{16,0},{1,17},{17,1},{2,18},{18,2},{3,19},{19,3},{4,20},{20... | collective-permute-start | bytes 12296 | tf_op jit(solution)/shard_map/ppermute | solution.py:502
  119.9 10.2 %collective-permute-start.18 = (bf16[720,256]{1,0:T(8,128)(2,1)S(1)}, bf16[720,256]{1,0:T(8,128)(2,1)}, u32[]{:S(2)}, u32[]{:S(2)}) collective-permute-start(bf16[720,256]{1,0:T(8,128)(2,1)S(1)} %get-tuple-element.59.refs_2_), channel_id=1, source_target_pairs={{1,2},{2,1},{5,6},{6,5},{9,10},{10,9},{13,14},{14,13},{17,18},{18,... | collective-permute-start | bytes 1105928 | tf_op jit(solution)/shard_map/ppermute | solution.py:446
  121.3 15.9 %collective-permute-start.19 = (bf16[720,256]{1,0:T(8,128)(2,1)}, bf16[720,256]{1,0:T(8,128)(2,1)}, u32[]{:S(2)}, u32[]{:S(2)}) collective-permute-start(bf16[720,256]{1,0:T(8,128)(2,1)} %collective-permute-done.17.refs_4_), channel_id=1, source_target_pairs={{2,3},{1,0},{6,7},{5,4},{10,11},{9,8},{14,15},{13,12},{18,19},{17,... | collective-permute-start | bytes 1105928 | tf_op jit(solution)/shard_map/ppermute | solution.py:447
  127.4 9.8 %copy-start.3 = (bf16[720,256]{1,0:T(8,128)(2,1)S(1)}, bf16[720,256]{1,0:T(8,128)(2,1)}, u32[]{:S(2)}) copy-start(bf16[720,256]{1,0:T(8,128)(2,1)} %copy-done.2) | copy-start | bytes 1105924
  127.4 9.8 %copy-start.11 = (bf16[128,2944]{1,0:T(8,128)(2,1)S(1)}, bf16[128,2944]{1,0:T(8,128)(2,1)}, u32[]{:S(2)}) copy-start(bf16[128,2944]{1,0:T(8,128)(2,1)} %copy-done.10) | copy-start | bytes 2260996
  127.4 9.8 %copy-start.13 = (bf16[128,2944]{1,0:T(8,128)(2,1)S(1)}, bf16[128,2944]{1,0:T(8,128)(2,1)}, u32[]{:S(2)}) copy-start(bf16[128,2944]{1,0:T(8,128)(2,1)} %copy-done.12) | copy-start | bytes 2260996
  153.2 1.8 %collective-permute-start.20 = (bf16[2,128,720]{2,1,0:T(8,128)(2,1)S(1)}, bf16[2,128,720]{2,1,0:T(8,128)(2,1)S(1)}, u32[]{:S(2)}, u32[]{:S(2)}) collective-permute-start(bf16[2,128,720]{2,1,0:T(8,128)(2,1)S(1)} %get-tuple-element.69), channel_id=1, source_target_pairs={{0,4},{4,0},{8,12},{12,8},{1,5},{5,1},{9,13},{13,9},{2,6},{6,2},{1... | collective-permute-start | bytes 1105928 | tf_op jit(solution)/shard_map/ppermute | solution.py:438
  155.1 7.5 %collective-permute-start.21 = (bf16[32,720]{1,0:T(8,128)(2,1)S(1)}, bf16[32,720]{1,0:T(8,128)(2,1)S(1)}, u32[]{:S(2)}, u32[]{:S(2)}) collective-permute-start(bf16[32,720]{1,0:T(8,128)(2,1)S(1)} %get-tuple-element.77), channel_id=1, source_target_pairs={{0,8},{1,9},{2,10},{3,11},{4,12},{5,13},{6,14},{7,15},{8,0},{9,1},... | collective-permute-start | bytes 138248 | tf_op jit(solution)/shard_map/ppermute | solution.py:544
  156.7 10.3 %collective-permute-start.22 = (bf16[32,720]{1,0:T(8,128)(2,1)S(1)}, bf16[32,720]{1,0:T(8,128)(2,1)S(1)}, u32[]{:S(2)}, u32[]{:S(2)}) collective-permute-start(bf16[32,720]{1,0:T(8,128)(2,1)S(1)} %get-tuple-element.76), channel_id=1, source_target_pairs={{0,1},{1,0},{2,3},{3,2},{4,5},{5,4},{6,7},{7,6},{8,9},{9,8},{10,11... | collective-permute-start | bytes 138248 | tf_op jit(solution)/shard_map/ppermute | solution.py:544
  156.8 10.2 %collective-permute-start.23 = (bf16[32,720]{1,0:T(8,128)(2,1)S(1)}, bf16[32,720]{1,0:T(8,128)(2,1)S(1)}, u32[]{:S(2)}, u32[]{:S(2)}) collective-permute-start(bf16[32,720]{1,0:T(8,128)(2,1)S(1)} %get-tuple-element.75), channel_id=1, source_target_pairs={{0,9},{1,8},{2,11},{3,10},{4,13},{5,12},{6,15},{7,14},{8,1},{9,0},... | collective-permute-start | bytes 138248 | tf_op jit(solution)/shard_map/ppermute | solution.py:544
  158.7 8.3 %collective-permute-start.24 = (bf16[32,720]{1,0:T(8,128)(2,1)S(1)}, bf16[32,720]{1,0:T(8,128)(2,1)S(1)}, u32[]{:S(2)}, u32[]{:S(2)}) collective-permute-start(bf16[32,720]{1,0:T(8,128)(2,1)S(1)} %get-tuple-element.74), channel_id=1, source_target_pairs={{0,2},{1,3},{2,0},{3,1},{4,6},{5,7},{6,4},{7,5},{8,10},{9,11},{10,... | collective-permute-start | bytes 138248 | tf_op jit(solution)/shard_map/ppermute | solution.py:544
  161.7 8.3 %collective-permute-start.25 = (bf16[32,720]{1,0:T(8,128)(2,1)S(1)}, bf16[32,720]{1,0:T(8,128)(2,1)S(1)}, u32[]{:S(2)}, u32[]{:S(2)}) collective-permute-start(bf16[32,720]{1,0:T(8,128)(2,1)S(1)} %get-tuple-element.73), channel_id=1, source_target_pairs={{0,10},{1,11},{2,8},{3,9},{4,14},{5,15},{6,12},{7,13},{8,2},{9,3},... | collective-permute-start | bytes 138248 | tf_op jit(solution)/shard_map/ppermute | solution.py:544
  162.6 7.4 %collective-permute-start.26 = (bf16[32,720]{1,0:T(8,128)(2,1)S(1)}, bf16[32,720]{1,0:T(8,128)(2,1)S(1)}, u32[]{:S(2)}, u32[]{:S(2)}) collective-permute-start(bf16[32,720]{1,0:T(8,128)(2,1)S(1)} %get-tuple-element.72), channel_id=1, source_target_pairs={{0,3},{1,2},{2,1},{3,0},{4,7},{5,6},{6,5},{7,4},{8,11},{9,10},{10,... | collective-permute-start | bytes 138248 | tf_op jit(solution)/shard_map/ppermute | solution.py:544
  166.9 6.8 %collective-permute-start.27 = (bf16[32,720]{1,0:T(8,128)(2,1)S(1)}, bf16[32,720]{1,0:T(8,128)(2,1)S(1)}, u32[]{:S(2)}, u32[]{:S(2)}) collective-permute-start(bf16[32,720]{1,0:T(8,128)(2,1)S(1)} %get-tuple-element.71), channel_id=1, source_target_pairs={{0,11},{1,10},{2,9},{3,8},{4,15},{5,14},{6,13},{7,12},{8,3},{9,2},... | collective-permute-start | bytes 138248 | tf_op jit(solution)/shard_map/ppermute | solution.py:544
  (6 other events, 7.2 us)

commit v3 on v2

--- a/solution.py
+++ b/solution.py
@@ -206,7 +206,7 @@
 def inner_kernel(plan, arrays, place_ref, *refs):
     tokens = refs[:arrays]
     weight_ref = refs[arrays]
-    act_ref, most_ref, rows_ref, mask_ref = refs[arrays + 2 :]
+    act_ref, most_ref, rows_ref, mask_ref = refs[-4:]
     width = weight_ref.shape[3]
 
     @pl.when(pl.program_id(0) == 0)
@@ -282,7 +282,7 @@
         in_specs=[pl.BlockSpec(memory_space=pltpu.SMEM)]
         + [pl.BlockSpec(t.shape, lambda i: (0, 0)) for t in tokens]
         + [pl.BlockSpec((slots, 2, block, width), lambda i: (0, 0, i, 0))]
-        + [pl.BlockSpec(memory_space=pl.ANY)],
+        + [pl.BlockSpec(memory_space=pl.ANY)] * len(after),
         out_specs=[
             pl.BlockSpec((block, plan.rows), lambda i: (i, 0)),
             pl.BlockSpec((8, LANES), lambda i: (0, 0)),
@@ -297,7 +297,7 @@
         ],
         compiler_params=params(),
         cost_estimate=HINT,
-    )(place, *tokens, weights, after)
+    )(place, *tokens, weights, *after)
 
 
 def outer_kernel(plan, arrays, before, blocks, place_ref, *refs):
@@ -438,14 +438,24 @@
     return lax.ppermute(x, axis, [(i, i ^ offset) for i in range(count)])
 
 
-def gather_sub(x, subs):
+def gather_direct(x, subs):
     if subs != 4:
         return [x] + [swap(x, "sub", k, subs) for k in range(1, subs)]
+    one = swap(x, "sub", 1, subs)
     two = swap(x, "sub", 2, subs)
-    one = swap(x, "sub", 1, subs)
     middle = lax.ppermute(x, "sub", [(1, 2), (2, 1)])
-    ends = lax.ppermute(two, "sub", [(2, 3), (1, 0)])
-    return [x, one, two, middle, ends]
+    return [x, one, two, middle]
+
+
+def gather_ends(parts):
+    if len(parts) != 4:
+        return parts
+    return parts + [lax.ppermute(parts[2], "sub", [(2, 3), (1, 0)])]
+
+
+def gather_sub(x, subs):
+    parts = gather_direct(x, subs)
+    return gather_ends(parts) if subs == 4 else parts
 
 
 def add(a, b):
@@ -474,17 +484,14 @@
     outer_scales = jnp.transpose(down_scales, (0, 2, 1))
     own = join(near, inner_weights)
     other = swap(own, "ep", 1, eps)
-    held = [[own, other]]
-    for j in range(1, columns):
-        arrived = swap(own, "ep", 2 * j, eps)
-        held.append([arrived, swap(arrived, "ep", 1, eps)])
+    across = [swap(own, "ep", 2 * j, eps) for j in range(1, columns)]
 
     capacity_rows = group * subs * 2 // rows * slots * capacity
 
     def plan(first, count, holds):
         return Plan(first, count, holds, slots, subs, group, top, eps)
 
-    if columns == 2 and capacity_rows % 384 == 0:
+    if columns == 2 and subs == 4 and capacity_rows % 384 == 0:
         most = 2 * capacity_rows
         first = capacity_rows // 384 * 256
         second = capacity_rows
@@ -492,23 +499,28 @@
         holds = (first,)
         plan0, plan1 = plan(0, first, holds), plan(first, second, holds)
         plan2 = plan(first + second, last, holds)
-        everything = held[0] + held[1]
-        act0, mark = inner(plan0, place, held[0], inner_weights, own)
-        mark = swap(mark, "ep", 1, eps)
-        parts0 = gather_sub(act0, subs)
-        act1, longest = inner(plan1, place, everything, inner_weights, mark)
-        parts1 = gather_sub(act1, subs)
+        act0, mark = inner(plan0, place, [own, other], inner_weights, [own])
+        parts0 = gather_direct(act0, subs)
+        outer_weights = dequant(outer_codes, outer_scales, mark)
+        moved = join(across, mark)
+        everything = [own, other, moved, swap(moved, "ep", 1, eps)]
+        act1, longest = inner(
+            plan1, place, everything, inner_weights, [parts0[1], parts0[3], outer_weights]
+        )
+        parts0 = gather_ends(parts0)
+        sums = outer(plan0, place, [own, other], parts0, [], outer_weights)
+        parts1 = gather_direct(act1, subs)
+        passed = [parts1[0], parts1[1], join(parts1[2:3], sums[0]), parts1[3]]
+        parts1 = parts1 + gather_ends(passed)[4:]
         for shift in range(1, groups):
             moved = lax.ppermute(
                 longest, "grp", [(i, (i + shift) % groups) for i in range(groups)]
             )
             longest = jnp.maximum(longest, moved)
-        outer_weights = dequant(outer_codes, outer_scales, longest)
-        sums = outer(plan0, place, held[0], parts0, [], outer_weights)
         sums = outer(plan1, place, everything, parts1, sums, outer_weights)
 
         def more(kept, sent):
-            act, _ = inner(plan2, place, everything, inner_weights, kept)
+            act, _ = inner(plan2, place, everything, inner_weights, [kept])
             return tuple(
                 outer(
                     plan2, place, everything, gather_sub(act, subs), [kept, sent], outer_weights
@@ -523,8 +535,9 @@
         each = plan(0, count, ())
         outer_weights = dequant(outer_codes, outer_scales, own)
         keeps, sends = [], []
+        held = [[own, other]] + [[a, swap(a, "ep", 1, eps)] for a in across]
         for pair in held:
-            act, _ = inner(each, place, pair, inner_weights, own)
+            act, _ = inner(each, place, pair, inner_weights, [own])
             kept, sent = outer(each, place, pair, gather_sub(act, subs), [], outer_weights)
             keeps.append(kept)
             sends.append(sent)

time: 176 us -> 156 us (0.89)
  waiting for transfers between devices: 71.2 us -> 51.8 us
  local copies, waits for them, and re-layouts: 20.8 us -> 18.7 us
  starting transfers between devices: 31.2 us -> 33.1 us
    ppermute x12 -> x11, waiting for transfers between devices: 57.4 us -> 25 us  [swap(): return lax.ppermute(x, axis, [(i, i ^ offset) for i in range(count)])]
    ppermute x4, waiting for transfers between devices: 7.11 us -> 21.1 us  [the longest x2 21.1 us: gather_ends(): return parts + [lax.ppermute(parts[2], 'sub', [(2, 3), (1, 0)])]]
    ppermute x12 -> x11, starting transfers between devices: 13 us -> 16.2 us  [swap(): return lax.ppermute(x, axis, [(i, i ^ offset) for i in range(count)])]
    ppermute x7, waiting for transfers between devices: 6.74 us -> 3.57 us  [local(): lax.ppermute(block, ('ep', 'sub'), pairs)]
    unnamed x29 -> x15, local copies, waits for them, and re-layouts: 18.7 us -> 16.6 us
    ppermute x1, waiting for transfers between devices: 0.01 us -> 2.08 us  [local(): lax.ppermute(longest, 'grp', [(i, (i + shift) % groups) for i in range(gr...]
  transfers between devices with their start and end apart: 24 -> 23, of which waited for: 9 -> 15; matrix products, arithmetic and copies ran while one was open for 2% -> 2% of each run, Pallas kernels for 14% -> 25%
where the time goes in v3:
time: 156 us; the launch traced here: 155 us
  waiting for transfers between devices  51.8 us (33%)
  Pallas kernels  50.7 us (32%)
  starting transfers between devices  33.1 us (21%)
  local copies, waits for them, and re-layouts  18.7 us (12%)
    pallas_call x2, Pallas kernels, inner(): pl.pallas_call(functools.partial(inner_kernel, plan, arrays), grid=(units...  26.1 us
    ppermute x11, waiting for transfers between devices, swap(): return lax.ppermute(x, axis, [(i, i ^ offset) for i in range(count)])  25 us
    ppermute x2, waiting for transfers between devices, gather_ends(): return parts + [lax.ppermute(parts[2], 'sub', [(2, 3), (1, 0)])]  21.1 us
    unnamed x15, local copies, waits for them, and re-layouts  16.6 us
    ppermute x11, starting transfers between devices, swap(): return lax.ppermute(x, axis, [(i, i ^ offset) for i in range(count)])  16.2 us
    pallas_call x2, Pallas kernels, outer(): pl.pallas_call(functools.partial(outer_kernel, plan, arrays, len(befores)...  14 us
    ppermute x7, starting transfers between devices, local(): lax.ppermute(block, ('ep', 'sub'), pairs)  11.2 us
    pallas_call x2, Pallas kernels, dequant(): pl.pallas_call(dequant_kernel, grid=(count,), in_specs=[pl.BlockSpec((1,...  8.03 us
  transfers between devices with their start and end apart: 23, of which 15 were waited for; matrix products, arithmetic and copies ran while one was open for 2% of the time, Pallas kernels for 25%

profile of v3, /device:TPU:0, one launch (start us, length us, event | category | flops | bytes accessed | tf_op | source)
XLA Modules:
  0.0 155.4 jit_solution(15259929628582585113)
XLA Ops:
  3.2 5.1 %collective-permute-start.6 = (bf16[32,2944]{1,0:T(8,128)(2,1)S(1)}, bf16[32,2944]{1,0:T(8,128)(2,1)S(1)}, u32[]{:S(2)}, u32[]{:S(2)}) collective-permute-start(bf16[32,2944]{1,0:T(8,128)(2,1)S(1)} %shard_map.82._after_ref.refs_0_), channel_id=1, source_target_pairs={{0,3},{1,2},{2,1},{3,0},{4,7},{5,6},{6,5},{7,4},{8,11},{9,10},{10,... | collective-permute-start | bytes 565256 | tf_op jit(solution)/shard_map/ppermute | solution.py:438
  9.0 1.6 copy.9
  10.5 5.8 %copy-done = bf16[2,2880,2,720]{1,3,2,0:T(8,128)(2,1)S(1)} copy-done((bf16[2,2880,2,720]{1,3,2,0:T(8,128)(2,1)S(1)}, bf16[2,2880,2,720]{1,3,2,0:T(8,128)(2,1)}, u32[]{:S(2)}) %copy-start) | copy-done | bytes 16588824
  16.3 5.4 %shard_map.83 = bf16[4,720,2880]{2,1,0:T(8,128)(2,1)S(1)} custom-call(bf16[4,720,2880]{2,1,0:T(8,128)(2,1)S(1)} %bitcast.30, bf16[4,720,90]{2,1,0:T(8,128)(2,1)S(1)} %bitcast.32, bf16[32,2944]{1,0:T(8,128)(2,1)S(1)} %shard_map.82._after_ref.refs_0_), custom_call_target="tpu_custom_call" | custom-call | flops 1024 | bytes 1024 | tf_op jit(solution)/shard_map/pallas_call | solution.py:90
  21.7 2.6 %collective-permute-done.5.refs_2_ = bf16[32,2944]{1,0:T(8,128)(2,1)S(1)} collective-permute-done((bf16[32,2944]{1,0:T(8,128)(2,1)S(1)}, bf16[32,2944]{1,0:T(8,128)(2,1)S(1)}, u32[]{:S(2)}, u32[]{:S(2)}) %collective-permute-start.5) | collective-permute-done | bytes 188448 | tf_op jit(solution)/shard_map/ppermute | solution.py:438
  24.4 3.2 %copy-done.6 = bf16[4,720,2880]{2,1,0:T(8,128)(2,1)} copy-done((bf16[4,720,2880]{2,1,0:T(8,128)(2,1)}, bf16[4,720,2880]{2,1,0:T(8,128)(2,1)S(1)}, u32[]{:S(2)}) %copy-start.6) | copy-done | bytes 16588824
  27.5 1.6 %collective-permute-start.8 = (bf16[128,2944]{1,0:T(8,128)(2,1)S(1)}, bf16[128,2944]{1,0:T(8,128)(2,1)S(1)}, u32[]{:S(2)}, u32[]{:S(2)}) collective-permute-start(bf16[128,2944]{1,0:T(8,128)(2,1)S(1)} %shard_map.84.refs_0_.refs_3_), channel_id=1, source_target_pairs={{0,8},{4,12},{8,0},{12,4},{1,9},{5,13},{9,1},{13,5},{2,10},{6,14},... | collective-permute-start | bytes 2261000 | tf_op jit(solution)/shard_map/ppermute | solution.py:438
  29.8 10.2 %shard_map.85 = (bf16[720,256]{1,0:T(8,128)(2,1)S(1)}, f32[8,128]{1,0:T(8,128)S(1)}) custom-call(s32[2]{0:T(128)S(1)} %pad_add_fusion.place_ref, bf16[128,2944]{1,0:T(8,128)(2,1)S(1)} %shard_map.84.refs_0_.refs_3_, bf16[128,2944]{1,0:T(8,128)(2,1)S(1)} %collective-permute-done.7.refs_1_, bf16[2,2,720,2880]{3,2,1,0:T(8,128)(2,1)} %bitcast.37, ...), custom_call_target="tpu_custom_call" | custom-call | flops 1024 | bytes 1024 | tf_op jit(solution)/shard_map/pallas_call | solution.py:279
  40.0 6.8 %collective-permute-done.8.refs_0_ = bf16[128,2944]{1,0:T(8,128)(2,1)S(1)} collective-permute-done((bf16[128,2944]{1,0:T(8,128)(2,1)S(1)}, bf16[128,2944]{1,0:T(8,128)(2,1)S(1)}, u32[]{:S(2)}, u32[]{:S(2)}) %collective-permute-start.8) | collective-permute-done | bytes 753696 | tf_op jit(solution)/shard_map/ppermute | solution.py:438
  48.4 4.1 %collective-permute-start.10 = (bf16[720,256]{1,0:T(8,128)(2,1)S(1)}, bf16[720,256]{1,0:T(8,128)(2,1)S(1)}, u32[]{:S(2)}, u32[]{:S(2)}) collective-permute-start(bf16[720,256]{1,0:T(8,128)(2,1)S(1)} %get-tuple-element.57.refs_2_), channel_id=1, source_target_pairs={{0,1},{1,0},{2,3},{3,2},{4,5},{5,4},{6,7},{7,6},{8,9},{9,8},{10,11... | collective-permute-start | bytes 1105928 | tf_op jit(solution)/shard_map/ppermute | solution.py:438
  54.0 3.4 %copy-done.1 = bf16[2,2880,720]{1,2,0:T(8,128)(2,1)S(1)} copy-done((bf16[2,2880,720]{1,2,0:T(8,128)(2,1)S(1)}, bf16[2,2880,720]{1,2,0:T(8,128)(2,1)}, u32[]{:S(2)}) %copy-start.1) | copy-done | bytes 8294424
  57.5 2.7 %shard_map.87.refs_7_.refs_11_ = bf16[2,720,2880]{2,1,0:T(8,128)(2,1)S(1)} custom-call(bf16[2,720,2880]{2,1,0:T(8,128)(2,1)S(1)} %bitcast.31, bf16[2,720,90]{2,1,0:T(8,128)(2,1)S(1)} %bitcast.33, f32[8,128]{1,0:T(8,128)S(1)} %get-tuple-element.56.refs_1_._after_ref), custom_call_target="tpu_custom_call" | custom-call | flops 1024 | bytes 1024 | tf_op jit(solution)/shard_map/pallas_call | solution.py:90
  60.1 1.8 %collective-permute-done.10.refs_5_.refs_3_ = bf16[720,256]{1,0:T(8,128)(2,1)S(1)} collective-permute-done((bf16[720,256]{1,0:T(8,128)(2,1)S(1)}, bf16[720,256]{1,0:T(8,128)(2,1)S(1)}, u32[]{:S(2)}, u32[]{:S(2)}) %collective-permute-start.10) | collective-permute-done | bytes 368672 | tf_op jit(solution)/shard_map/ppermute | solution.py:438
  61.9 15.9 %shard_map.88 = (bf16[720,384]{1,0:T(8,128)(2,1)S(1)}, f32[8,128]{1,0:T(8,128)S(1)}) custom-call(s32[2]{0:T(128)S(1)} %pad_add_fusion.place_ref, bf16[128,2944]{1,0:T(8,128)(2,1)S(1)} %shard_map.84.refs_0_.refs_3_, bf16[128,2944]{1,0:T(8,128)(2,1)S(1)} %collective-permute-done.7.refs_1_, bf16[128,2944]{1,0:T(8,128)(2,1)} %shard_map.86.refs_2_, ...), custom_call_target="tpu_custom_call" | custom-call | flops 1024 | bytes 1024 | tf_op jit(solution)/shard_map/pallas_call | solution.py:279
  77.9 2.1 %collective-permute-start.14 = (bf16[720,384]{1,0:T(8,128)(2,1)S(1)}, bf16[720,384]{1,0:T(8,128)(2,1)S(1)}, u32[]{:S(2)}, u32[]{:S(2)}) collective-permute-start(bf16[720,384]{1,0:T(8,128)(2,1)S(1)} %get-tuple-element.59.refs_4_), channel_id=1, source_target_pairs={{0,2},{1,3},{2,0},{3,1},{4,6},{5,7},{6,4},{7,5},{8,10},{9,11},{10,... | collective-permute-start | bytes 1658888 | tf_op jit(solution)/shard_map/ppermute | solution.py:438
  80.0 1.5 collective-permute-start.17
  81.5 9.3 %collective-permute-done.17.refs_6_ = bf16[720,256]{1,0:T(8,128)(2,1)S(1)} collective-permute-done((bf16[720,256]{1,0:T(8,128)(2,1)S(1)}, bf16[720,256]{1,0:T(8,128)(2,1)S(1)}, u32[]{:S(2)}, u32[]{:S(2)}) %collective-permute-start.17) | collective-permute-done | bytes 368672 | tf_op jit(solution)/shard_map/ppermute | solution.py:453
  90.8 4.9 %shard_map.89 = (bf16[1,128,720]{2,1,0:T(8,128)(2,1)S(1)}, bf16[1,128,720]{2,1,0:T(8,128)(2,1)S(1)}) custom-call(s32[2]{0:T(128)S(1)} %pad_add_fusion.place_ref, bf16[128,2944]{1,0:T(8,128)(2,1)S(1)} %shard_map.84.refs_0_.refs_3_, bf16[128,2944]{1,0:T(8,128)(2,1)S(1)} %collective-permute-done.7.refs_1_, bf16[720,256]{1,0:T(8,128)(2,1)S(1)} %get-tuple-element.57.refs_2_, ...), custom_call_target="tpu_custom_call" | custom-call | flops 1024 | bytes 1024 | tf_op jit(solution)/shard_map/pallas_call | solution.py:384
  96.5 2.3 %collective-permute-start.13 = (bf16[720,384]{1,0:T(8,128)(2,1)S(1)}, bf16[720,384]{1,0:T(8,128)(2,1)S(1)}, u32[]{:S(2)}, u32[]{:S(2)}) collective-permute-start(bf16[720,384]{1,0:T(8,128)(2,1)S(1)} %get-tuple-element.59.refs_4_), channel_id=1, source_target_pairs={{0,1},{1,0},{2,3},{3,2},{4,5},{5,4},{6,7},{7,6},{8,9},{9,8},{10,11... | collective-permute-start | bytes 1658888 | tf_op jit(solution)/shard_map/ppermute | solution.py:438
  98.7 6.8 %collective-permute-done.14.refs_0_.refs_6_ = bf16[720,384]{1,0:T(8,128)(2,1)S(1)} collective-permute-done((bf16[720,384]{1,0:T(8,128)(2,1)S(1)}, bf16[720,384]{1,0:T(8,128)(2,1)S(1)}, u32[]{:S(2)}, u32[]{:S(2)}) %collective-permute-start.14) | collective-permute-done | bytes 552992 | tf_op jit(solution)/shard_map/ppermute | solution.py:438
  105.6 1.3 collective-permute-start.18
  106.9 1.6 %collective-permute-start.12 = (f32[8,128]{1,0:T(8,128)S(1)}, f32[8,128]{1,0:T(8,128)S(1)}, u32[]{:S(2)}, u32[]{:S(2)}) collective-permute-start(f32[8,128]{1,0:T(8,128)S(1)} %get-tuple-element.58), channel_id=1, source_target_pairs={{0,16},{16,0},{1,17},{17,1},{2,18},{18,2},{3,19},{19,3},{4,20},{20... | collective-permute-start | bytes 12296 | tf_op jit(solution)/shard_map/ppermute | solution.py:516
  108.5 2.1 %collective-permute-done.12 = f32[8,128]{1,0:T(8,128)S(1)} collective-permute-done((f32[8,128]{1,0:T(8,128)S(1)}, f32[8,128]{1,0:T(8,128)S(1)}, u32[]{:S(2)}, u32[]{:S(2)}) %collective-permute-start.12) | collective-permute-done | bytes 4128 | tf_op jit(solution)/shard_map/ppermute | solution.py:516
  111.7 4.8 %collective-permute-done.13.refs_5_ = bf16[720,384]{1,0:T(8,128)(2,1)S(1)} collective-permute-done((bf16[720,384]{1,0:T(8,128)(2,1)S(1)}, bf16[720,384]{1,0:T(8,128)(2,1)S(1)}, u32[]{:S(2)}, u32[]{:S(2)}) %collective-permute-start.13) | collective-permute-done | bytes 552992 | tf_op jit(solution)/shard_map/ppermute | solution.py:438
  116.5 11.8 %collective-permute-done.18.refs_8_ = bf16[720,384]{1,0:T(8,128)(2,1)S(1)} collective-permute-done((bf16[720,384]{1,0:T(8,128)(2,1)S(1)}, bf16[720,384]{1,0:T(8,128)(2,1)S(1)}, u32[]{:S(2)}, u32[]{:S(2)}) %collective-permute-start.18) | collective-permute-done | bytes 552992 | tf_op jit(solution)/shard_map/ppermute | solution.py:453
  128.3 9.0 %shard_map.91 = (bf16[2,128,720]{2,1,0:T(8,128)(2,1)S(1)}, bf16[2,128,720]{2,1,0:T(8,128)(2,1)S(1)}) custom-call(s32[2]{0:T(128)S(1)} %pad_add_fusion.place_ref, bf16[128,2944]{1,0:T(8,128)(2,1)S(1)} %shard_map.84.refs_0_.refs_3_, bf16[128,2944]{1,0:T(8,128)(2,1)S(1)} %collective-permute-done.7.refs_1_, bf16[128,2944]{1,0:T(8,128)(2,1)} %shard_map.86.refs_2_, ...), custom_call_target="tpu_custom_call" | custom-call | flops 1024 | bytes 1024 | tf_op jit(solution)/shard_map/pallas_call | solution.py:384
  137.4 1.7 %collective-permute-done.19 = bf16[2,128,720]{2,1,0:T(8,128)(2,1)S(1)} collective-permute-done((bf16[2,128,720]{2,1,0:T(8,128)(2,1)S(1)}, bf16[2,128,720]{2,1,0:T(8,128)(2,1)S(1)}, u32[]{:S(2)}, u32[]{:S(2)}) %collective-permute-start.19) | collective-permute-done | bytes 368672 | tf_op jit(solution)/shard_map/ppermute | solution.py:438
  139.2 2.6 %collective-permute-start.26 = (bf16[32,720]{1,0:T(8,128)(2,1)S(1)}, bf16[32,720]{1,0:T(8,128)(2,1)S(1)}, u32[]{:S(2)}, u32[]{:S(2)}) collective-permute-start(bf16[32,720]{1,0:T(8,128)(2,1)S(1)} %get-tuple-element.71), channel_id=1, source_target_pairs={{0,11},{1,10},{2,9},{3,8},{4,15},{5,14},{6,13},{7,12},{8,3},{9,2},... | collective-permute-start | bytes 138248 | tf_op jit(solution)/shard_map/ppermute | solution.py:557
  141.8 2.2 %collective-permute-start.25 = (bf16[32,720]{1,0:T(8,128)(2,1)S(1)}, bf16[32,720]{1,0:T(8,128)(2,1)S(1)}, u32[]{:S(2)}, u32[]{:S(2)}) collective-permute-start(bf16[32,720]{1,0:T(8,128)(2,1)S(1)} %get-tuple-element.72), channel_id=1, source_target_pairs={{0,3},{1,2},{2,1},{3,0},{4,7},{5,6},{6,5},{7,4},{8,11},{9,10},{10,... | collective-permute-start | bytes 138248 | tf_op jit(solution)/shard_map/ppermute | solution.py:557
  144.1 2.9 %collective-permute-start.23 = (bf16[32,720]{1,0:T(8,128)(2,1)S(1)}, bf16[32,720]{1,0:T(8,128)(2,1)S(1)}, u32[]{:S(2)}, u32[]{:S(2)}) collective-permute-start(bf16[32,720]{1,0:T(8,128)(2,1)S(1)} %get-tuple-element.74), channel_id=1, source_target_pairs={{0,2},{1,3},{2,0},{3,1},{4,6},{5,7},{6,4},{7,5},{8,10},{9,11},{10,... | collective-permute-start | bytes 138248 | tf_op jit(solution)/shard_map/ppermute | solution.py:557
  147.1 2.8 %collective-permute-start.21 = (bf16[32,720]{1,0:T(8,128)(2,1)S(1)}, bf16[32,720]{1,0:T(8,128)(2,1)S(1)}, u32[]{:S(2)}, u32[]{:S(2)}) collective-permute-start(bf16[32,720]{1,0:T(8,128)(2,1)S(1)} %get-tuple-element.76), channel_id=1, source_target_pairs={{0,1},{1,0},{2,3},{3,2},{4,5},{5,4},{6,7},{7,6},{8,9},{9,8},{10,11... | collective-permute-start | bytes 138248 | tf_op jit(solution)/shard_map/ppermute | solution.py:557
  154.0 1.4 shard_map.92
  (47 shorter events, 13.4 us)
Async XLA Ops:
  0.0 0.9 copy-start.2
  0.9 0.7 copy-start.3
  1.6 0.7 copy-start.4
  2.3 0.7 copy-start.5
  3.2 18.5 %collective-permute-start.6 = (bf16[32,2944]{1,0:T(8,128)(2,1)S(1)}, bf16[32,2944]{1,0:T(8,128)(2,1)S(1)}, u32[]{:S(2)}, u32[]{:S(2)}) collective-permute-start(bf16[32,2944]{1,0:T(8,128)(2,1)S(1)} %shard_map.82._after_ref.refs_0_), channel_id=1, source_target_pairs={{0,3},{1,2},{2,1},{3,0},{4,7},{5,6},{6,5},{7,4},{8,11},{9,10},{10,... | collective-permute-start | bytes 565256 | tf_op jit(solution)/shard_map/ppermute | solution.py:438
  8.3 16.0 %collective-permute-start.5 = (bf16[32,2944]{1,0:T(8,128)(2,1)S(1)}, bf16[32,2944]{1,0:T(8,128)(2,1)S(1)}, u32[]{:S(2)}, u32[]{:S(2)}) collective-permute-start(bf16[32,2944]{1,0:T(8,128)(2,1)S(1)} %shard_map.82._after_ref.refs_0_), channel_id=1, source_target_pairs={{0,2},{1,3},{2,0},{3,1},{4,6},{5,7},{6,4},{7,5},{8,10},{9,11},{10,... | collective-permute-start | bytes 565256 | tf_op jit(solution)/shard_map/ppermute | solution.py:438
  8.3 16.0 %collective-permute-start.4 = (bf16[32,2944]{1,0:T(8,128)(2,1)S(1)}, bf16[32,2944]{1,0:T(8,128)(2,1)S(1)}, u32[]{:S(2)}, u32[]{:S(2)}) collective-permute-start(bf16[32,2944]{1,0:T(8,128)(2,1)S(1)} %shard_map.82._after_ref.refs_0_), channel_id=1, source_target_pairs={{0,1},{1,0},{2,3},{3,2},{4,5},{5,4},{6,7},{7,6},{8,9},{9,8},{10,11... | collective-permute-start | bytes 565256 | tf_op jit(solution)/shard_map/ppermute | solution.py:438
  10.5 5.8 %copy-start = (bf16[2,2880,2,720]{1,3,2,0:T(8,128)(2,1)S(1)}, bf16[2,2880,2,720]{1,3,2,0:T(8,128)(2,1)}, u32[]{:S(2)}) copy-start(bf16[2,2880,2,720]{1,3,2,0:T(8,128)(2,1)} %param.14) | copy-start | bytes 49766404
  21.7 5.8 %copy-start.6 = (bf16[4,720,2880]{2,1,0:T(8,128)(2,1)}, bf16[4,720,2880]{2,1,0:T(8,128)(2,1)S(1)}, u32[]{:S(2)}) copy-start(bf16[4,720,2880]{2,1,0:T(8,128)(2,1)S(1)} %shard_map.83) | copy-start | bytes 49766404
  27.5 2.2 %collective-permute-start.7 = (bf16[128,2944]{1,0:T(8,128)(2,1)S(1)}, bf16[128,2944]{1,0:T(8,128)(2,1)S(1)}, u32[]{:S(2)}, u32[]{:S(2)}) collective-permute-start(bf16[128,2944]{1,0:T(8,128)(2,1)S(1)} %shard_map.84.refs_0_.refs_3_), channel_id=1, source_target_pairs={{0,4},{4,0},{8,12},{12,8},{1,5},{5,1},{9,13},{13,9},{2,6},{6,2},{1... | collective-permute-start | bytes 2261000 | tf_op jit(solution)/shard_map/ppermute | solution.py:438
  27.5 19.3 %collective-permute-start.8 = (bf16[128,2944]{1,0:T(8,128)(2,1)S(1)}, bf16[128,2944]{1,0:T(8,128)(2,1)S(1)}, u32[]{:S(2)}, u32[]{:S(2)}) collective-permute-start(bf16[128,2944]{1,0:T(8,128)(2,1)S(1)} %shard_map.84.refs_0_.refs_3_), channel_id=1, source_target_pairs={{0,8},{4,12},{8,0},{12,4},{1,9},{5,13},{9,1},{13,5},{2,10},{6,14},... | collective-permute-start | bytes 2261000 | tf_op jit(solution)/shard_map/ppermute | solution.py:438
  47.7 14.2 %collective-permute-start.9 = (bf16[128,2944]{1,0:T(8,128)(2,1)}, bf16[128,2944]{1,0:T(8,128)(2,1)}, u32[]{:S(2)}, u32[]{:S(2)}) collective-permute-start(bf16[128,2944]{1,0:T(8,128)(2,1)} %shard_map.86.refs_2_), channel_id=1, source_target_pairs={{0,4},{4,0},{8,12},{12,8},{1,5},{5,1},{9,13},{13,9},{2,6},{6,2},{1... | collective-permute-start | bytes 2261000 | tf_op jit(solution)/shard_map/ppermute | solution.py:438
  47.7 12.4 %collective-permute-start.11 = (bf16[720,256]{1,0:T(8,128)(2,1)S(1)}, bf16[720,256]{1,0:T(8,128)(2,1)S(1)}, u32[]{:S(2)}, u32[]{:S(2)}) collective-permute-start(bf16[720,256]{1,0:T(8,128)(2,1)S(1)} %get-tuple-element.57.refs_2_), channel_id=1, source_target_pairs={{1,2},{2,1},{5,6},{6,5},{9,10},{10,9},{13,14},{14,13},{17,18},{18,... | collective-permute-start | bytes 1105928 | tf_op jit(solution)/shard_map/ppermute | solution.py:446
  48.4 13.5 %collective-permute-start.10 = (bf16[720,256]{1,0:T(8,128)(2,1)S(1)}, bf16[720,256]{1,0:T(8,128)(2,1)S(1)}, u32[]{:S(2)}, u32[]{:S(2)}) collective-permute-start(bf16[720,256]{1,0:T(8,128)(2,1)S(1)} %get-tuple-element.57.refs_2_), channel_id=1, source_target_pairs={{0,1},{1,0},{2,3},{3,2},{4,5},{5,4},{6,7},{7,6},{8,9},{9,8},{10,11... | collective-permute-start | bytes 1105928 | tf_op jit(solution)/shard_map/ppermute | solution.py:438
  52.6 27.4 %collective-permute-start.16 = (bf16[720,256]{1,0:T(8,128)(2,1)S(1)}, bf16[720,256]{1,0:T(8,128)(2,1)S(1)}, u32[]{:S(2)}, u32[]{:S(2)}) collective-permute-start(bf16[720,256]{1,0:T(8,128)(2,1)S(1)} %get-tuple-element.57.refs_2_), channel_id=1, source_target_pairs={{0,2},{1,3},{2,0},{3,1},{4,6},{5,7},{6,4},{7,5},{8,10},{9,11},{10,... | collective-permute-start | bytes 1105928 | tf_op jit(solution)/shard_map/ppermute | solution.py:438
  54.0 3.4 %copy-start.1 = (bf16[2,2880,720]{1,2,0:T(8,128)(2,1)S(1)}, bf16[2,2880,720]{1,2,0:T(8,128)(2,1)}, u32[]{:S(2)}) copy-start(bf16[2,2880,720]{1,2,0:T(8,128)(2,1)} %param.16) | copy-start | bytes 24883204
  77.9 27.6 %collective-permute-start.14 = (bf16[720,384]{1,0:T(8,128)(2,1)S(1)}, bf16[720,384]{1,0:T(8,128)(2,1)S(1)}, u32[]{:S(2)}, u32[]{:S(2)}) collective-permute-start(bf16[720,384]{1,0:T(8,128)(2,1)S(1)} %get-tuple-element.59.refs_4_), channel_id=1, source_target_pairs={{0,2},{1,3},{2,0},{3,1},{4,6},{5,7},{6,4},{7,5},{8,10},{9,11},{10,... | collective-permute-start | bytes 1658888 | tf_op jit(solution)/shard_map/ppermute | solution.py:438
  80.0 10.8 %collective-permute-start.17 = (bf16[720,256]{1,0:T(8,128)(2,1)S(1)}, bf16[720,256]{1,0:T(8,128)(2,1)S(1)}, u32[]{:S(2)}, u32[]{:S(2)}) collective-permute-start(bf16[720,256]{1,0:T(8,128)(2,1)S(1)} %collective-permute-done.16.refs_4_), channel_id=1, source_target_pairs={{2,3},{1,0},{6,7},{5,4},{10,11},{9,8},{14,15},{13,12},{18,19},{17,... | collective-permute-start | bytes 1105928 | tf_op jit(solution)/shard_map/ppermute | solution.py:453
  95.7 16.0 %collective-permute-start.15 = (bf16[720,384]{1,0:T(8,128)(2,1)S(1)}, bf16[720,384]{1,0:T(8,128)(2,1)S(1)}, u32[]{:S(2)}, u32[]{:S(2)}) collective-permute-start(bf16[720,384]{1,0:T(8,128)(2,1)S(1)} %get-tuple-element.59.refs_4_), channel_id=1, source_target_pairs={{1,2},{2,1},{5,6},{6,5},{9,10},{10,9},{13,14},{14,13},{17,18},{18,... | collective-permute-start | bytes 1658888 | tf_op jit(solution)/shard_map/ppermute | solution.py:446
  96.5 20.0 %collective-permute-start.13 = (bf16[720,384]{1,0:T(8,128)(2,1)S(1)}, bf16[720,384]{1,0:T(8,128)(2,1)S(1)}, u32[]{:S(2)}, u32[]{:S(2)}) collective-permute-start(bf16[720,384]{1,0:T(8,128)(2,1)S(1)} %get-tuple-element.59.refs_4_), channel_id=1, source_target_pairs={{0,1},{1,0},{2,3},{3,2},{4,5},{5,4},{6,7},{7,6},{8,9},{9,8},{10,11... | collective-permute-start | bytes 1658888 | tf_op jit(solution)/shard_map/ppermute | solution.py:438
  105.6 22.7 %collective-permute-start.18 = (bf16[720,384]{1,0:T(8,128)(2,1)S(1)}, bf16[720,384]{1,0:T(8,128)(2,1)S(1)}, u32[]{:S(2)}, u32[]{:S(2)}) collective-permute-start(bf16[720,384]{1,0:T(8,128)(2,1)S(1)} %shard_map.90), channel_id=1, source_target_pairs={{2,3},{1,0},{6,7},{5,4},{10,11},{9,8},{14,15},{13,12},{18,19},{17,... | collective-permute-start | bytes 1658888 | tf_op jit(solution)/shard_map/ppermute | solution.py:453
  106.9 3.7 %collective-permute-start.12 = (f32[8,128]{1,0:T(8,128)S(1)}, f32[8,128]{1,0:T(8,128)S(1)}, u32[]{:S(2)}, u32[]{:S(2)}) collective-permute-start(f32[8,128]{1,0:T(8,128)S(1)} %get-tuple-element.58), channel_id=1, source_target_pairs={{0,16},{16,0},{1,17},{17,1},{2,18},{18,2},{3,19},{19,3},{4,20},{20... | collective-permute-start | bytes 12296 | tf_op jit(solution)/shard_map/ppermute | solution.py:516
  137.3 1.8 %collective-permute-start.19 = (bf16[2,128,720]{2,1,0:T(8,128)(2,1)S(1)}, bf16[2,128,720]{2,1,0:T(8,128)(2,1)S(1)}, u32[]{:S(2)}, u32[]{:S(2)}) collective-permute-start(bf16[2,128,720]{2,1,0:T(8,128)(2,1)S(1)} %get-tuple-element.69), channel_id=1, source_target_pairs={{0,4},{4,0},{8,12},{12,8},{1,5},{5,1},{9,13},{13,9},{2,6},{6,2},{1... | collective-permute-start | bytes 1105928 | tf_op jit(solution)/shard_map/ppermute | solution.py:438
  139.2 7.9 %collective-permute-start.26 = (bf16[32,720]{1,0:T(8,128)(2,1)S(1)}, bf16[32,720]{1,0:T(8,128)(2,1)S(1)}, u32[]{:S(2)}, u32[]{:S(2)}) collective-permute-start(bf16[32,720]{1,0:T(8,128)(2,1)S(1)} %get-tuple-element.71), channel_id=1, source_target_pairs={{0,11},{1,10},{2,9},{3,8},{4,15},{5,14},{6,13},{7,12},{8,3},{9,2},... | collective-permute-start | bytes 138248 | tf_op jit(solution)/shard_map/ppermute | solution.py:557
  141.8 8.1 %collective-permute-start.25 = (bf16[32,720]{1,0:T(8,128)(2,1)S(1)}, bf16[32,720]{1,0:T(8,128)(2,1)S(1)}, u32[]{:S(2)}, u32[]{:S(2)}) collective-permute-start(bf16[32,720]{1,0:T(8,128)(2,1)S(1)} %get-tuple-element.72), channel_id=1, source_target_pairs={{0,3},{1,2},{2,1},{3,0},{4,7},{5,6},{6,5},{7,4},{8,11},{9,10},{10,... | collective-permute-start | bytes 138248 | tf_op jit(solution)/shard_map/ppermute | solution.py:557
  144.1 6.4 %collective-permute-start.24 = (bf16[32,720]{1,0:T(8,128)(2,1)S(1)}, bf16[32,720]{1,0:T(8,128)(2,1)S(1)}, u32[]{:S(2)}, u32[]{:S(2)}) collective-permute-start(bf16[32,720]{1,0:T(8,128)(2,1)S(1)} %get-tuple-element.73), channel_id=1, source_target_pairs={{0,10},{1,11},{2,8},{3,9},{4,14},{5,15},{6,12},{7,13},{8,2},{9,3},... | collective-permute-start | bytes 138248 | tf_op jit(solution)/shard_map/ppermute | solution.py:557
  144.1 7.4 %collective-permute-start.23 = (bf16[32,720]{1,0:T(8,128)(2,1)S(1)}, bf16[32,720]{1,0:T(8,128)(2,1)S(1)}, u32[]{:S(2)}, u32[]{:S(2)}) collective-permute-start(bf16[32,720]{1,0:T(8,128)(2,1)S(1)} %get-tuple-element.74), channel_id=1, source_target_pairs={{0,2},{1,3},{2,0},{3,1},{4,6},{5,7},{6,4},{7,5},{8,10},{9,11},{10,... | collective-permute-start | bytes 138248 | tf_op jit(solution)/shard_map/ppermute | solution.py:557
  146.9 5.1 %collective-permute-start.22 = (bf16[32,720]{1,0:T(8,128)(2,1)S(1)}, bf16[32,720]{1,0:T(8,128)(2,1)S(1)}, u32[]{:S(2)}, u32[]{:S(2)}) collective-permute-start(bf16[32,720]{1,0:T(8,128)(2,1)S(1)} %get-tuple-element.75), channel_id=1, source_target_pairs={{0,9},{1,8},{2,11},{3,10},{4,13},{5,12},{6,15},{7,14},{8,1},{9,0},... | collective-permute-start | bytes 138248 | tf_op jit(solution)/shard_map/ppermute | solution.py:557
  147.1 5.8 %collective-permute-start.21 = (bf16[32,720]{1,0:T(8,128)(2,1)S(1)}, bf16[32,720]{1,0:T(8,128)(2,1)S(1)}, u32[]{:S(2)}, u32[]{:S(2)}) collective-permute-start(bf16[32,720]{1,0:T(8,128)(2,1)S(1)} %get-tuple-element.76), channel_id=1, source_target_pairs={{0,1},{1,0},{2,3},{3,2},{4,5},{5,4},{6,7},{7,6},{8,9},{9,8},{10,11... | collective-permute-start | bytes 138248 | tf_op jit(solution)/shard_map/ppermute | solution.py:557
  149.9 4.1 %collective-permute-start.20 = (bf16[32,720]{1,0:T(8,128)(2,1)S(1)}, bf16[32,720]{1,0:T(8,128)(2,1)S(1)}, u32[]{:S(2)}, u32[]{:S(2)}) collective-permute-start(bf16[32,720]{1,0:T(8,128)(2,1)S(1)} %get-tuple-element.77), channel_id=1, source_target_pairs={{0,8},{1,9},{2,10},{3,11},{4,12},{5,13},{6,14},{7,15},{8,0},{9,1},... | collective-permute-start | bytes 138248 | tf_op jit(solution)/shard_map/ppermute | solution.py:557

commit v4 on v2

--- a/solution.py
+++ b/solution.py
@@ -11,7 +11,7 @@
 swish_beta = 1.702
 META = 64
 LANES = 128
-VMEM_LIMIT = 26 * 1024 * 1024
+VMEM_LIMIT = 24 * 1024 * 1024
 HINT = pl.CostEstimate(flops=1024, bytes_accessed=1024, transcendentals=0)
 F32 = jnp.float32
 BF16 = jnp.bfloat16
@@ -69,7 +69,7 @@
     )
 
 
-def dequant_kernel(codes_ref, scales_ref, _after_ref, out_ref):
+def dequant_kernel(codes_ref, scales_ref, _after_ref, out_ref, mark_ref):
     width = codes_ref.shape[2]
     scales = scales_ref[0]
     blocks = scales.shape[1]
@@ -82,6 +82,7 @@
         inside = jnp.logical_and(column >= first, column < first + width // blocks)
         wide = dot(scales, inside.astype(F32).astype(BF16), ((1,), (0,)))
         out_ref[0, :, at:end] = (codes_ref[0, :, at:end].astype(F32) * wide).astype(BF16)
+    mark_ref[...] = jnp.zeros_like(mark_ref)
 
 
 def dequant(codes, scales, after):
@@ -95,32 +96,45 @@
             pl.BlockSpec((1, rows, blocks), lambda i: (i, 0, 0)),
             pl.BlockSpec(memory_space=pl.ANY),
         ],
-        out_specs=pl.BlockSpec((1, rows, width), lambda i: (i, 0, 0)),
-        out_shape=jax.ShapeDtypeStruct(codes.shape, BF16),
+        out_specs=[
+            pl.BlockSpec((1, rows, width), lambda i: (i, 0, 0)),
+            pl.BlockSpec((8, LANES), lambda i: (0, 0)),
+        ],
+        out_shape=[
+            jax.ShapeDtypeStruct(codes.shape, BF16),
+            jax.ShapeDtypeStruct((8, LANES), F32),
+        ],
         compiler_params=params(),
         cost_estimate=HINT,
-    )(codes, scales, after)
-
-
-def join_kernel(count, *refs):
-    out_ref = refs[count + 1]
-    rows = refs[0].shape[0]
-    for k in range(count):
-        out_ref[k * rows : (k + 1) * rows] = refs[k][...]
-
-
-def join(parts, after):
+    )(pltpu.with_memory_space_constraint(codes, pltpu.HBM), scales, after)
+
+
+def join_kernel(count, pieces, *refs):
+    outs = refs[-pieces:]
+    rows, size = refs[0].shape[0], outs[0].shape[0]
+    for p, out_ref in enumerate(outs):
+        if size >= rows:
+            for k in range(size // rows):
+                out_ref[k * rows : (k + 1) * rows] = refs[p * (size // rows) + k][...]
+        else:
+            at = p * size % rows
+            out_ref[...] = refs[p * size // rows][at : at + size]
+
+
+def join(parts, after, pieces=1):
     rows, width = parts[0].shape
     count = len(parts)
+    size = count * rows // pieces
     return pl.pallas_call(
-        functools.partial(join_kernel, count),
+        functools.partial(join_kernel, count, pieces),
         grid=(1,),
         in_specs=[pl.BlockSpec((rows, width), lambda i: (0, 0))] * count
-        + [pl.BlockSpec(memory_space=pl.ANY)],
-        out_specs=pl.BlockSpec((count * rows, width), lambda i: (0, 0)),
-        out_shape=jax.ShapeDtypeStruct((count * rows, width), BF16),
+        + [pl.BlockSpec(memory_space=pl.ANY)] * len(after),
+        out_specs=[pl.BlockSpec((size, width), lambda i: (0, 0))] * pieces,
+        out_shape=[jax.ShapeDtypeStruct((size, width), BF16)] * pieces,
         compiler_params=params(),
-    )(*parts, after)
+        cost_estimate=HINT,
+    )(*parts, *after)
 
 
 class Plan:
@@ -134,8 +148,8 @@
     named = jnp.zeros((meta.shape[0], 1), F32)
     weight = jnp.zeros((meta.shape[0], 1), F32)
     for k in range(top):
-        hit = (meta[:, META + k : META + k + 1] == expert).astype(F32)
-        at = META + k
+        at = meta.shape[1] - META + k
+        hit = (meta[:, at : at + 1] == expert).astype(F32)
         total = (
             meta[:, at + top : at + top + 1]
             + meta[:, at + 2 * top : at + 2 * top + 1]
@@ -203,66 +217,111 @@
     )
 
 
-def inner_kernel(plan, arrays, place_ref, *refs):
+def metas_of(layout, refs, width):
+    metas, at = [], 0
+    for count in layout:
+        several = [ref[:, width:].astype(F32) for ref in refs[at : at + count]]
+        metas.append(jnp.concatenate(several, axis=0))
+        at += count
+    return metas
+
+
+def rows_kernel(plan, layout, place_ref, *refs):
+    arrays = sum(layout)
     tokens = refs[:arrays]
-    weight_ref = refs[arrays]
-    act_ref, most_ref, rows_ref, mask_ref = refs[arrays + 2 :]
-    width = weight_ref.shape[3]
-
-    @pl.when(pl.program_id(0) == 0)
-    def _():
-        ep, sub = place_ref[0], place_ref[1]
-        metas = []
-        for c in range(arrays // 2):
-            pair = [tokens[2 * c + h][:, width - META :].astype(F32) for h in range(2)]
-            metas.append(jnp.concatenate(pair, axis=0))
-        columns, bounds = route(metas, plan, ep, sub)
+    meta_ref, most_ref = refs[arrays : arrays + 2]
+    outs = refs[arrays + 2 :]
+    width = outs[0].shape[0]
+    ep, sub = place_ref[0], place_ref[1]
+    metas = metas_of(layout, tokens, width)
+    at = 0
+    for ref in tokens:
+        meta_ref[at : at + ref.shape[0]] = ref[:, width - META :]
+        at += ref.shape[0]
+    columns, bounds = route(metas, plan, ep, sub)
+    begin = 0
+    for part, mask_ref in enumerate(outs[1::2]):
+        mask_ref[...] = jnp.zeros_like(mask_ref)
+        size = mask_ref.shape[1]
         for slot, mask in enumerate(slot_masks(bounds, plan)):
-            mask_ref[slot : slot + 1] = mask
-        half = tokens[0].shape[0]
-        hots = []
-        for places in columns:
-            hot = None
-            for place, _w in places:
-                hit = rows_of(place, plan).astype(F32)
-                hot = hit if hot is None else hot + hit
-            hots.append(hot.astype(BF16))
-        chunk = 256
-        for at in range(0, width, chunk):
-            end = min(at + chunk, width)
-            total = None
-            for c, hot in enumerate(hots):
-                for h in range(2):
-                    part = dot(
-                        tokens[2 * c + h][:, at:end], hot[h * half : (h + 1) * half], ((0,), (0,))
-                    )
-                    total = part if total is None else total + part
-            rows_ref[at:end] = total.astype(BF16)
-        lane = lax.broadcasted_iota(jnp.int32, (metas[0].shape[0], LANES), 1).astype(F32)
-        start = [jnp.zeros((1, 1), F32)] * plan.eps
-        owner = lax.div(lax.broadcasted_iota(jnp.int32, (1, LANES), 1), plan.slots)
-        for column, meta in enumerate(metas):
-            flags = jnp.zeros((meta.shape[0], LANES), F32)
-            for k in range(plan.top):
-                flags = flags + (meta[:, META + k : META + k + 1] == lane).astype(F32)
-            counts = jnp.sum(flags, axis=0, keepdims=True)
-            for e in range(plan.eps):
-                if column:
-                    start[e] = jnp.maximum(start[e], float(plan.holds[column - 1]))
-                start[e] = start[e] + jnp.sum(
-                    jnp.where(owner == e, counts, 0.0), axis=1, keepdims=True
-                )
-        most_ref[...] = jnp.broadcast_to(functools.reduce(jnp.maximum, start), most_ref.shape)
-
-    slots, _two, block, _width = weight_ref.shape
-    both = dot(weight_ref[...].reshape(slots * 2 * block, width), rows_ref[...], ((1,), (0,)))
-    gating, upward = both[:block], both[block : 2 * block]
-    for slot in range(1, plan.slots):
-        mine = mask_ref[slot : slot + 1] > 0.0
-        at = 2 * slot * block
-        gating = jnp.where(mine, both[at : at + block], gating)
-        upward = jnp.where(mine, both[at + block : at + 2 * block], upward)
+            mask_ref[slot : slot + 1] = mask[:, begin : begin + size]
+        begin += size
+    hots = []
+    for places in columns:
+        hot = None
+        for place, _weight in places:
+            hit = rows_of(place, plan).astype(F32)
+            hot = hit if hot is None else hot + hit
+        hots.append(hot.astype(BF16))
+    hot = jnp.concatenate(hots, axis=0) if len(hots) > 1 else hots[0]
+    chunk = 256
+    for at in range(0, width, chunk):
+        end = min(at + chunk, width)
+        several = [ref[:, at:end] for ref in tokens]
+        total = dot(jnp.concatenate(several, axis=0), hot, ((0,), (0,)))
+        begin = 0
+        for rows_ref in outs[::2]:
+            rows_ref[at:end] = total[:, begin : begin + rows_ref.shape[1]].astype(BF16)
+            begin += rows_ref.shape[1]
+    lane = lax.broadcasted_iota(jnp.int32, (metas[0].shape[0], LANES), 1).astype(F32)
+    owner = lax.div(lax.broadcasted_iota(jnp.int32, (1, LANES), 1), plan.slots)
+    start = [jnp.zeros((1, 1), F32)] * plan.eps
+    for column, meta in enumerate(metas):
+        flags = jnp.zeros((meta.shape[0], LANES), F32)
+        for k in range(plan.top):
+            flags = flags + (meta[:, k : k + 1] == lane).astype(F32)
+        counts = jnp.sum(flags, axis=0, keepdims=True)
+        for e in range(plan.eps):
+            if column:
+                start[e] = jnp.maximum(start[e], float(plan.holds[column - 1]))
+            start[e] = start[e] + jnp.sum(
+                jnp.where(owner == e, counts, 0.0), axis=1, keepdims=True
+            )
+    most_ref[...] = jnp.broadcast_to(functools.reduce(jnp.maximum, start), most_ref.shape)
+
+
+def rows_in(plan, place, held, split=None):
+    layout = tuple(len(arrays) for arrays in held)
+    tokens = [t for arrays in held for t in arrays]
+    width = tokens[0].shape[1] - META
+    total = sum(t.shape[0] for t in tokens)
+    split = split or (plan.rows,)
+    specs = [pl.BlockSpec((total, LANES), lambda i: (0, 0)), pl.BlockSpec((8, LANES), lambda i: (0, 0))]
+    shapes = [
+        jax.ShapeDtypeStruct((total, LANES), BF16),
+        jax.ShapeDtypeStruct((8, LANES), F32),
+    ]
+    for size in split:
+        specs.append(pl.BlockSpec((width, size), lambda i: (0, 0)))
+        specs.append(pl.BlockSpec((8, size), lambda i: (0, 0)))
+        shapes.append(jax.ShapeDtypeStruct((width, size), BF16))
+        shapes.append(jax.ShapeDtypeStruct((8, size), F32))
+    return pl.pallas_call(
+        functools.partial(rows_kernel, plan, layout),
+        grid=(1,),
+        in_specs=[pl.BlockSpec(memory_space=pltpu.SMEM)]
+        + [pl.BlockSpec(t.shape, lambda i: (0, 0)) for t in tokens],
+        out_specs=specs,
+        out_shape=shapes,
+        compiler_params=params(),
+        cost_estimate=HINT,
+    )(place, *tokens)
+
+
+def inner_kernel(plan, rows_ref, mask_ref, weight_ref, *refs):
+    act_ref, mark_ref = refs[-2:]
+    gating = upward = None
+    for slot in range(plan.slots):
+        gate = dot(weight_ref[slot, 0], rows_ref[...], ((1,), (0,)))
+        up = dot(weight_ref[slot, 1], rows_ref[...], ((1,), (0,)))
+        if slot == 0:
+            gating, upward = gate, up
+        else:
+            mine = mask_ref[slot : slot + 1] > 0.0
+            gating = jnp.where(mine, gate, gating)
+            upward = jnp.where(mine, up, upward)
     act_ref[...] = (gating * jax.nn.sigmoid(swish_beta * gating) * (upward + 1.0)).astype(BF16)
+    mark_ref[...] = jnp.zeros_like(mark_ref)
 
 
 def piece(total):
@@ -272,40 +331,37 @@
     return total
 
 
-def inner(plan, place, tokens, weights, after):
+def inner(plan, rows, mask, weights, after):
     slots, _two, units, width = weights.shape
     block = piece(units)
-    arrays = len(tokens)
     return pl.pallas_call(
-        functools.partial(inner_kernel, plan, arrays),
+        functools.partial(inner_kernel, plan),
         grid=(units // block,),
-        in_specs=[pl.BlockSpec(memory_space=pltpu.SMEM)]
-        + [pl.BlockSpec(t.shape, lambda i: (0, 0)) for t in tokens]
-        + [pl.BlockSpec((slots, 2, block, width), lambda i: (0, 0, i, 0))]
-        + [pl.BlockSpec(memory_space=pl.ANY)],
+        in_specs=[
+            pl.BlockSpec(rows.shape, lambda i: (0, 0)),
+            pl.BlockSpec(mask.shape, lambda i: (0, 0)),
+            pl.BlockSpec((slots, 2, block, width), lambda i: (0, 0, i, 0)),
+        ]
+        + [pl.BlockSpec(memory_space=pl.ANY)] * len(after),
         out_specs=[
-            pl.BlockSpec((block, plan.rows), lambda i: (i, 0)),
+            pl.BlockSpec((block, rows.shape[1]), lambda i: (i, 0)),
             pl.BlockSpec((8, LANES), lambda i: (0, 0)),
         ],
         out_shape=[
-            jax.ShapeDtypeStruct((units, plan.rows), BF16),
+            jax.ShapeDtypeStruct((units, rows.shape[1]), BF16),
             jax.ShapeDtypeStruct((8, LANES), F32),
-        ],
-        scratch_shapes=[
-            pltpu.VMEM((width, plan.rows), BF16),
-            pltpu.VMEM((8, plan.rows), F32),
         ],
         compiler_params=params(),
         cost_estimate=HINT,
-    )(place, *tokens, weights, after)
-
-
-def outer_kernel(plan, arrays, before, blocks, place_ref, *refs):
-    metas_in = refs[:arrays]
+    )(rows, mask, weights, *after)
+
+
+def outer_kernel(plan, before, blocks, ends, place_ref, meta_ref, *refs):
+    arrays = 0
     parts = refs[arrays : arrays + blocks]
     befores = refs[arrays + blocks : arrays + blocks + before]
-    rest = refs[arrays + blocks + before :]
-    weight_ref, keep_ref, send_ref, act_ref, sum_ref = rest
+    weight_ref = refs[arrays + blocks + before]
+    keep_ref, send_ref, act_ref, sum_ref = refs[-4:]
     sub = place_ref[1]
     units = parts[0].shape[0]
     slot = pl.program_id(0)
@@ -318,7 +374,7 @@
                 @pl.when(jnp.bitwise_xor(sub, k) == b)
                 def _():
                     at = slice(b * units, (b + 1) * units)
-                    if k == 3 and blocks == 5:
+                    if k == 3 and ends:
                         inside = jnp.logical_or(sub == 1, sub == 2)
 
                         @pl.when(inside)
@@ -334,10 +390,10 @@
     ep = place_ref[0]
 
     def routed():
+        count = 2 * keep_ref.shape[1]
         metas = []
-        for c in range(arrays // 2):
-            pair = [metas_in[2 * c + h][...].astype(F32) for h in range(2)]
-            metas.append(jnp.concatenate(pair, axis=0))
+        for c in range(keep_ref.shape[0]):
+            metas.append(meta_ref[c * count : (c + 1) * count].astype(F32))
         return route(metas, plan, ep, sub)
 
     out = dot(weight_ref[0], act_ref[...], ((1,), (0,)))
@@ -375,20 +431,20 @@
                 ref[c] = value.astype(BF16)
 
 
-def outer(plan, place, tokens, parts, befores, weights):
+def outer(plan, place, meta, parts, befores, weights, after=()):
     slots, columns_out, width = weights.shape
-    arrays, blocks = len(tokens), len(parts)
-    half = tokens[0].shape[0]
-    last = tokens[0].shape[1] // LANES - 1
-    result = jax.ShapeDtypeStruct((arrays // 2, half, columns_out), BF16)
+    blocks = len(parts)
+    half = plan.group * plan.subs
+    result = jax.ShapeDtypeStruct((meta.shape[0] // (2 * half), half, columns_out), BF16)
     return pl.pallas_call(
-        functools.partial(outer_kernel, plan, arrays, len(befores), blocks),
+        functools.partial(outer_kernel, plan, len(befores), blocks, blocks > plan.subs),
         grid=(slots,),
         in_specs=[pl.BlockSpec(memory_space=pltpu.SMEM)]
-        + [pl.BlockSpec((half, LANES), lambda i: (0, last)) for t in tokens]
+        + [pl.BlockSpec(meta.shape, lambda i: (0, 0))]
         + [pl.BlockSpec(p.shape, lambda i: (0, 0)) for p in parts]
         + [pl.BlockSpec(b.shape, lambda i: (0, 0, 0)) for b in befores]
-        + [pl.BlockSpec((1, columns_out, width), lambda i: (i, 0, 0))],
+        + [pl.BlockSpec((1, columns_out, width), lambda i: (i, 0, 0))]
+        + [pl.BlockSpec(memory_space=pl.ANY)] * len(after),
         out_specs=[pl.BlockSpec(result.shape, lambda i: (0, 0, 0))] * 2,
         out_shape=[result, result],
         scratch_shapes=[
@@ -397,7 +453,7 @@
         ],
         compiler_params=params(),
         cost_estimate=HINT,
-    )(place, *tokens, *parts, *befores, weights)
+    )(place, meta, *parts, *befores, weights, *after)
 
 
 def finish_kernel(subs, columns, place_ref, *refs):
@@ -438,14 +494,18 @@
     return lax.ppermute(x, axis, [(i, i ^ offset) for i in range(count)])
 
 
-def gather_sub(x, subs):
-    if subs != 4:
-        return [x] + [swap(x, "sub", k, subs) for k in range(1, subs)]
-    two = swap(x, "sub", 2, subs)
-    one = swap(x, "sub", 1, subs)
-    middle = lax.ppermute(x, "sub", [(1, 2), (2, 1)])
-    ends = lax.ppermute(two, "sub", [(2, 3), (1, 0)])
-    return [x, one, two, middle, ends]
+def gather(x, subs):
+    return [x] + [swap(x, "sub", k, subs) for k in range(1, subs)]
+
+
+def gather_line(x):
+    one = swap(x, "sub", 1, 4)
+    two = swap(x, "sub", 2, 4)
+    return [x, one, two, lax.ppermute(x, "sub", [(1, 2), (2, 1)])]
+
+
+def gather_ends(two):
+    return lax.ppermute(two, "sub", [(2, 3), (1, 0)])
 
 
 def add(a, b):
@@ -469,22 +529,19 @@
     near = [packed] + [swap(packed, "sub", k, subs) for k in range(1, subs)]
     codes = jnp.transpose(inner_codes, (0, 2, 3, 1)).reshape(slots * 2, units, -1)
     scales = jnp.transpose(inner_scales, (0, 2, 3, 1)).reshape(slots * 2, units, -1)
-    inner_weights = dequant(codes, scales, packed).reshape(slots, 2, units, -1)
+    inner_weights, mark = dequant(codes, scales, packed)
+    inner_weights = inner_weights.reshape(slots, 2, units, -1)
     outer_codes = jnp.transpose(down_codes, (0, 2, 1))
     outer_scales = jnp.transpose(down_scales, (0, 2, 1))
-    own = join(near, inner_weights)
+    own = join(near, [mark])[0]
     other = swap(own, "ep", 1, eps)
-    held = [[own, other]]
-    for j in range(1, columns):
-        arrived = swap(own, "ep", 2 * j, eps)
-        held.append([arrived, swap(arrived, "ep", 1, eps)])
 
     capacity_rows = group * subs * 2 // rows * slots * capacity
 
     def plan(first, count, holds):
         return Plan(first, count, holds, slots, subs, group, top, eps)
 
-    if columns == 2 and capacity_rows % 384 == 0:
+    if columns == 2 and subs == 4 and capacity_rows % 384 == 0:
         most = 2 * capacity_rows
         first = capacity_rows // 384 * 256
         second = capacity_rows
@@ -492,28 +549,32 @@
         holds = (first,)
         plan0, plan1 = plan(0, first, holds), plan(first, second, holds)
         plan2 = plan(first + second, last, holds)
-        everything = held[0] + held[1]
-        act0, mark = inner(plan0, place, held[0], inner_weights, own)
-        mark = swap(mark, "ep", 1, eps)
-        parts0 = gather_sub(act0, subs)
-        act1, longest = inner(plan1, place, everything, inner_weights, mark)
-        parts1 = gather_sub(act1, subs)
+        pair = [own, other]
+        meta0, _, rows0, mask0 = rows_in(plan0, place, [pair])
+        act0, mark = inner(plan0, rows0, mask0, inner_weights, [])
+        parts0 = gather_line(act0)
+        moved = join([swap(n, "ep", 2, eps) for n in near], [mark], 4)
+        everything = [pair, list(moved) + [swap(m, "ep", 1, eps) for m in moved]]
+        meta1, longest, rows1, mask1, rows2, mask2 = rows_in(
+            plan(first, second + last, holds), place, everything, (second, last)
+        )
+        act1, _ = inner(plan1, rows1, mask1, inner_weights, [])
+        act1 = join([act1], parts0[1:])[0]
+        parts0.append(gather_ends(parts0[2]))
+        parts1 = gather(act1, subs)
+        outer_weights, _ = dequant(outer_codes, outer_scales, parts1[1])
+        sums = outer(plan0, place, meta0, parts0, [], outer_weights, parts1[1:3])
         for shift in range(1, groups):
             moved = lax.ppermute(
                 longest, "grp", [(i, (i + shift) % groups) for i in range(groups)]
             )
             longest = jnp.maximum(longest, moved)
-        outer_weights = dequant(outer_codes, outer_scales, longest)
-        sums = outer(plan0, place, held[0], parts0, [], outer_weights)
-        sums = outer(plan1, place, everything, parts1, sums, outer_weights)
+        sums = outer(plan1, place, meta1, parts1, sums, outer_weights)
 
         def more(kept, sent):
-            act, _ = inner(plan2, place, everything, inner_weights, kept)
-            return tuple(
-                outer(
-                    plan2, place, everything, gather_sub(act, subs), [kept, sent], outer_weights
-                )
-            )
+            act, _ = inner(plan2, rows2, mask2, inner_weights, [kept])
+            parts = gather(act, subs)
+            return tuple(outer(plan2, place, meta1, parts, [kept, sent], outer_weights))
 
         keep, send = lax.cond(
             longest[0, 0] > float(first + second), more, lambda a, b: (a, b), *sums
@@ -521,11 +582,14 @@
     else:
         count = -(-capacity_rows // LANES) * LANES
         each = plan(0, count, ())
-        outer_weights = dequant(outer_codes, outer_scales, own)
+        outer_weights, _ = dequant(outer_codes, outer_scales, own)
         keeps, sends = [], []
+        across = [swap(own, "ep", 2 * j, eps) for j in range(1, columns)]
+        held = [[own, other]] + [[a, swap(a, "ep", 1, eps)] for a in across]
         for pair in held:
-            act, _ = inner(each, place, pair, inner_weights, own)
-            kept, sent = outer(each, place, pair, gather_sub(act, subs), [], outer_weights)
+            meta, _, rows_here, mask = rows_in(each, place, [pair])
+            act, _ = inner(each, rows_here, mask, inner_weights, [])
+            kept, sent = outer(each, place, meta, gather(act, subs), [], outer_weights)
             keeps.append(kept)
             sends.append(sent)
         keep, send = jnp.concatenate(keeps, axis=0), jnp.concatenate(sends, axis=0)

time: 176 us -> 153 us (0.87)
  waiting for transfers between devices: 71.2 us -> 42.1 us
  local copies, waits for them, and re-layouts: 20.8 us -> 7.03 us
  Pallas kernels: 50.7 us -> 61.6 us
  starting transfers between devices: 31.2 us -> 40.2 us
    ppermute x12 -> x18, waiting for transfers between devices: 57.4 us -> 21.8 us  [swap(): return lax.ppermute(x, axis, [(i, i ^ offset) for i in range(count)])]
    unnamed x29 -> x19, local copies, waits for them, and re-layouts: 18.7 us -> 4.88 us
    ppermute x12 -> x18, starting transfers between devices: 13 us -> 25.3 us  [swap(): return lax.ppermute(x, axis, [(i, i ^ offset) for i in range(count)])]
    pallas_call x2, Pallas kernels: 8.03 us -> 18.3 us  [dequant(): pl.pallas_call(dequant_kernel, grid=(count,), in_specs=[pl.BlockSpec((1,...]
    ppermute x4 -> x2, waiting for transfers between devices: 7.11 us -> 14 us  [the longest x1 14 us: gather_ends(): return lax.ppermute(two, 'sub', [(2, 3), (1, 0)])]
    ppermute x4 -> x2, starting transfers between devices: 4.82 us -> 2.13 us  [the longest x1 1.46 us: gather_ends(): return lax.ppermute(two, 'sub', [(2, 3), (1, 0)])]
    pallas_call x5 -> x9, Pallas kernels: 41.1 us -> 41.7 us  [the longest x2 20.3 us: inner(): pl.pallas_call(functools.partial(inner_kernel, plan), grid=(units // bloc...]
  transfers between devices with their start and end apart: 24 -> 28, of which waited for: 9 -> 11; matrix products, arithmetic and copies ran while one was open for 2% -> 2% of each run, Pallas kernels for 14% -> 33%
where the time goes in v4:
time: 153 us; the launch traced here: 152 us
  Pallas kernels  61.6 us (40%)
  waiting for transfers between devices  42.1 us (28%)
  starting transfers between devices  40.2 us (26%)
  local copies, waits for them, and re-layouts  7.03 us (5%)
    ppermute x18, starting transfers between devices, swap(): return lax.ppermute(x, axis, [(i, i ^ offset) for i in range(count)])  25.3 us
    ppermute x18, waiting for transfers between devices, swap(): return lax.ppermute(x, axis, [(i, i ^ offset) for i in range(count)])  21.8 us
    pallas_call x2, Pallas kernels, inner(): pl.pallas_call(functools.partial(inner_kernel, plan), grid=(units // bloc...  20.3 us
    pallas_call x2, Pallas kernels, dequant(): pl.pallas_call(dequant_kernel, grid=(count,), in_specs=[pl.BlockSpec((1,...  18.3 us
    pallas_call x2, Pallas kernels, outer(): pl.pallas_call(functools.partial(outer_kernel, plan, len(befores), blocks...  14.7 us
    ppermute x1, waiting for transfers between devices, gather_ends(): return lax.ppermute(two, 'sub', [(2, 3), (1, 0)])  14 us
    ppermute x7, starting transfers between devices, local(): lax.ppermute(block, ('ep', 'sub'), pairs)  11.2 us
    pallas_call x2, Pallas kernels, rows_in(): pl.pallas_call(functools.partial(rows_kernel, plan, layout), grid=(1,), i...  6.53 us
  transfers between devices with their start and end apart: 28, of which 11 were waited for; matrix products, arithmetic and copies ran while one was open for 2% of the time, Pallas kernels for 33%

profile of v4, /device:TPU:0, one launch (start us, length us, event | category | flops | bytes accessed | tf_op | source)
XLA Modules:
  0.0 152.2 jit_solution(10853428830613077234)
XLA Ops:
  3.2 3.0 %collective-permute-start.3 = (bf16[32,2944]{1,0:T(8,128)(2,1)S(1)}, bf16[32,2944]{1,0:T(8,128)(2,1)S(1)}, u32[]{:S(2)}, u32[]{:S(2)}) collective-permute-start(bf16[32,2944]{1,0:T(8,128)(2,1)S(1)} %shard_map.82._after_ref.refs_0_), channel_id=1, source_target_pairs={{0,1},{1,0},{2,3},{3,2},{4,5},{5,4},{6,7},{7,6},{8,9},{9,8},{10,11... | collective-permute-start | bytes 565256 | tf_op jit(solution)/shard_map/ppermute | solution.py:494
  6.3 2.6 %collective-permute-start.4 = (bf16[32,2944]{1,0:T(8,128)(2,1)S(1)}, bf16[32,2944]{1,0:T(8,128)(2,1)S(1)}, u32[]{:S(2)}, u32[]{:S(2)}) collective-permute-start(bf16[32,2944]{1,0:T(8,128)(2,1)S(1)} %shard_map.82._after_ref.refs_0_), channel_id=1, source_target_pairs={{0,2},{1,3},{2,0},{3,1},{4,6},{5,7},{6,4},{7,5},{8,10},{9,11},{10,... | collective-permute-start | bytes 565256 | tf_op jit(solution)/shard_map/ppermute | solution.py:494
  8.9 1.5 %copy.9 = bf16[2,2,720,90]{3,2,1,0:T(8,128)(2,1)S(1)} copy(bf16[2,2,720,90]{2,1,3,0:T(2,128)(2,1)} %bitcast.40) | data formatting | bytes 1036800 | tf_op jit(solution)/shard_map/transpose | solution.py:531
  10.4 13.3 %shard_map.83 = (bf16[4,720,2880]{2,1,0:T(8,128)(2,1)}, f32[8,128]{1,0:T(8,128)S(1)}) custom-call(bf16[4,720,2880]{2,1,0:T(8,128)(2,1)} %bitcast.37, bf16[4,720,90]{2,1,0:T(8,128)(2,1)S(1)} %bitcast.30, bf16[32,2944]{1,0:T(8,128)(2,1)S(1)} %shard_map.82._after_ref.refs_0_), custom_call_target="tpu_custom_call" | custom-call | flops 1024 | bytes 1024 | tf_op jit(solution)/shard_map/pallas_call | solution.py:91
  23.9 1.8 %collective-permute-start.7 = (bf16[32,2944]{1,0:T(8,128)(2,1)S(1)}, bf16[32,2944]{1,0:T(8,128)(2,1)S(1)}, u32[]{:S(2)}, u32[]{:S(2)}) collective-permute-start(bf16[32,2944]{1,0:T(8,128)(2,1)S(1)} %shard_map.82._after_ref.refs_0_), channel_id=1, source_target_pairs={{0,8},{4,12},{8,0},{12,4},{1,9},{5,13},{9,1},{13,5},{2,10},{6,14},... | collective-permute-start | bytes 565256 | tf_op jit(solution)/shard_map/ppermute | solution.py:494
  26.0 1.7 %collective-permute-start.8 = (bf16[32,2944]{1,0:T(8,128)(2,1)S(1)}, bf16[32,2944]{1,0:T(8,128)(2,1)S(1)}, u32[]{:S(2)}, u32[]{:S(2)}) collective-permute-start(bf16[32,2944]{1,0:T(8,128)(2,1)S(1)} %collective-permute-done.3.refs_1_), channel_id=1, source_target_pairs={{0,8},{4,12},{8,0},{12,4},{1,9},{5,13},{9,1},{13,5},{2,10},{6,14},... | collective-permute-start | bytes 565256 | tf_op jit(solution)/shard_map/ppermute | solution.py:494
  28.1 2.4 %shard_map.85 = (bf16[256,128]{1,0:T(8,128)(2,1)S(1)}, f32[8,128]{1,0:T(8,128)}, bf16[2880,256]{1,0:T(8,128)(2,1)S(1)}, f32[8,256]{1,0:T(8,128)S(1)}) custom-call(s32[2]{0:T(128)S(1)} %pad_add_fusion.place_ref, bf16[128,2944]{1,0:T(8,128)(2,1)S(1)} %shard_map.84.refs_0_, bf16[128,2944]{1,0:T(8,128)(2,1)S(1)} %collective-permute-done.6.refs_1_), custom_call_target="tpu_custom_call" | custom-call | flops 1024 | bytes 1024 | tf_op jit(solution)/shard_map/pallas_call | solution.py:299
  31.1 9.1 %shard_map.86 = (bf16[720,256]{1,0:T(8,128)(2,1)S(1)}, f32[8,128]{1,0:T(8,128)S(1)}) custom-call(bf16[2880,256]{1,0:T(8,128)(2,1)S(1)} %get-tuple-element.69.rows_ref, f32[8,256]{1,0:T(8,128)S(1)} %get-tuple-element.70.mask_ref, bf16[2,2,720,2880]{3,2,1,0:T(8,128)(2,1)} %bitcast.34), custom_call_target="tpu_custom_call" | custom-call | flops 1024 | bytes 1024 | tf_op jit(solution)/shard_map/pallas_call | solution.py:337
  40.2 2.9 %collective-permute-done.9.refs_2_ = bf16[32,2944]{1,0:T(8,128)(2,1)S(1)} collective-permute-done((bf16[32,2944]{1,0:T(8,128)(2,1)S(1)}, bf16[32,2944]{1,0:T(8,128)(2,1)S(1)}, u32[]{:S(2)}, u32[]{:S(2)}) %collective-permute-start.9) | collective-permute-done | bytes 188448 | tf_op jit(solution)/shard_map/ppermute | solution.py:494
  43.8 2.3 %collective-permute-start.16 = (bf16[720,256]{1,0:T(8,128)(2,1)S(1)}, bf16[720,256]{1,0:T(8,128)(2,1)S(1)}, u32[]{:S(2)}, u32[]{:S(2)}) collective-permute-start(bf16[720,256]{1,0:T(8,128)(2,1)S(1)} %get-tuple-element.82.refs_0_), channel_id=1, source_target_pairs={{0,1},{1,0},{2,3},{3,2},{4,5},{5,4},{6,7},{7,6},{8,9},{9,8},{10,11... | collective-permute-start | bytes 1105928 | tf_op jit(solution)/shard_map/ppermute | solution.py:494
  46.1 2.1 %collective-permute-start.17 = (bf16[720,256]{1,0:T(8,128)(2,1)S(1)}, bf16[720,256]{1,0:T(8,128)(2,1)S(1)}, u32[]{:S(2)}, u32[]{:S(2)}) collective-permute-start(bf16[720,256]{1,0:T(8,128)(2,1)S(1)} %get-tuple-element.82.refs_0_), channel_id=1, source_target_pairs={{0,2},{1,3},{2,0},{3,1},{4,6},{5,7},{6,4},{7,5},{8,10},{9,11},{10,... | collective-permute-start | bytes 1105928 | tf_op jit(solution)/shard_map/ppermute | solution.py:494
  50.6 4.2 %shard_map.88 = (bf16[512,128]{1,0:T(8,128)(2,1)}, f32[8,128]{1,0:T(8,128)S(1)}, bf16[2880,384]{1,0:T(8,128)(2,1)S(1)}, f32[8,384]{1,0:T(8,128)S(1)}, bf16[2880,128]{1,0:T(8,128)(2,1)}, /*index=5*/f32[8,128]{1,0:T(8,128)S(1)}) custom-call(s32[2]{0:T(128)S(1)} %pad_add_fusion.place_ref, bf16[128,2944]{1,0:T(8,128)(2,1)S(1)} %shard_map.84.refs_0_, ...), custom_call_target="tpu_custom_call" | custom-call | flops 1024 | bytes 1024 | tf_op jit(solution)/shard_map/pallas_call | solution.py:299
  54.8 11.2 %shard_map.89 = (bf16[720,384]{1,0:T(8,128)(2,1)S(1)}, f32[8,128]{1,0:T(8,128)}) custom-call(bf16[2880,384]{1,0:T(8,128)(2,1)S(1)} %get-tuple-element.79.rows_ref, f32[8,384]{1,0:T(8,128)S(1)} %get-tuple-element.80.mask_ref, bf16[2,2,720,2880]{3,2,1,0:T(8,128)(2,1)S(1)} %bitcast.36), custom_call_target="tpu_custom_call" | custom-call | flops 1024 | bytes 1024 | tf_op jit(solution)/shard_map/pallas_call | solution.py:337
  66.5 7.4 %collective-permute-start.19 = (bf16[720,384]{1,0:T(8,128)(2,1)S(1)}, bf16[720,384]{1,0:T(8,128)(2,1)S(1)}, u32[]{:S(2)}, u32[]{:S(2)}) collective-permute-start(bf16[720,384]{1,0:T(8,128)(2,1)S(1)} %shard_map.90.refs_0_), channel_id=1, source_target_pairs={{0,1},{1,0},{2,3},{3,2},{4,5},{5,4},{6,7},{7,6},{8,9},{9,8},{10,11... | collective-permute-start | bytes 1658888 | tf_op jit(solution)/shard_map/ppermute | solution.py:494
  74.9 1.4 collective-permute-start.21
  76.3 1.5 collective-permute-start.22
  77.8 1.6 %collective-permute-start.15 = (f32[8,128]{1,0:T(8,128)S(1)}, f32[8,128]{1,0:T(8,128)S(1)}, u32[]{:S(2)}, u32[]{:S(2)}) collective-permute-start(f32[8,128]{1,0:T(8,128)S(1)} %get-tuple-element.77), channel_id=1, source_target_pairs={{0,16},{16,0},{1,17},{17,1},{2,18},{18,2},{3,19},{19,3},{4,20},{20... | collective-permute-start | bytes 12296 | tf_op jit(solution)/shard_map/ppermute | solution.py:568
  82.7 15.6 %collective-permute-done.19._after_ref.refs_6_.refs_1_ = bf16[720,384]{1,0:T(8,128)(2,1)S(1)} collective-permute-done((bf16[720,384]{1,0:T(8,128)(2,1)S(1)}, bf16[720,384]{1,0:T(8,128)(2,1)S(1)}, u32[]{:S(2)}, u32[]{:S(2)}) %collective-permute-start.19) | collective-permute-done | bytes 552992 | tf_op jit(solution)/shard_map/ppermute | solution.py:494
  98.3 4.9 %shard_map.91 = (bf16[2,720,2880]{2,1,0:T(8,128)(2,1)S(1)}, f32[8,128]{1,0:T(8,128)}) custom-call(bf16[2,720,2880]{2,1,0:T(8,128)(2,1)} %bitcast.38, bf16[2,720,90]{2,1,0:T(8,128)(2,1)S(1)} %bitcast.31, bf16[720,384]{1,0:T(8,128)(2,1)S(1)} %collective-permute-done.19._after_ref.refs_6_.refs_1_), custom_call_target="tpu_custom_call" | custom-call | flops 1024 | bytes 1024 | tf_op jit(solution)/shard_map/pallas_call | solution.py:91
  103.2 14.0 %collective-permute-done.22.refs_4_ = bf16[720,256]{1,0:T(8,128)(2,1)} collective-permute-done((bf16[720,256]{1,0:T(8,128)(2,1)S(1)}, bf16[720,256]{1,0:T(8,128)(2,1)}, u32[]{:S(2)}, u32[]{:S(2)}) %collective-permute-start.22) | collective-permute-done | bytes 368672 | tf_op jit(solution)/shard_map/ppermute | solution.py:508
  117.2 5.4 %shard_map.92 = (bf16[1,128,720]{2,1,0:T(8,128)(2,1)S(1)}, bf16[1,128,720]{2,1,0:T(8,128)(2,1)S(1)}) custom-call(s32[2]{0:T(128)S(1)} %pad_add_fusion.place_ref, bf16[256,128]{1,0:T(8,128)(2,1)S(1)} %copy-done.2, bf16[720,256]{1,0:T(8,128)(2,1)S(1)} %get-tuple-element.82.refs_0_, bf16[720,256]{1,0:T(8,128)(2,1)S(1)} %collective-permute-done.16.refs_1_, ...), custom_call_target="tpu_custom_call" | custom-call | flops 1024 | bytes 1024 | tf_op jit(solution)/shard_map/pallas_call | solution.py:439
  122.6 9.3 %shard_map.93 = (bf16[2,128,720]{2,1,0:T(8,128)(2,1)S(1)}, bf16[2,128,720]{2,1,0:T(8,128)(2,1)S(1)}) custom-call(s32[2]{0:T(128)S(1)} %pad_add_fusion.place_ref, bf16[512,128]{1,0:T(8,128)(2,1)S(1)} %copy-done.8, bf16[720,384]{1,0:T(8,128)(2,1)S(1)} %shard_map.90.refs_0_, bf16[720,384]{1,0:T(8,128)(2,1)S(1)} %collective-permute-done.19._after_ref.refs_6_.refs_1_, ...), custom_call_target="tpu_custom_call" | custom-call | flops 1024 | bytes 1024 | tf_op jit(solution)/shard_map/pallas_call | solution.py:439
  132.3 1.7 %collective-permute-done.23 = bf16[2,128,720]{2,1,0:T(8,128)(2,1)S(1)} collective-permute-done((bf16[2,128,720]{2,1,0:T(8,128)(2,1)S(1)}, bf16[2,128,720]{2,1,0:T(8,128)(2,1)S(1)}, u32[]{:S(2)}, u32[]{:S(2)}) %collective-permute-start.23) | collective-permute-done | bytes 368672 | tf_op jit(solution)/shard_map/ppermute | solution.py:494
  134.2 1.6 %collective-permute-start.24 = (bf16[32,720]{1,0:T(8,128)(2,1)S(1)}, bf16[32,720]{1,0:T(8,128)(2,1)S(1)}, u32[]{:S(2)}, u32[]{:S(2)}) collective-permute-start(bf16[32,720]{1,0:T(8,128)(2,1)S(1)} %get-tuple-element.104), channel_id=1, source_target_pairs={{0,8},{1,9},{2,10},{3,11},{4,12},{5,13},{6,14},{7,15},{8,0},{9,1},... | collective-permute-start | bytes 138248 | tf_op jit(solution)/shard_map/ppermute | solution.py:608
  135.7 1.5 collective-permute-start.25
  137.7 2.5 %collective-permute-start.27 = (bf16[32,720]{1,0:T(8,128)(2,1)S(1)}, bf16[32,720]{1,0:T(8,128)(2,1)S(1)}, u32[]{:S(2)}, u32[]{:S(2)}) collective-permute-start(bf16[32,720]{1,0:T(8,128)(2,1)S(1)} %get-tuple-element.101), channel_id=1, source_target_pairs={{0,2},{1,3},{2,0},{3,1},{4,6},{5,7},{6,4},{7,5},{8,10},{9,11},{10,... | collective-permute-start | bytes 138248 | tf_op jit(solution)/shard_map/ppermute | solution.py:608
  140.2 1.4 collective-permute-start.28
  141.6 2.5 %collective-permute-start.29 = (bf16[32,720]{1,0:T(8,128)(2,1)S(1)}, bf16[32,720]{1,0:T(8,128)(2,1)S(1)}, u32[]{:S(2)}, u32[]{:S(2)}) collective-permute-start(bf16[32,720]{1,0:T(8,128)(2,1)S(1)} %get-tuple-element.99), channel_id=1, source_target_pairs={{0,3},{1,2},{2,1},{3,0},{4,7},{5,6},{6,5},{7,4},{8,11},{9,10},{10,... | collective-permute-start | bytes 138248 | tf_op jit(solution)/shard_map/ppermute | solution.py:608
  144.0 1.3 collective-permute-start.30
  145.4 2.3 %collective-permute-done.28.refs_5_ = bf16[32,720]{1,0:T(8,128)(2,1)S(1)} collective-permute-done((bf16[32,720]{1,0:T(8,128)(2,1)S(1)}, bf16[32,720]{1,0:T(8,128)(2,1)S(1)}, u32[]{:S(2)}, u32[]{:S(2)}) %collective-permute-start.28) | collective-permute-done | bytes 46112 | tf_op jit(solution)/shard_map/ppermute | solution.py:608
  148.0 2.8 %collective-permute-done.30.refs_7_ = bf16[32,720]{1,0:T(8,128)(2,1)S(1)} collective-permute-done((bf16[32,720]{1,0:T(8,128)(2,1)S(1)}, bf16[32,720]{1,0:T(8,128)(2,1)S(1)}, u32[]{:S(2)}, u32[]{:S(2)}) %collective-permute-start.30) | collective-permute-done | bytes 46112 | tf_op jit(solution)/shard_map/ppermute | solution.py:608
  150.8 1.4 shard_map.94
  (63 shorter events, 13.3 us)
Async XLA Ops:
  3.2 20.5 %collective-permute-start.3 = (bf16[32,2944]{1,0:T(8,128)(2,1)S(1)}, bf16[32,2944]{1,0:T(8,128)(2,1)S(1)}, u32[]{:S(2)}, u32[]{:S(2)}) collective-permute-start(bf16[32,2944]{1,0:T(8,128)(2,1)S(1)} %shard_map.82._after_ref.refs_0_), channel_id=1, source_target_pairs={{0,1},{1,0},{2,3},{3,2},{4,5},{5,4},{6,7},{7,6},{8,9},{9,8},{10,11... | collective-permute-start | bytes 565256 | tf_op jit(solution)/shard_map/ppermute | solution.py:494
  6.3 17.5 %collective-permute-start.4 = (bf16[32,2944]{1,0:T(8,128)(2,1)S(1)}, bf16[32,2944]{1,0:T(8,128)(2,1)S(1)}, u32[]{:S(2)}, u32[]{:S(2)}) collective-permute-start(bf16[32,2944]{1,0:T(8,128)(2,1)S(1)} %shard_map.82._after_ref.refs_0_), channel_id=1, source_target_pairs={{0,2},{1,3},{2,0},{3,1},{4,6},{5,7},{6,4},{7,5},{8,10},{9,11},{10,... | collective-permute-start | bytes 565256 | tf_op jit(solution)/shard_map/ppermute | solution.py:494
  8.9 14.9 %collective-permute-start.5 = (bf16[32,2944]{1,0:T(8,128)(2,1)S(1)}, bf16[32,2944]{1,0:T(8,128)(2,1)S(1)}, u32[]{:S(2)}, u32[]{:S(2)}) collective-permute-start(bf16[32,2944]{1,0:T(8,128)(2,1)S(1)} %shard_map.82._after_ref.refs_0_), channel_id=1, source_target_pairs={{0,3},{1,2},{2,1},{3,0},{4,7},{5,6},{6,5},{7,4},{8,11},{9,10},{10,... | collective-permute-start | bytes 565256 | tf_op jit(solution)/shard_map/ppermute | solution.py:494
  23.8 4.3 %collective-permute-start.6 = (bf16[128,2944]{1,0:T(8,128)(2,1)S(1)}, bf16[128,2944]{1,0:T(8,128)(2,1)S(1)}, u32[]{:S(2)}, u32[]{:S(2)}) collective-permute-start(bf16[128,2944]{1,0:T(8,128)(2,1)S(1)} %shard_map.84.refs_0_), channel_id=1, source_target_pairs={{0,4},{4,0},{8,12},{12,8},{1,5},{5,1},{9,13},{13,9},{2,6},{6,2},{1... | collective-permute-start | bytes 2261000 | tf_op jit(solution)/shard_map/ppermute | solution.py:494
  23.9 16.3 %collective-permute-start.7 = (bf16[32,2944]{1,0:T(8,128)(2,1)S(1)}, bf16[32,2944]{1,0:T(8,128)(2,1)S(1)}, u32[]{:S(2)}, u32[]{:S(2)}) collective-permute-start(bf16[32,2944]{1,0:T(8,128)(2,1)S(1)} %shard_map.82._after_ref.refs_0_), channel_id=1, source_target_pairs={{0,8},{4,12},{8,0},{12,4},{1,9},{5,13},{9,1},{13,5},{2,10},{6,14},... | collective-permute-start | bytes 565256 | tf_op jit(solution)/shard_map/ppermute | solution.py:494
  25.7 14.5 %collective-permute-start.10 = (bf16[32,2944]{1,0:T(8,128)(2,1)S(1)}, bf16[32,2944]{1,0:T(8,128)(2,1)S(1)}, u32[]{:S(2)}, u32[]{:S(2)}) collective-permute-start(bf16[32,2944]{1,0:T(8,128)(2,1)S(1)} %collective-permute-done.5.refs_3_), channel_id=1, source_target_pairs={{0,8},{4,12},{8,0},{12,4},{1,9},{5,13},{9,1},{13,5},{2,10},{6,14},... | collective-permute-start | bytes 565256 | tf_op jit(solution)/shard_map/ppermute | solution.py:494
  26.0 14.2 %collective-permute-start.8 = (bf16[32,2944]{1,0:T(8,128)(2,1)S(1)}, bf16[32,2944]{1,0:T(8,128)(2,1)S(1)}, u32[]{:S(2)}, u32[]{:S(2)}) collective-permute-start(bf16[32,2944]{1,0:T(8,128)(2,1)S(1)} %collective-permute-done.3.refs_1_), channel_id=1, source_target_pairs={{0,8},{4,12},{8,0},{12,4},{1,9},{5,13},{9,1},{13,5},{2,10},{6,14},... | collective-permute-start | bytes 565256 | tf_op jit(solution)/shard_map/ppermute | solution.py:494
  27.7 15.5 %collective-permute-start.9 = (bf16[32,2944]{1,0:T(8,128)(2,1)S(1)}, bf16[32,2944]{1,0:T(8,128)(2,1)S(1)}, u32[]{:S(2)}, u32[]{:S(2)}) collective-permute-start(bf16[32,2944]{1,0:T(8,128)(2,1)S(1)} %collective-permute-done.4.refs_2_), channel_id=1, source_target_pairs={{0,8},{4,12},{8,0},{12,4},{1,9},{5,13},{9,1},{13,5},{2,10},{6,14},... | collective-permute-start | bytes 565256 | tf_op jit(solution)/shard_map/ppermute | solution.py:494
  31.1 23.7 %copy-start.6 = (bf16[4,720,2880]{2,1,0:T(8,128)(2,1)S(1)}, bf16[4,720,2880]{2,1,0:T(8,128)(2,1)}, u32[]{:S(2)}) copy-start(bf16[4,720,2880]{2,1,0:T(8,128)(2,1)} %get-tuple-element.71) | copy-start | bytes 49766404
  43.2 5.6 %collective-permute-start.11 = (bf16[32,2944]{1,0:T(8,128)(2,1)S(1)}, bf16[32,2944]{1,0:T(8,128)(2,1)S(1)}, u32[]{:S(2)}, u32[]{:S(2)}) collective-permute-start(bf16[32,2944]{1,0:T(8,128)(2,1)S(1)} %get-tuple-element.73.refs_2_), channel_id=1, source_target_pairs={{0,4},{4,0},{8,12},{12,8},{1,5},{5,1},{9,13},{13,9},{2,6},{6,2},{1... | collective-permute-start | bytes 565256 | tf_op jit(solution)/shard_map/ppermute | solution.py:494
  43.3 5.6 %collective-permute-start.12 = (bf16[32,2944]{1,0:T(8,128)(2,1)S(1)}, bf16[32,2944]{1,0:T(8,128)(2,1)S(1)}, u32[]{:S(2)}, u32[]{:S(2)}) collective-permute-start(bf16[32,2944]{1,0:T(8,128)(2,1)S(1)} %get-tuple-element.74.refs_3_), channel_id=1, source_target_pairs={{0,4},{4,0},{8,12},{12,8},{1,5},{5,1},{9,13},{13,9},{2,6},{6,2},{1... | collective-permute-start | bytes 565256 | tf_op jit(solution)/shard_map/ppermute | solution.py:494
  43.8 22.2 %collective-permute-start.16 = (bf16[720,256]{1,0:T(8,128)(2,1)S(1)}, bf16[720,256]{1,0:T(8,128)(2,1)S(1)}, u32[]{:S(2)}, u32[]{:S(2)}) collective-permute-start(bf16[720,256]{1,0:T(8,128)(2,1)S(1)} %get-tuple-element.82.refs_0_), channel_id=1, source_target_pairs={{0,1},{1,0},{2,3},{3,2},{4,5},{5,4},{6,7},{7,6},{8,9},{9,8},{10,11... | collective-permute-start | bytes 1105928 | tf_op jit(solution)/shard_map/ppermute | solution.py:494
  46.1 20.3 %collective-permute-start.17 = (bf16[720,256]{1,0:T(8,128)(2,1)S(1)}, bf16[720,256]{1,0:T(8,128)(2,1)S(1)}, u32[]{:S(2)}, u32[]{:S(2)}) collective-permute-start(bf16[720,256]{1,0:T(8,128)(2,1)S(1)} %get-tuple-element.82.refs_0_), channel_id=1, source_target_pairs={{0,2},{1,3},{2,0},{3,1},{4,6},{5,7},{6,4},{7,5},{8,10},{9,11},{10,... | collective-permute-start | bytes 1105928 | tf_op jit(solution)/shard_map/ppermute | solution.py:494
  48.2 18.2 %collective-permute-start.18 = (bf16[720,256]{1,0:T(8,128)(2,1)S(1)}, bf16[720,256]{1,0:T(8,128)(2,1)S(1)}, u32[]{:S(2)}, u32[]{:S(2)}) collective-permute-start(bf16[720,256]{1,0:T(8,128)(2,1)S(1)} %get-tuple-element.82.refs_0_), channel_id=1, source_target_pairs={{1,2},{2,1},{5,6},{6,5},{9,10},{10,9},{13,14},{14,13},{17,18},{18,... | collective-permute-start | bytes 1105928 | tf_op jit(solution)/shard_map/ppermute | solution.py:504
  48.9 1.5 collective-permute-start.13
  49.0 1.7 %collective-permute-start.14 = (bf16[32,2944]{1,0:T(8,128)(2,1)S(1)}, bf16[32,2944]{1,0:T(8,128)(2,1)S(1)}, u32[]{:S(2)}, u32[]{:S(2)}) collective-permute-start(bf16[32,2944]{1,0:T(8,128)(2,1)S(1)} %get-tuple-element.76.refs_5_), channel_id=1, source_target_pairs={{0,4},{4,0},{8,12},{12,8},{1,5},{5,1},{9,13},{13,9},{2,6},{6,2},{1... | collective-permute-start | bytes 565256 | tf_op jit(solution)/shard_map/ppermute | solution.py:494
  66.5 31.8 %collective-permute-start.19 = (bf16[720,384]{1,0:T(8,128)(2,1)S(1)}, bf16[720,384]{1,0:T(8,128)(2,1)S(1)}, u32[]{:S(2)}, u32[]{:S(2)}) collective-permute-start(bf16[720,384]{1,0:T(8,128)(2,1)S(1)} %shard_map.90.refs_0_), channel_id=1, source_target_pairs={{0,1},{1,0},{2,3},{3,2},{4,5},{5,4},{6,7},{7,6},{8,9},{9,8},{10,11... | collective-permute-start | bytes 1658888 | tf_op jit(solution)/shard_map/ppermute | solution.py:494
  73.8 43.4 %collective-permute-start.20 = (bf16[720,384]{1,0:T(8,128)(2,1)S(1)}, bf16[720,384]{1,0:T(8,128)(2,1)S(1)}, u32[]{:S(2)}, u32[]{:S(2)}) collective-permute-start(bf16[720,384]{1,0:T(8,128)(2,1)S(1)} %shard_map.90.refs_0_), channel_id=1, source_target_pairs={{0,2},{1,3},{2,0},{3,1},{4,6},{5,7},{6,4},{7,5},{8,10},{9,11},{10,... | collective-permute-start | bytes 1658888 | tf_op jit(solution)/shard_map/ppermute | solution.py:494
  74.9 47.7 %collective-permute-start.21 = (bf16[720,384]{1,0:T(8,128)(2,1)S(1)}, bf16[720,384]{1,0:T(8,128)(2,1)}, u32[]{:S(2)}, u32[]{:S(2)}) collective-permute-start(bf16[720,384]{1,0:T(8,128)(2,1)S(1)} %shard_map.90.refs_0_), channel_id=1, source_target_pairs={{0,3},{1,2},{2,1},{3,0},{4,7},{5,6},{6,5},{7,4},{8,11},{9,10},{10,... | collective-permute-start | bytes 1658888 | tf_op jit(solution)/shard_map/ppermute | solution.py:494
  76.3 40.9 %collective-permute-start.22 = (bf16[720,256]{1,0:T(8,128)(2,1)S(1)}, bf16[720,256]{1,0:T(8,128)(2,1)}, u32[]{:S(2)}, u32[]{:S(2)}) collective-permute-start(bf16[720,256]{1,0:T(8,128)(2,1)S(1)} %collective-permute-done.17.refs_2_), channel_id=1, source_target_pairs={{2,3},{1,0},{6,7},{5,4},{10,11},{9,8},{14,15},{13,12},{18,19},{17,... | collective-permute-start | bytes 1105928 | tf_op jit(solution)/shard_map/ppermute | solution.py:508
  77.8 3.7 %collective-permute-start.15 = (f32[8,128]{1,0:T(8,128)S(1)}, f32[8,128]{1,0:T(8,128)S(1)}, u32[]{:S(2)}, u32[]{:S(2)}) collective-permute-start(f32[8,128]{1,0:T(8,128)S(1)} %get-tuple-element.77), channel_id=1, source_target_pairs={{0,16},{16,0},{1,17},{17,1},{2,18},{18,2},{3,19},{19,3},{4,20},{20... | collective-permute-start | bytes 12296 | tf_op jit(solution)/shard_map/ppermute | solution.py:568
  80.6 36.6 %copy-start.2 = (bf16[256,128]{1,0:T(8,128)(2,1)S(1)}, bf16[256,128]{1,0:T(8,128)(2,1)}, u32[]{:S(2)}) copy-start(bf16[256,128]{1,0:T(8,128)(2,1)} %copy-done.1) | copy-start | bytes 196612
  98.3 24.3 %copy-start.8 = (bf16[512,128]{1,0:T(8,128)(2,1)S(1)}, bf16[512,128]{1,0:T(8,128)(2,1)}, u32[]{:S(2)}) copy-start(bf16[512,128]{1,0:T(8,128)(2,1)} %get-tuple-element.78.meta_ref) | copy-start | bytes 393220
  122.6 9.4 %copy-start.7 = (bf16[2880,128]{1,0:T(8,128)(2,1)S(1)}, bf16[2880,128]{1,0:T(8,128)(2,1)}, u32[]{:S(2)}) copy-start(bf16[2880,128]{1,0:T(8,128)(2,1)} %get-tuple-element.89) | copy-start | bytes 2211844
  132.2 1.8 %collective-permute-start.23 = (bf16[2,128,720]{2,1,0:T(8,128)(2,1)S(1)}, bf16[2,128,720]{2,1,0:T(8,128)(2,1)S(1)}, u32[]{:S(2)}, u32[]{:S(2)}) collective-permute-start(bf16[2,128,720]{2,1,0:T(8,128)(2,1)S(1)} %get-tuple-element.96), channel_id=1, source_target_pairs={{0,4},{4,0},{8,12},{12,8},{1,5},{5,1},{9,13},{13,9},{2,6},{6,2},{1... | collective-permute-start | bytes 1105928 | tf_op jit(solution)/shard_map/ppermute | solution.py:494
  134.2 7.4 %collective-permute-start.24 = (bf16[32,720]{1,0:T(8,128)(2,1)S(1)}, bf16[32,720]{1,0:T(8,128)(2,1)S(1)}, u32[]{:S(2)}, u32[]{:S(2)}) collective-permute-start(bf16[32,720]{1,0:T(8,128)(2,1)S(1)} %get-tuple-element.104), channel_id=1, source_target_pairs={{0,8},{1,9},{2,10},{3,11},{4,12},{5,13},{6,14},{7,15},{8,0},{9,1},... | collective-permute-start | bytes 138248 | tf_op jit(solution)/shard_map/ppermute | solution.py:608
  135.7 8.3 %collective-permute-start.25 = (bf16[32,720]{1,0:T(8,128)(2,1)S(1)}, bf16[32,720]{1,0:T(8,128)(2,1)S(1)}, u32[]{:S(2)}, u32[]{:S(2)}) collective-permute-start(bf16[32,720]{1,0:T(8,128)(2,1)S(1)} %get-tuple-element.103), channel_id=1, source_target_pairs={{0,1},{1,0},{2,3},{3,2},{4,5},{5,4},{6,7},{7,6},{8,9},{9,8},{10,11... | collective-permute-start | bytes 138248 | tf_op jit(solution)/shard_map/ppermute | solution.py:608
  137.2 8.2 %collective-permute-start.26 = (bf16[32,720]{1,0:T(8,128)(2,1)S(1)}, bf16[32,720]{1,0:T(8,128)(2,1)S(1)}, u32[]{:S(2)}, u32[]{:S(2)}) collective-permute-start(bf16[32,720]{1,0:T(8,128)(2,1)S(1)} %get-tuple-element.102), channel_id=1, source_target_pairs={{0,9},{1,8},{2,11},{3,10},{4,13},{5,12},{6,15},{7,14},{8,1},{9,0},... | collective-permute-start | bytes 138248 | tf_op jit(solution)/shard_map/ppermute | solution.py:608
  137.7 7.7 %collective-permute-start.27 = (bf16[32,720]{1,0:T(8,128)(2,1)S(1)}, bf16[32,720]{1,0:T(8,128)(2,1)S(1)}, u32[]{:S(2)}, u32[]{:S(2)}) collective-permute-start(bf16[32,720]{1,0:T(8,128)(2,1)S(1)} %get-tuple-element.101), channel_id=1, source_target_pairs={{0,2},{1,3},{2,0},{3,1},{4,6},{5,7},{6,4},{7,5},{8,10},{9,11},{10,... | collective-permute-start | bytes 138248 | tf_op jit(solution)/shard_map/ppermute | solution.py:608
  140.2 7.5 %collective-permute-start.28 = (bf16[32,720]{1,0:T(8,128)(2,1)S(1)}, bf16[32,720]{1,0:T(8,128)(2,1)S(1)}, u32[]{:S(2)}, u32[]{:S(2)}) collective-permute-start(bf16[32,720]{1,0:T(8,128)(2,1)S(1)} %get-tuple-element.100), channel_id=1, source_target_pairs={{0,10},{1,11},{2,8},{3,9},{4,14},{5,15},{6,12},{7,13},{8,2},{9,3},... | collective-permute-start | bytes 138248 | tf_op jit(solution)/shard_map/ppermute | solution.py:608
  141.6 6.4 %collective-permute-start.29 = (bf16[32,720]{1,0:T(8,128)(2,1)S(1)}, bf16[32,720]{1,0:T(8,128)(2,1)S(1)}, u32[]{:S(2)}, u32[]{:S(2)}) collective-permute-start(bf16[32,720]{1,0:T(8,128)(2,1)S(1)} %get-tuple-element.99), channel_id=1, source_target_pairs={{0,3},{1,2},{2,1},{3,0},{4,7},{5,6},{6,5},{7,4},{8,11},{9,10},{10,... | collective-permute-start | bytes 138248 | tf_op jit(solution)/shard_map/ppermute | solution.py:608
  144.0 6.8 %collective-permute-start.30 = (bf16[32,720]{1,0:T(8,128)(2,1)S(1)}, bf16[32,720]{1,0:T(8,128)(2,1)S(1)}, u32[]{:S(2)}, u32[]{:S(2)}) collective-permute-start(bf16[32,720]{1,0:T(8,128)(2,1)S(1)} %get-tuple-element.98), channel_id=1, source_target_pairs={{0,11},{1,10},{2,9},{3,8},{4,15},{5,14},{6,13},{7,12},{8,3},{9,2},... | collective-permute-start | bytes 138248 | tf_op jit(solution)/shard_map/ppermute | solution.py:608
  (5 other events, 3.6 us)
